TPU v7x, 32 devices: a whole 2x2x4 slice. The times are simulated.
32 devices in a mesh: grp: 4 (over y, x), dev: 8 (over z, core).
Axes of the slice: x: 2, y: 2, z: 4, core: 2. Of those that a mesh axis runs over, the one named last changes fastest.
Arguments:
- blocks: bfloat16 [256, 64, 4096], P(('grp', 'dev')), may hold values from -6 to 6
- coords: int32 [3, 256], P(None, ('grp', 'dev')), may hold values from 0 to 15, as said below
- counts: int32 [32], P(('grp', 'dev')), may hold values from 1 to 8, as said below
- row_place: int32 [16], replicated, may hold values from 0 to 15, as said below
- factor_one: bfloat16 [16, 4096], P('dev'), may hold values from -0.75 to 0.75
- factor_two: bfloat16 [16, 4096], P('dev'), may hold values from -0.75 to 0.75
- factor_three: bfloat16 [16, 4096], P('dev'), may hold values from -0.75 to 0.75
Outputs:
- new_rows: float32 [16, 4096], P('dev')
- gram: float32 [64, 64], replicated
Inputs may be any that keep to these rules, and one draw needn't show every extreme that they name: `coords`: every mode-1 id of a slot on the device with dev index d has its row-block position in [d * 2, (d + 1) * 2); on one device, the row-block positions of the mode-2 ids of its 8 slots lie in pairwise different ranges [e * 2, (e + 1) * 2), and so do those of the mode-3 ids. `counts`: some device has all 8 slots live. `row_place`: A permutation of 0 to 15.
All inputs are finite; a program needn't handle non-finite values.
Results may differ from a plain program's by a relative error of at most 0.0056.
Values may be sent and summed in bfloat16 or wider, within the bound.
No kernel may reach another device: no remote copies, remote signals or barrier semaphores. Data moves between devices by JAX's collectives and lax.ppermute only.
A program may use at most 128 MiB of HBM per device.

v0:
```python
import jax
import jax.numpy as jnp
from jax import lax
from jax.sharding import PartitionSpec as P


def look_place(ids, row_place):
    table = jnp.arange(row_place.shape[0])
    hits = ids[:, None] == table[None, :]
    return jnp.sum(jnp.where(hits, row_place[None, :], 0), axis=1)


def body(blocks, coords, counts, row_place, factor_one, factor_two, factor_three):
    slot_count = blocks.shape[0]
    edge = blocks.shape[1]
    rank_width = factor_one.shape[1] // edge
    row_blocks = factor_one.shape[0]
    live = (jnp.arange(slot_count) < counts[0]).astype(jnp.float32)
    pos_one = look_place(coords[0], row_place)
    pos_two = look_place(coords[1], row_place)
    pos_three = look_place(coords[2], row_place)
    local_one = pos_one % row_blocks
    pieces = (
        lax.all_gather(factor_two, "dev", axis=0, tiled=True),
        lax.all_gather(factor_three, "dev", axis=0, tiled=True),
    )
    taken = pieces[0].shape[0]
    offsets = jnp.arange(taken)
    pick_two = (pos_two[:, None] == offsets[None, :]).astype(jnp.bfloat16)
    pick_three = (pos_three[:, None] == offsets[None, :]).astype(jnp.bfloat16)
    chosen_two = jnp.dot(pick_two, pieces[0], preferred_element_type=jnp.float32)
    chosen_three = jnp.dot(pick_three, pieces[1], preferred_element_type=jnp.float32)
    upper = chosen_two.astype(jnp.bfloat16).reshape(slot_count, edge, rank_width)
    lower = chosen_three.astype(jnp.bfloat16).reshape(slot_count, edge, rank_width)
    tensor_rows = blocks.reshape(slot_count, edge * edge, edge)
    first = jnp.einsum(
        "bmk,bks->bms", tensor_rows, lower, preferred_element_type=jnp.float32
    ).astype(jnp.bfloat16)
    first = first.reshape(slot_count, edge, edge, rank_width)
    contrib = jnp.einsum("bajs,bjr->bars", first, upper, preferred_element_type=jnp.float32)
    contrib = contrib.reshape(slot_count, edge, rank_width * rank_width)
    owners = jnp.arange(row_blocks)
    assign = (local_one[:, None] == owners[None, :]).astype(jnp.float32) * live[:, None]
    panels = jnp.einsum("bl,bam->lam", assign, contrib, precision=lax.Precision.HIGHEST)
    panels = panels.reshape(row_blocks * edge, rank_width * rank_width)
    old_rows = factor_one.reshape(row_blocks * edge, rank_width)
    share = lax.psum_scatter(panels, "grp", scatter_dimension=1, tiled=True)
    panel_b = share.astype(jnp.bfloat16)
    proj_terms = jnp.dot(panel_b.T, old_rows, preferred_element_type=jnp.float32)
    proj = lax.psum(proj_terms, "dev").astype(jnp.bfloat16)
    row_terms = jnp.dot(panel_b, proj, preferred_element_type=jnp.float32)
    rows = lax.psum(row_terms, "grp")
    gram_local = jnp.dot(
        rows.T, rows, precision=lax.Precision.HIGHEST, preferred_element_type=jnp.float32
    )
    gmat = lax.psum(gram_local, "dev")
    trace_value = jnp.trace(gmat)
    rows_total = row_blocks * edge * lax.axis_size("dev")
    new_rows = (rows * lax.rsqrt(trace_value / (rows_total * rank_width))).reshape(
        row_blocks, edge * rank_width
    )
    gram = gmat * (rank_width / trace_value)
    return (new_rows, gram)


def solution(mesh):
    placed = (
        P(("grp", "dev"), None, None),
        P(None, ("grp", "dev")),
        P(("grp", "dev")),
        P(),
        P("dev", None),
        P("dev", None),
        P("dev", None),
    )
    return jax.shard_map(
        body, mesh=mesh, in_specs=placed, out_specs=(P("dev", None), P()), check_vma=False
    )
```

profile of v0, /device:TPU:0, one launch (start us, length us, event | category | flops | bytes accessed | tf_op | source)
XLA Modules:
  0.0 236.2 jit_solution(15236030686440279479)
XLA Ops:
  7.2 0.0 reduce-scatter.2.cloned.1.call-start
  7.2 0.8 slice_bitcast_fusion
  8.0 15.9 %all-gather.1 = bf16[8,2,4096]{2,1,0:T(2,128)(2,1)S(1)} all-gather(bf16[1,2,4096]{2,1,0:T(2,128)(2,1)} %bitcast.37), channel_id=1, replica_groups=mesh['grp'=4,'dev'=8] {'dev'}, dimensions={0}, use_global_device_ids=true | all-gather | bytes 147456 | tf_op jit(solution)/shard_map/all_gather | solution.py:25
  23.9 0.1 reshape.63
  24.0 0.9 select_reduce_fusion.3
  24.8 0.2 convolution_convert_fusion.1
  25.1 0.2 reshape.53
  25.2 12.6 %reshape.54 = bf16[8,4096,64]{2,1,0:T(8,128)(2,1)} reshape(bf16[8,64,4096]{2,1,0:T(8,128)(2,1)} %param.7) | data formatting | bytes 8388608 | tf_op jit(solution)/shard_map/reshape | solution.py:35
  37.8 8.4 %fusion.2 = bf16[8,4096,64]{1,2,0:T(8,128)(2,1)} fusion(bf16[8,64,64]{2,1,0:T(8,128)(2,1)S(1)} %reshape.53, bf16[8,4096,64]{2,1,0:T(8,128)(2,1)} %reshape.54), kind=kOutput, calls=%fused_computation.4 | convolution fusion | flops 270532608 | bytes 8454144 | tf_op jit(solution)/shard_map/bmk,bks->bms/dot_general | solution.py:36
  46.2 0.0 copy-start
  46.2 8.4 %copy.40 = bf16[8,4096,64]{2,1,0:T(8,128)(2,1)} copy(bf16[8,4096,64]{1,2,0:T(8,128)(2,1)} %fusion.2) | data formatting | bytes 8388608 | tf_op jit(solution)/shard_map/reshape | solution.py:39
  54.6 0.0 copy-done
  54.6 14.0 %all-gather = bf16[8,2,4096]{2,1,0:T(2,128)(2,1)S(1)} all-gather(bf16[1,2,4096]{2,1,0:T(2,128)(2,1)S(1)} %bitcast.38), channel_id=1, replica_groups=mesh['grp'=4,'dev'=8] {'dev'}, dimensions={0}, use_global_device_ids=true | all-gather | bytes 147456 | tf_op jit(solution)/shard_map/all_gather | solution.py:24
  68.6 0.1 reshape.61
  68.6 0.2 convolution_convert_fusion.2
  68.9 0.2 reshape.52
  69.0 11.5 %convolution_bitcast_fusion = f32[8,64,64,64]{3,2,1,0:T(8,128)} fusion(bf16[8,64,64,64]{3,2,1,0:T(8,128)(2,1)} %bitcast.35, bf16[8,64,64]{2,1,0:T(8,128)(2,1)S(1)} %reshape.52), kind=kOutput, calls=%fused_computation | convolution fusion | flops 268435456 | bytes 12648448 | tf_op jit(solution)/shard_map/bajs,bjr->bars/dot_general | solution.py:40
  80.5 14.8 %reshape.56 = f32[8,64,4096]{2,1,0:T(8,128)} reshape(f32[8,64,64,64]{3,2,1,0:T(8,128)} %convolution_bitcast_fusion) | data formatting | bytes 16777216 | tf_op jit(solution)/shard_map/reshape | solution.py:41
  95.9 0.0 copy-start.1
  95.9 15.3 %fusion = f32[2,64,4096]{2,0,1:T(2,128)S(1)} fusion(f32[8,64,4096]{2,1,0:T(8,128)} %reshape.56, f32[8]{0:T(128)S(1)} %compare_convert_fusion, s32[8]{0:T(128)S(1)} %and_select_fusion), kind=kOutput, calls=%fused_computation.1 | convolution fusion | flops 50331680 | bytes 10485824 | tf_op jit(solution)/shard_map/bl,bam->lam/dot_general | solution.py:44
  111.3 2.6 %copy.33 = f32[2,64,4096]{2,1,0:T(8,128)} copy(f32[2,64,4096]{2,0,1:T(2,128)S(1)} %fusion) | data formatting | bytes 4194304 | tf_op jit(solution)/shard_map/bl,bam->lam/dot_general | solution.py:44
  113.8 0.0 reduce-scatter.2.cloned.1.call-update
  113.9 0.0 copy-done.1
  113.9 0.1 reshape.58
  114.0 36.2 %reduce-scatter.2.cloned.1.call-done = f32[128,1024]{1,0:T(8,128)} async-done(((f32[128,4096]{1,0:T(8,128)}), f32[128,1024]{1,0:T(8,128)}) %reduce-scatter.2.cloned.1.call-update) | async-done | bytes 524304 | tf_op jit(solution)/shard_map/reduce_scatter | solution.py:47
  150.2 1.3 fusion.7
  151.5 31.6 %all-reduce.1 = bf16[1024,64]{0,1:T(8,128)(2,1)S(1)} all-reduce(f32[1024,64]{0,1:T(8,128)S(1)} %fusion.7), channel_id=1, replica_groups=mesh['grp'=4,'dev'=8] {'dev'}, use_global_device_ids=true, to_apply=%region_4.5 | all-reduce | flops 65536 | bytes 393216 | tf_op jit(solution)/shard_map/psum | solution.py:50
  183.1 1.3 fusion.4
  184.3 15.4 %psum.22 = f32[128,64]{0,1:T(8,128)S(1)} all-reduce(f32[128,64]{0,1:T(8,128)S(1)} %fusion.4), channel_id=1, replica_groups=mesh['grp'=4,'dev'=8] {'grp'}, use_global_device_ids=true, to_apply=%region_5.6 | all-reduce | flops 8192 | bytes 65536 | tf_op jit(solution)/shard_map/psum | solution.py:52
  199.8 0.2 fusion.19
  199.9 25.9 %psum.23 = f32[64,64]{1,0:T(8,128)S(1)} all-reduce(f32[64,64]{1,0:T(8,128)S(1)} %fusion.19), channel_id=1, replica_groups=mesh['grp'=4,'dev'=8] {'dev'}, use_global_device_ids=true, to_apply=%region_6.7 | all-reduce | flops 4096 | bytes 32768 | tf_op jit(solution)/shard_map/psum | solution.py:56
  225.9 0.6 select_reduce_fusion
  227.2 0.6 broadcast_multiply_fusion
  228.5 0.1 copy.34
  228.6 0.7 reshape.59
  (3 shorter events, 0.0 us)
Async XLA Ops:
  7.2 143.0 %reduce-scatter.2.cloned.1.call-start = ((), (), s32[]{:S(2)}) async-start(), calls=%async_computation.1 | async-start | bytes 2621440 | tf_op jit(solution)/shard_map/reduce_scatter | solution.py:47
  46.2 8.4 %copy-start = (bf16[2,4096]{1,0:T(2,128)(2,1)S(1)}, bf16[2,4096]{1,0:T(2,128)(2,1)}, u32[]{:S(2)}) copy-start(bf16[2,4096]{1,0:T(2,128)(2,1)} %param.12) | copy-start | bytes 49156
  95.9 17.9 %copy-start.1 = (bf16[2,4096]{1,0:T(2,128)(2,1)S(1)}, bf16[2,4096]{1,0:T(2,128)(2,1)}, u32[]{:S(2)}) copy-start(bf16[2,4096]{1,0:T(2,128)(2,1)} %param.11) | copy-start | bytes 49156
Sparse Core Ops, SparseCore 0:
  114.0 36.1 reduce-scatter.1
where the time goes:
time: 237 us; the launch traced here: 236 us
  blocking collectives  103 us (43%)
  local copies, waits for them, and re-layouts  40.5 us (17%)
  matrix products  38.3 us (16%)
  waiting for transfers between devices  36.2 us (15%)
  between operations  16.2 us (7%)
    reduce_scatter x1, waiting for transfers between devices, body(): share = lax.psum_scatter(panels, 'grp', scatter_dimension=1, tiled=True)  36.2 us
    psum x1, blocking collectives, body(): proj = lax.psum(proj_terms, 'dev').astype(jnp.bfloat16)  31.6 us
    psum x1, blocking collectives, body(): gmat = lax.psum(gram_local, 'dev')  25.9 us
    all_gather x1, blocking collectives, body(): lax.all_gather(factor_three, 'dev', axis=0, tiled=True)  15.9 us
    psum x1, blocking collectives, body(): rows = lax.psum(row_terms, 'grp')  15.4 us
    dot_general x1, matrix products, body(): jnp.einsum('bl,bam->lam', assign, contrib, precision=lax.Precision.HIGHEST)  15.3 us
    reshape x1, local copies, waits for them, and re-layouts, body(): contrib = contrib.reshape(slot_count, edge, rank_width * rank_width)  14.8 us
    all_gather x1, blocking collectives, body(): lax.all_gather(factor_two, 'dev', axis=0, tiled=True)  14 us
  transfers between devices with their start and end apart: 1, of which 1 were waited for; matrix products, arithmetic and copies ran while one was open for 0% of the time, Pallas kernels for 0%

commit v1 on v0

v1 whole, which is shorter than its diff:
```python
import functools

import jax
import jax.numpy as jnp
from jax import lax
from jax.experimental import pallas as pl
from jax.experimental.pallas import tpu as pltpu
from jax.sharding import PartitionSpec as P

F32 = jnp.float32
BF16 = jnp.bfloat16
VMEM = pl.BlockSpec(memory_space=pltpu.VMEM)
SMEM = pl.BlockSpec(memory_space=pltpu.SMEM)
DIRECT_LIMIT = 8


def swap(x, axis, size, mask):
    return lax.ppermute(x, axis, [(i, i ^ mask) for i in range(size)])


def is_direct(size):
    return size <= DIRECT_LIMIT and size & (size - 1) == 0


def params(limit):
    return pltpu.CompilerParams(vmem_limit_bytes=limit)


def dup(u):
    return jnp.concatenate([u, u], axis=1)


def contract_kernel(
    coords, counts, row_place, me, table, block, out, zbuf, vbuf, wbuf, *, slots, row_blocks, edge, rank
):
    s = pl.program_id(0)
    half = edge // 2
    lanes = 2 * rank
    depth = slots * edge
    pos = [row_place[coords[m, s]] for m in range(3)]

    def factor_rows(p):
        piece = (p // row_blocks) ^ me[0]
        at = (piece * row_blocks + p % row_blocks) * edge
        return table[pl.ds(pl.multiple_of(at, edge), edge), :]

    u2 = dup(factor_rows(pos[1])[:, :rank].astype(F32))
    u3 = dup(factor_rows(pos[2])[:, rank:].astype(F32))
    lane = lax.broadcasted_iota(jnp.int32, (edge, lanes), 1)
    low = lane < rank
    low3 = jnp.where(low, u3, 0.0).astype(BF16)
    high3 = jnp.where(low, 0.0, u3).astype(BF16)
    none = jnp.zeros_like(low3)
    weight = jnp.concatenate(
        [
            jnp.concatenate([low3, none], axis=1),
            jnp.concatenate([none, low3], axis=1),
            jnp.concatenate([high3, none], axis=1),
            jnp.concatenate([none, high3], axis=1),
        ],
        axis=0,
    )
    slabs = []
    for j in range(half):
        cols = slice(j * 2 * edge, (j + 1) * 2 * edge)
        slabs.append(jnp.concatenate([block[0, :half, cols], block[0, half:, cols]], axis=1))
    first = jnp.dot(jnp.concatenate(slabs, axis=0), weight, preferred_element_type=F32)
    for j in range(half):
        for q in range(2):
            zbuf[pl.ds(s * edge + 2 * j + q, half, stride=depth), :] = first[
                j * half : (j + 1) * half, q * lanes : (q + 1) * lanes
            ]
    mine = jnp.where(s < counts[0], pos[0] % row_blocks, row_blocks)
    for p in range(row_blocks // 2):
        keep = 2 * p + lane // rank == mine
        wbuf[pl.ds(pl.multiple_of(s * edge, edge), edge), p * lanes : (p + 1) * lanes] = jnp.where(
            keep, u2, 0.0
        )

    @pl.when(s == slots - 1)
    def _():
        left = wbuf[...].T.astype(BF16)
        rows = row_blocks * rank
        for a in range(0, half, 2):
            right = jnp.concatenate(
                [zbuf[a * depth : (a + 1) * depth, :], zbuf[(a + 1) * depth : (a + 2) * depth, :]], axis=1
            ).astype(BF16)
            panel = jnp.dot(left, right, preferred_element_type=F32)
            for b in range(2):
                vbuf[pl.ds(a + b, rows, stride=half), :] = panel[:, b * lanes : (b + 1) * lanes]
        share = rank // out.shape[0]
        for p in range(row_blocks):
            for r in range(rank):
                at = (p * rank + r) * half
                out[r // share, p * half : (p + 1) * half, (r % share) * lanes : (r % share + 1) * lanes] = (
                    vbuf[at : at + half, :].astype(BF16)
                )


def contract(coords, counts, row_place, me, table, blocks, row_blocks, rank, shares):
    slots, edge, width = blocks.shape
    half, lanes = edge // 2, 2 * rank
    out = (shares, row_blocks * half, rank // shares * lanes)
    flops = 2 * slots * edge * width * 4 * edge + 2 * row_blocks * rank * slots * edge * edge * rank
    return pl.pallas_call(
        functools.partial(contract_kernel, slots=slots, row_blocks=row_blocks, edge=edge, rank=rank),
        grid=(slots,),
        in_specs=[SMEM, SMEM, SMEM, SMEM, VMEM, pl.BlockSpec((1, edge, width), lambda s: (s, 0, 0))],
        out_specs=VMEM,
        out_shape=jax.ShapeDtypeStruct(out, BF16),
        scratch_shapes=[
            pltpu.VMEM((half * slots * edge, lanes), F32),
            pltpu.VMEM((row_blocks * rank * half, lanes), F32),
            pltpu.VMEM((slots * edge, row_blocks * rank), F32),
        ],
        compiler_params=params(48 * 1024 * 1024),
        cost_estimate=pl.CostEstimate(
            flops=flops, bytes_accessed=2 * blocks.size + 4 * row_blocks * edge * rank * rank, transcendentals=0
        ),
        name="contract",
    )(coords, counts, row_place, me, table, blocks)


def project_kernel(core, old, *refs, rank, row_blocks):
    pieces, panel, keep, send, buf = refs[:-4], refs[-4], refs[-3], refs[-2], refs[-1]
    total = pieces[0][...].astype(F32)
    for piece in pieces[1:]:
        total = total + piece[...].astype(F32)
    total = total.astype(BF16)
    panel[...] = total
    edge = old.shape[0] // row_blocks
    half, lanes = edge // 2, 2 * rank
    parts = []
    for q in range(2):
        rows = [old[p * edge + q * half : p * edge + (q + 1) * half, :] for p in range(row_blocks)]
        parts.append(jnp.concatenate(rows, axis=0))
    left = jnp.concatenate(parts, axis=1).astype(F32).T.astype(BF16)
    both = jnp.dot(left, total, preferred_element_type=F32)
    low = lax.broadcasted_iota(jnp.int32, (rank, lanes), 1) < rank
    sums = []
    for r in range(total.shape[1] // lanes):
        cols = slice(r * lanes, (r + 1) * lanes)
        own = jnp.where(low, both[:rank, cols], both[rank:, cols])
        sums.append(own + pltpu.roll(own, rank, 1))
    for r in range(0, len(sums), 2):
        buf[:, r // 2 * lanes : (r // 2 + 1) * lanes] = jnp.where(low, sums[r], sums[r + 1])
    count = keep.shape[0]
    if count == rank:
        keep[...] = buf[...].astype(BF16)
        send[...] = jnp.zeros_like(send)
    else:
        keep[...] = buf[pl.ds(pl.multiple_of(core[0] * count, count), count), :].astype(BF16)
        send[...] = buf[pl.ds(pl.multiple_of((1 - core[0]) * count, count), count), :].astype(BF16)


def project(core, old, pieces, rank, row_blocks, halves):
    height, width = pieces[0].shape
    count = rank // halves
    shapes = [
        jax.ShapeDtypeStruct((height, width), BF16),
        jax.ShapeDtypeStruct((count, width // 2), BF16),
        jax.ShapeDtypeStruct((count, width // 2), BF16),
    ]
    return pl.pallas_call(
        functools.partial(project_kernel, rank=rank, row_blocks=row_blocks),
        in_specs=[SMEM] + [VMEM] * (1 + len(pieces)),
        out_specs=[VMEM] * 3,
        out_shape=shapes,
        scratch_shapes=[pltpu.VMEM((rank, width // 2), F32)],
        compiler_params=params(32 * 1024 * 1024),
        name="project",
    )(core, old, *pieces)


def rows_kernel(core, panel, own, other, out, buf, *, rank):
    lanes = 2 * rank
    if own.shape[0] == rank:
        buf[...] = own[...].astype(F32)
    else:
        count = own.shape[0]
        buf[pl.ds(pl.multiple_of(core[0] * count, count), count), :] = own[...].astype(F32)
        buf[pl.ds(pl.multiple_of((1 - core[0]) * count, count), count), :] = other[...].astype(F32)
    low = lax.broadcasted_iota(jnp.int32, (rank, lanes), 1) < rank
    upper, lower = [], []
    for r in range(buf.shape[1] // lanes):
        value = buf[:, r * lanes : (r + 1) * lanes]
        turned = pltpu.roll(value, rank, 1)
        zero = jnp.zeros_like(value)
        upper += [jnp.where(low, value, zero).astype(BF16), jnp.where(low, turned, zero).astype(BF16)]
        lower += [jnp.where(low, zero, turned).astype(BF16), jnp.where(low, zero, value).astype(BF16)]
    right = jnp.concatenate([jnp.concatenate(upper, axis=1), jnp.concatenate(lower, axis=1)], axis=0)
    out[...] = lax.dot_general(
        panel[...], right, (((1,), (1,)), ((), ())), preferred_element_type=F32
    ).astype(BF16)


def row_terms(core, panel, own, other, rank):
    return pl.pallas_call(
        functools.partial(rows_kernel, rank=rank),
        in_specs=[SMEM] + [VMEM] * 3,
        out_specs=VMEM,
        out_shape=jax.ShapeDtypeStruct((panel.shape[0], 2 * rank), BF16),
        scratch_shapes=[pltpu.VMEM((rank, panel.shape[1] // 2), F32)],
        compiler_params=params(32 * 1024 * 1024),
        name="row_terms",
    )(core, panel, own, other)


def gram_kernel(*refs, rank):
    pieces, rows, gram = refs[:-2], refs[-2], refs[-1]
    total = pieces[0][...].astype(F32)
    for piece in pieces[1:]:
        total = total + piece[...].astype(F32)
    rows[...] = total
    full = jnp.dot(total.T, total, precision=lax.Precision.HIGHEST, preferred_element_type=F32)
    gram[...] = full[:rank, :rank] + full[rank:, rank:]


def gram_terms(pieces, rank):
    shapes = [jax.ShapeDtypeStruct(pieces[0].shape, F32), jax.ShapeDtypeStruct((rank, rank), F32)]
    return pl.pallas_call(
        functools.partial(gram_kernel, rank=rank),
        in_specs=[VMEM] * len(pieces),
        out_specs=[VMEM] * 2,
        out_shape=shapes,
        compiler_params=params(32 * 1024 * 1024),
        name="gram_terms",
    )(*pieces)


def body(blocks, coords, counts, row_place, factor_one, factor_two, factor_three):
    edge = blocks.shape[1]
    rank = factor_one.shape[1] // edge
    row_blocks = factor_one.shape[0]
    half = edge // 2
    n_grp, n_dev = lax.axis_size("grp"), lax.axis_size("dev")
    direct = is_direct(n_dev)
    index = lax.axis_index("dev").astype(jnp.int32)
    core = (index % 2).reshape(1)

    packed = jnp.concatenate(
        [f.reshape(row_blocks * edge, rank) for f in (factor_two, factor_three)], axis=1
    )
    if direct:
        same = [packed] + [swap(packed, "dev", n_dev, m) for m in range(2, n_dev, 2)]
        same = jnp.stack(same)
        table = jnp.stack([same, swap(same, "dev", n_dev, 1)], axis=1)
        table = table.reshape(n_dev * row_blocks * edge, 2 * rank)
        me = index.reshape(1)
    else:
        table = lax.all_gather(packed, "dev", axis=0, tiled=True)
        me = jnp.zeros_like(core)

    shares = contract(coords, counts, row_place, me, table, blocks, row_blocks, rank, n_grp)
    if is_direct(n_grp):
        group = lax.axis_index("grp")
        pieces = [lax.dynamic_index_in_dim(shares, group, 0, keepdims=False)]
        for m in range(1, n_grp):
            part = lax.dynamic_index_in_dim(shares, group ^ m, 0, keepdims=False)
            pieces.append(swap(part, "grp", n_grp, m))
    else:
        got = lax.all_to_all(shares, "grp", 0, 0)
        pieces = [got[g] for g in range(n_grp)]

    old = factor_one.reshape(row_blocks * edge, rank)
    panel, keep, send = project(core, old, pieces, rank, row_blocks, 2 if direct else 1)
    if direct:
        chip = (keep.astype(F32) + swap(send, "dev", n_dev, 1).astype(F32)).astype(BF16)
        total = chip.astype(F32)
        for m in range(2, n_dev, 2):
            total = total + swap(chip, "dev", n_dev, m).astype(F32)
        own = total.astype(BF16)
        other = swap(own, "dev", n_dev, 1)
    else:
        own = lax.psum(keep.astype(F32), "dev").astype(BF16)
        other = send
    terms = row_terms(core, panel, own, other, rank)
    if is_direct(n_grp):
        parts = [terms] + [swap(terms, "grp", n_grp, m) for m in range(1, n_grp)]
    else:
        got = lax.all_gather(terms, "grp")
        parts = [got[g] for g in range(n_grp)]
    rows, gram_local = gram_terms(parts, rank)
    if direct:
        chip = gram_local + swap(gram_local, "dev", n_dev, 1)
        gmat = chip
        for m in range(2, n_dev, 2):
            gmat = gmat + swap(chip, "dev", n_dev, m)
    else:
        gmat = lax.psum(gram_local, "dev")
    trace_value = jnp.trace(gmat)
    rows = rows.reshape(row_blocks, half, 2, rank).transpose(0, 2, 1, 3).reshape(row_blocks, edge * rank)
    rows_total = row_blocks * edge * n_dev
    new_rows = rows * lax.rsqrt(trace_value / (rows_total * rank))
    gram = gmat * (rank / trace_value)
    return (new_rows, gram)


def solution(mesh):
    placed = (
        P(("grp", "dev"), None, None),
        P(None, ("grp", "dev")),
        P(("grp", "dev")),
        P(),
        P("dev", None),
        P("dev", None),
        P("dev", None),
    )
    return jax.shard_map(
        body, mesh=mesh, in_specs=placed, out_specs=(P("dev", None), P()), check_vma=False
    )
```

time: 237 us -> 77.9 us (0.33)
  blocking collectives: 103 us -> 0 us
  matrix products: 38.3 us -> 0 us
  local copies, waits for them, and re-layouts: 40.5 us -> 6.19 us
  starting transfers between devices: 0.04 us -> 21.9 us
  between operations: 16.2 us -> 2.84 us
  Pallas kernels: 0 us -> 13.1 us
  waiting for transfers between devices: 36.2 us -> 32 us
    psum x3 -> x0, blocking collectives: 73 us -> none  [the longest x1 31.6 us: body(): proj = lax.psum(proj_terms, 'dev').astype(jnp.bfloat16)]
    dot_general x8 -> x0, matrix products: 38.3 us -> none  [the longest x1 15.3 us: body(): jnp.einsum('bl,bam->lam', assign, contrib, precision=lax.Precision.HIGHEST)]
    reduce_scatter x1 -> x0, waiting for transfers between devices: 36.2 us -> none  [body(): share = lax.psum_scatter(panels, 'grp', scatter_dimension=1, tiled=True)]
    reshape x7 -> x3, local copies, waits for them, and re-layouts: 36.9 us -> 1.72 us  [the longest x2 1.62 us: body(): f.reshape(row_blocks * edge, rank)]
    ppermute x0 -> x19, waiting for transfers between devices: none -> 32 us  [swap(): return lax.ppermute(x, axis, [(i, i ^ mask) for i in range(size)])]
    all_gather x2 -> x0, blocking collectives: 29.9 us -> none  [the longest x1 15.9 us: body(): lax.all_gather(factor_three, 'dev', axis=0, tiled=True)]
    ppermute x0 -> x19, starting transfers between devices: none -> 21.9 us  [swap(): return lax.ppermute(x, axis, [(i, i ^ mask) for i in range(size)])]
    pallas_call x0 -> x4, Pallas kernels: none -> 13.1 us  [the longest x1 11.8 us: contract(): pl.pallas_call(functools.partial(contract_kernel, slots=slots, row_blocks...]
  transfers between devices with their start and end apart: 1 -> 19, of which waited for: 1 -> 15; matrix products, arithmetic and copies ran while one was open for 0% -> 0% of each run, Pallas kernels for 0% -> 0%
where the time goes in v1:
time: 77.9 us; the launch traced here: 77.5 us
  waiting for transfers between devices  32 us (41%)
  starting transfers between devices  21.9 us (28%)
  Pallas kernels  13.1 us (17%)
  local copies, waits for them, and re-layouts  6.19 us (8%)
  between operations  2.84 us (4%)
  other arithmetic  1.43 us (2%)
    ppermute x19, waiting for transfers between devices, swap(): return lax.ppermute(x, axis, [(i, i ^ mask) for i in range(size)])  32 us
    ppermute x19, starting transfers between devices, swap(): return lax.ppermute(x, axis, [(i, i ^ mask) for i in range(size)])  21.9 us
    pallas_call x1, Pallas kernels, contract(): pl.pallas_call(functools.partial(contract_kernel, slots=slots, row_blocks...  11.8 us
    unnamed x8, local copies, waits for them, and re-layouts  3.53 us
    reshape x2, local copies, waits for them, and re-layouts, body(): f.reshape(row_blocks * edge, rank)  1.62 us
  transfers between devices with their start and end apart: 19, of which 15 were waited for; matrix products, arithmetic and copies ran while one was open for 0% of the time, Pallas kernels for 0%

profile of v1, /device:TPU:0, one launch (start us, length us, event | category | flops | bytes accessed | tf_op | source)
XLA Modules:
  0.0 77.5 jit_solution(4622149293786310373)
XLA Ops:
  0.6 0.8 %reshape.31 = bf16[128,64]{1,0:T(8,128)(2,1)S(1)} reshape(bf16[2,4096]{1,0:T(2,128)(2,1)} %param.12) | data formatting | bytes 32768 | tf_op jit(solution)/shard_map/reshape | solution.py:242
  1.4 0.8 %reshape.32 = bf16[128,64]{1,0:T(8,128)(2,1)S(1)} reshape(bf16[2,4096]{1,0:T(2,128)(2,1)} %param.13) | data formatting | bytes 32768 | tf_op jit(solution)/shard_map/reshape | solution.py:242
  2.3 0.1 pad_maximum_fusion.2
  2.3 3.1 %collective-permute-start = (bf16[128,128]{1,0:T(8,128)(2,1)S(1)}, bf16[128,128]{1,0:T(8,128)(2,1)S(1)}, u32[]{:S(2)}, u32[]{:S(2)}) collective-permute-start(bf16[128,128]{1,0:T(8,128)(2,1)S(1)} %pad_maximum_fusion.2), channel_id=1, source_target_pairs={{0,2},{1,3},{2,0},{3,1},{4,6},{5,7},{6,4},{7,5},{8,10},{9,11},{10,... | collective-permute-start | bytes 98312 | tf_op jit(solution)/shard_map/ppermute | solution.py:18
  5.4 2.6 %collective-permute-start.1 = (bf16[128,128]{1,0:T(8,128)(2,1)S(1)}, bf16[128,128]{1,0:T(8,128)(2,1)S(1)}, u32[]{:S(2)}, u32[]{:S(2)}) collective-permute-start(bf16[128,128]{1,0:T(8,128)(2,1)S(1)} %pad_maximum_fusion.2), channel_id=1, source_target_pairs={{0,4},{1,5},{2,6},{3,7},{4,0},{5,1},{6,2},{7,3},{8,12},{9,13},{10,... | collective-permute-start | bytes 98312 | tf_op jit(solution)/shard_map/ppermute | solution.py:18
  8.0 2.8 %collective-permute-done.1 = bf16[128,128]{1,0:T(8,128)(2,1)S(1)} collective-permute-done((bf16[128,128]{1,0:T(8,128)(2,1)S(1)}, bf16[128,128]{1,0:T(8,128)(2,1)S(1)}, u32[]{:S(2)}, u32[]{:S(2)}) %collective-permute-start.1) | collective-permute-done | bytes 32800 | tf_op jit(solution)/shard_map/ppermute | solution.py:18
  10.8 2.9 %collective-permute-done.2 = bf16[128,128]{1,0:T(8,128)(2,1)S(1)} collective-permute-done((bf16[128,128]{1,0:T(8,128)(2,1)S(1)}, bf16[128,128]{1,0:T(8,128)(2,1)S(1)}, u32[]{:S(2)}, u32[]{:S(2)}) %collective-permute-start.2) | collective-permute-done | bytes 32800 | tf_op jit(solution)/shard_map/ppermute | solution.py:18
  13.8 0.1 collective-permute-start.3
  14.5 0.7 collective-permute-done.3
  15.3 2.2 %copy-done = bf16[8,64,4096]{2,1,0:T(8,128)(2,1)S(1)} copy-done((bf16[8,64,4096]{2,1,0:T(8,128)(2,1)S(1)}, bf16[8,64,4096]{2,1,0:T(8,128)(2,1)}, u32[]{:S(2)}) %copy-start) | copy-done | bytes 4194328
  17.4 0.7 copy-done.1
  18.1 0.7 copy-done.2
  18.8 11.8 %contract.1 = bf16[4,64,2048]{2,1,0:T(8,128)(2,1)S(1)} custom-call(s32[3,8]{1,0:T(4,128)S(1)} %copy-done.1, s32[1]{0:T(128)S(6)} %copy.13.counts, s32[16]{0:T(128)S(1)} %copy-done.2, s32[1]{0:T(128)} %bitcast.1.me, bf16[1024,128]{1,0:T(8,128)(2,1)S(1)} %bitcast.21, bf16[8,64,4096]{2,1,0:T(8,128)(2,1)S(1)} %copy-done), custom_call_target="tpu_custom_call" | custom-call | flops 1610612736 | bytes 6291456 | tf_op jit(solution)/shard_map/contract/pallas_call | solution.py:105
  30.6 0.1 dynamic-slice_bitcast_fusion
  30.7 1.5 %collective-permute-start.4 = (bf16[64,2048]{1,0:T(8,128)(2,1)S(1)}, bf16[64,2048]{1,0:T(8,128)(2,1)S(1)}, u32[]{:S(2)}, u32[]{:S(2)}) collective-permute-start(bf16[64,2048]{1,0:T(8,128)(2,1)S(1)} %get-tuple-element.16), channel_id=1, source_target_pairs={{0,8},{8,0},{16,24},{24,16},{1,9},{9,1},{17,25},{25,17},{2,10},{10... | collective-permute-start | bytes 786440 | tf_op jit(solution)/shard_map/ppermute | solution.py:18
  32.2 1.5 %collective-permute-start.5 = (bf16[64,2048]{1,0:T(8,128)(2,1)S(1)}, bf16[64,2048]{1,0:T(8,128)(2,1)S(1)}, u32[]{:S(2)}, u32[]{:S(2)}) collective-permute-start(bf16[64,2048]{1,0:T(8,128)(2,1)S(1)} %get-tuple-element.15), channel_id=1, source_target_pairs={{0,16},{8,24},{16,0},{24,8},{1,17},{9,25},{17,1},{25,9},{2,18},{10... | collective-permute-start | bytes 786440 | tf_op jit(solution)/shard_map/ppermute | solution.py:18
  33.8 0.5 collective-permute-start.6
  34.3 0.1 reshape.29.old
  34.4 5.6 %collective-permute-done.4.refs_1_ = bf16[64,2048]{1,0:T(8,128)(2,1)S(1)} collective-permute-done((bf16[64,2048]{1,0:T(8,128)(2,1)S(1)}, bf16[64,2048]{1,0:T(8,128)(2,1)S(1)}, u32[]{:S(2)}, u32[]{:S(2)}) %collective-permute-start.4) | collective-permute-done | bytes 262176 | tf_op jit(solution)/shard_map/ppermute | solution.py:18
  39.9 6.0 %collective-permute-done.5.refs_2_ = bf16[64,2048]{1,0:T(8,128)(2,1)S(1)} collective-permute-done((bf16[64,2048]{1,0:T(8,128)(2,1)S(1)}, bf16[64,2048]{1,0:T(8,128)(2,1)S(1)}, u32[]{:S(2)}, u32[]{:S(2)}) %collective-permute-start.5) | collective-permute-done | bytes 262176 | tf_op jit(solution)/shard_map/ppermute | solution.py:18
  45.9 0.5 project.1
  46.5 0.1 collective-permute-start.7
  46.6 1.2 %collective-permute-done.7 = bf16[32,1024]{1,0:T(8,128)(2,1)S(1)} collective-permute-done((bf16[32,1024]{1,0:T(8,128)(2,1)S(1)}, bf16[32,1024]{1,0:T(8,128)(2,1)S(1)}, u32[]{:S(2)}, u32[]{:S(2)}) %collective-permute-start.7) | collective-permute-done | bytes 65568 | tf_op jit(solution)/shard_map/ppermute | solution.py:18
  47.8 0.4 collective-permute-start.10
  48.3 4.0 %collective-permute-start.9 = (bf16[32,1024]{1,0:T(8,128)(2,1)S(1)}, bf16[32,1024]{1,0:T(8,128)(2,1)S(1)}, u32[]{:S(2)}, u32[]{:S(2)}) collective-permute-start(bf16[32,1024]{1,0:T(8,128)(2,1)S(1)} %add_convert_fusion.1), channel_id=1, source_target_pairs={{0,4},{1,5},{2,6},{3,7},{4,0},{5,1},{6,2},{7,3},{8,12},{9,13},{10,... | collective-permute-start | bytes 196616 | tf_op jit(solution)/shard_map/ppermute | solution.py:18
  52.3 2.4 %collective-permute-done.10 = bf16[32,1024]{1,0:T(8,128)(2,1)S(1)} collective-permute-done((bf16[32,1024]{1,0:T(8,128)(2,1)S(1)}, bf16[32,1024]{1,0:T(8,128)(2,1)S(1)}, u32[]{:S(2)}, u32[]{:S(2)}) %collective-permute-start.10) | collective-permute-done | bytes 65568 | tf_op jit(solution)/shard_map/ppermute | solution.py:18
  54.6 2.0 %collective-permute-done.9 = bf16[32,1024]{1,0:T(8,128)(2,1)S(1)} collective-permute-done((bf16[32,1024]{1,0:T(8,128)(2,1)S(1)}, bf16[32,1024]{1,0:T(8,128)(2,1)S(1)}, u32[]{:S(2)}, u32[]{:S(2)}) %collective-permute-start.9) | collective-permute-done | bytes 65568 | tf_op jit(solution)/shard_map/ppermute | solution.py:18
  56.7 0.1 collective-permute-start.11
  56.8 1.2 %collective-permute-done.11.other = bf16[32,1024]{1,0:T(8,128)(2,1)S(1)} collective-permute-done((bf16[32,1024]{1,0:T(8,128)(2,1)S(1)}, bf16[32,1024]{1,0:T(8,128)(2,1)S(1)}, u32[]{:S(2)}, u32[]{:S(2)}) %collective-permute-start.11) | collective-permute-done | bytes 65568 | tf_op jit(solution)/shard_map/ppermute | solution.py:18
  58.0 0.4 row_terms.1.refs_0_
  58.4 0.6 collective-permute-start.12
  59.0 0.8 %collective-permute-start.13 = (bf16[64,128]{1,0:T(8,128)(2,1)S(1)}, bf16[64,128]{1,0:T(8,128)(2,1)S(1)}, u32[]{:S(2)}, u32[]{:S(2)}) collective-permute-start(bf16[64,128]{1,0:T(8,128)(2,1)S(1)} %row_terms.1.refs_0_), channel_id=1, source_target_pairs={{0,16},{8,24},{16,0},{24,8},{1,17},{9,25},{17,1},{25,9},{2,18},{10... | collective-permute-start | bytes 49160 | tf_op jit(solution)/shard_map/ppermute | solution.py:18
  59.8 2.1 %collective-permute-start.14 = (bf16[64,128]{1,0:T(8,128)(2,1)S(1)}, bf16[64,128]{1,0:T(8,128)(2,1)S(1)}, u32[]{:S(2)}, u32[]{:S(2)}) collective-permute-start(bf16[64,128]{1,0:T(8,128)(2,1)S(1)} %row_terms.1.refs_0_), channel_id=1, source_target_pairs={{0,24},{8,16},{16,8},{24,0},{1,25},{9,17},{17,9},{25,1},{2,26},{10... | collective-permute-start | bytes 49160 | tf_op jit(solution)/shard_map/ppermute | solution.py:18
  62.0 0.2 collective-permute-done.12.refs_1_
  62.2 0.5 collective-permute-done.13.refs_2_
  62.8 1.7 %collective-permute-done.14.refs_3_ = bf16[64,128]{1,0:T(8,128)(2,1)S(1)} collective-permute-done((bf16[64,128]{1,0:T(8,128)(2,1)S(1)}, bf16[64,128]{1,0:T(8,128)(2,1)S(1)}, u32[]{:S(2)}, u32[]{:S(2)}) %collective-permute-start.14) | collective-permute-done | bytes 16416 | tf_op jit(solution)/shard_map/ppermute | solution.py:18
  64.5 0.3 gram_terms.1
  64.8 0.1 collective-permute-start.15
  64.9 1.2 %collective-permute-done.15 = f32[64,64]{1,0:T(8,128)S(1)} collective-permute-done((f32[64,64]{1,0:T(8,128)S(1)}, f32[64,64]{1,0:T(8,128)S(1)}, u32[]{:S(2)}, u32[]{:S(2)}) %collective-permute-start.15) | collective-permute-done | bytes 16416 | tf_op jit(solution)/shard_map/ppermute | solution.py:18
  66.1 1.3 %collective-permute-start.16 = (f32[64,64]{1,0:T(8,128)S(1)}, f32[64,64]{1,0:T(8,128)S(1)}, u32[]{:S(2)}, u32[]{:S(2)}) collective-permute-start(f32[64,64]{1,0:T(8,128)S(1)} %add.50), channel_id=1, source_target_pairs={{0,2},{1,3},{2,0},{3,1},{4,6},{5,7},{6,4},{7,5},{8,10},{9,11},{10,... | collective-permute-start | bytes 49160 | tf_op jit(solution)/shard_map/ppermute | solution.py:18
  67.4 0.9 %collective-permute-start.17 = (f32[64,64]{1,0:T(8,128)S(1)}, f32[64,64]{1,0:T(8,128)S(1)}, u32[]{:S(2)}, u32[]{:S(2)}) collective-permute-start(f32[64,64]{1,0:T(8,128)S(1)} %add.50), channel_id=1, source_target_pairs={{0,4},{1,5},{2,6},{3,7},{4,0},{5,1},{6,2},{7,3},{8,12},{9,13},{10,... | collective-permute-start | bytes 49160 | tf_op jit(solution)/shard_map/ppermute | solution.py:18
  68.3 2.2 %collective-permute-start.18 = (f32[64,64]{1,0:T(8,128)S(1)}, f32[64,64]{1,0:T(8,128)S(1)}, u32[]{:S(2)}, u32[]{:S(2)}) collective-permute-start(f32[64,64]{1,0:T(8,128)S(1)} %add.50), channel_id=1, source_target_pairs={{0,6},{1,7},{2,4},{3,5},{4,2},{5,3},{6,0},{7,1},{8,14},{9,15},{10,... | collective-permute-start | bytes 49160 | tf_op jit(solution)/shard_map/ppermute | solution.py:18
  70.5 2.4 %collective-permute-done.17 = f32[64,64]{1,0:T(8,128)S(1)} collective-permute-done((f32[64,64]{1,0:T(8,128)S(1)}, f32[64,64]{1,0:T(8,128)S(1)}, u32[]{:S(2)}, u32[]{:S(2)}) %collective-permute-start.17) | collective-permute-done | bytes 16416 | tf_op jit(solution)/shard_map/ppermute | solution.py:18
  72.9 1.1 %collective-permute-done.18 = f32[64,64]{1,0:T(8,128)S(1)} collective-permute-done((f32[64,64]{1,0:T(8,128)S(1)}, f32[64,64]{1,0:T(8,128)S(1)}, u32[]{:S(2)}, u32[]{:S(2)}) %collective-permute-start.18) | collective-permute-done | bytes 16416 | tf_op jit(solution)/shard_map/ppermute | solution.py:18
  74.0 0.6 select_reduce_fusion
  76.0 0.1 mul.23
  76.1 0.7 mul.25
  76.8 0.6 broadcast_multiply_fusion
  (19 shorter events, 0.2 us)
Async XLA Ops:
  2.3 5.7 %collective-permute-start = (bf16[128,128]{1,0:T(8,128)(2,1)S(1)}, bf16[128,128]{1,0:T(8,128)(2,1)S(1)}, u32[]{:S(2)}, u32[]{:S(2)}) collective-permute-start(bf16[128,128]{1,0:T(8,128)(2,1)S(1)} %pad_maximum_fusion.2), channel_id=1, source_target_pairs={{0,2},{1,3},{2,0},{3,1},{4,6},{5,7},{6,4},{7,5},{8,10},{9,11},{10,... | collective-permute-start | bytes 98312 | tf_op jit(solution)/shard_map/ppermute | solution.py:18
  5.4 5.4 %collective-permute-start.1 = (bf16[128,128]{1,0:T(8,128)(2,1)S(1)}, bf16[128,128]{1,0:T(8,128)(2,1)S(1)}, u32[]{:S(2)}, u32[]{:S(2)}) collective-permute-start(bf16[128,128]{1,0:T(8,128)(2,1)S(1)} %pad_maximum_fusion.2), channel_id=1, source_target_pairs={{0,4},{1,5},{2,6},{3,7},{4,0},{5,1},{6,2},{7,3},{8,12},{9,13},{10,... | collective-permute-start | bytes 98312 | tf_op jit(solution)/shard_map/ppermute | solution.py:18
  8.0 5.7 %collective-permute-start.2 = (bf16[128,128]{1,0:T(8,128)(2,1)S(1)}, bf16[128,128]{1,0:T(8,128)(2,1)S(1)}, u32[]{:S(2)}, u32[]{:S(2)}) collective-permute-start(bf16[128,128]{1,0:T(8,128)(2,1)S(1)} %pad_maximum_fusion.2), channel_id=1, source_target_pairs={{0,6},{1,7},{2,4},{3,5},{4,2},{5,3},{6,0},{7,1},{8,14},{9,15},{10,... | collective-permute-start | bytes 98312 | tf_op jit(solution)/shard_map/ppermute | solution.py:18
  13.8 1.4 %collective-permute-start.3 = (bf16[4,128,128]{2,1,0:T(8,128)(2,1)S(1)}, bf16[4,128,128]{2,1,0:T(8,128)(2,1)S(1)}, u32[]{:S(2)}, u32[]{:S(2)}) collective-permute-start(bf16[4,128,128]{2,1,0:T(8,128)(2,1)S(1)} %get-tuple-element.19), channel_id=1, source_target_pairs={{0,1},{1,0},{2,3},{3,2},{4,5},{5,4},{6,7},{7,6},{8,9},{9,8},{10,11... | collective-permute-start | bytes 393224 | tf_op jit(solution)/shard_map/ppermute | solution.py:18
  15.2 19.0 %copy-start.3 = (bf16[2,4096]{1,0:T(2,128)(2,1)S(1)}, bf16[2,4096]{1,0:T(2,128)(2,1)}, u32[]{:S(2)}) copy-start(bf16[2,4096]{1,0:T(2,128)(2,1)} %param.11) | copy-start | bytes 49156
  15.3 2.2 %copy-start = (bf16[8,64,4096]{2,1,0:T(8,128)(2,1)S(1)}, bf16[8,64,4096]{2,1,0:T(8,128)(2,1)}, u32[]{:S(2)}) copy-start(bf16[8,64,4096]{2,1,0:T(8,128)(2,1)} %block.1) | copy-start | bytes 12582916
  17.4 0.7 copy-start.1
  18.1 0.7 copy-start.2
  30.7 9.2 %collective-permute-start.4 = (bf16[64,2048]{1,0:T(8,128)(2,1)S(1)}, bf16[64,2048]{1,0:T(8,128)(2,1)S(1)}, u32[]{:S(2)}, u32[]{:S(2)}) collective-permute-start(bf16[64,2048]{1,0:T(8,128)(2,1)S(1)} %get-tuple-element.16), channel_id=1, source_target_pairs={{0,8},{8,0},{16,24},{24,16},{1,9},{9,1},{17,25},{25,17},{2,10},{10... | collective-permute-start | bytes 786440 | tf_op jit(solution)/shard_map/ppermute | solution.py:18
  32.2 13.7 %collective-permute-start.5 = (bf16[64,2048]{1,0:T(8,128)(2,1)S(1)}, bf16[64,2048]{1,0:T(8,128)(2,1)S(1)}, u32[]{:S(2)}, u32[]{:S(2)}) collective-permute-start(bf16[64,2048]{1,0:T(8,128)(2,1)S(1)} %get-tuple-element.15), channel_id=1, source_target_pairs={{0,16},{8,24},{16,0},{24,8},{1,17},{9,25},{17,1},{25,9},{2,18},{10... | collective-permute-start | bytes 786440 | tf_op jit(solution)/shard_map/ppermute | solution.py:18
  33.8 12.2 %collective-permute-start.6 = (bf16[64,2048]{1,0:T(8,128)(2,1)S(1)}, bf16[64,2048]{1,0:T(8,128)(2,1)S(1)}, u32[]{:S(2)}, u32[]{:S(2)}) collective-permute-start(bf16[64,2048]{1,0:T(8,128)(2,1)S(1)} %get-tuple-element.14), channel_id=1, source_target_pairs={{0,24},{8,16},{16,8},{24,0},{1,25},{9,17},{17,9},{25,1},{2,26},{10... | collective-permute-start | bytes 786440 | tf_op jit(solution)/shard_map/ppermute | solution.py:18
  46.5 1.3 %collective-permute-start.7 = (bf16[32,1024]{1,0:T(8,128)(2,1)S(1)}, bf16[32,1024]{1,0:T(8,128)(2,1)S(1)}, u32[]{:S(2)}, u32[]{:S(2)}) collective-permute-start(bf16[32,1024]{1,0:T(8,128)(2,1)S(1)} %get-tuple-element.9), channel_id=1, source_target_pairs={{0,1},{1,0},{2,3},{3,2},{4,5},{5,4},{6,7},{7,6},{8,9},{9,8},{10,11... | collective-permute-start | bytes 196616 | tf_op jit(solution)/shard_map/ppermute | solution.py:18
  47.8 6.8 %collective-permute-start.10 = (bf16[32,1024]{1,0:T(8,128)(2,1)S(1)}, bf16[32,1024]{1,0:T(8,128)(2,1)S(1)}, u32[]{:S(2)}, u32[]{:S(2)}) collective-permute-start(bf16[32,1024]{1,0:T(8,128)(2,1)S(1)} %add_convert_fusion.1), channel_id=1, source_target_pairs={{0,6},{1,7},{2,4},{3,5},{4,2},{5,3},{6,0},{7,1},{8,14},{9,15},{10,... | collective-permute-start | bytes 196616 | tf_op jit(solution)/shard_map/ppermute | solution.py:18
  48.3 6.4 %collective-permute-start.8 = (bf16[32,1024]{1,0:T(8,128)(2,1)S(1)}, bf16[32,1024]{1,0:T(8,128)(2,1)S(1)}, u32[]{:S(2)}, u32[]{:S(2)}) collective-permute-start(bf16[32,1024]{1,0:T(8,128)(2,1)S(1)} %add_convert_fusion.1), channel_id=1, source_target_pairs={{0,2},{1,3},{2,0},{3,1},{4,6},{5,7},{6,4},{7,5},{8,10},{9,11},{10,... | collective-permute-start | bytes 196616 | tf_op jit(solution)/shard_map/ppermute | solution.py:18
  48.3 8.4 %collective-permute-start.9 = (bf16[32,1024]{1,0:T(8,128)(2,1)S(1)}, bf16[32,1024]{1,0:T(8,128)(2,1)S(1)}, u32[]{:S(2)}, u32[]{:S(2)}) collective-permute-start(bf16[32,1024]{1,0:T(8,128)(2,1)S(1)} %add_convert_fusion.1), channel_id=1, source_target_pairs={{0,4},{1,5},{2,6},{3,7},{4,0},{5,1},{6,2},{7,3},{8,12},{9,13},{10,... | collective-permute-start | bytes 196616 | tf_op jit(solution)/shard_map/ppermute | solution.py:18
  56.7 1.3 %collective-permute-start.11 = (bf16[32,1024]{1,0:T(8,128)(2,1)S(1)}, bf16[32,1024]{1,0:T(8,128)(2,1)S(1)}, u32[]{:S(2)}, u32[]{:S(2)}) collective-permute-start(bf16[32,1024]{1,0:T(8,128)(2,1)S(1)} %add_convert_fusion.own), channel_id=1, source_target_pairs={{0,1},{1,0},{2,3},{3,2},{4,5},{5,4},{6,7},{7,6},{8,9},{9,8},{10,11... | collective-permute-start | bytes 196616 | tf_op jit(solution)/shard_map/ppermute | solution.py:18
  58.4 3.8 %collective-permute-start.12 = (bf16[64,128]{1,0:T(8,128)(2,1)S(1)}, bf16[64,128]{1,0:T(8,128)(2,1)S(1)}, u32[]{:S(2)}, u32[]{:S(2)}) collective-permute-start(bf16[64,128]{1,0:T(8,128)(2,1)S(1)} %row_terms.1.refs_0_), channel_id=1, source_target_pairs={{0,8},{8,0},{16,24},{24,16},{1,9},{9,1},{17,25},{25,17},{2,10},{10... | collective-permute-start | bytes 49160 | tf_op jit(solution)/shard_map/ppermute | solution.py:18
  59.0 3.7 %collective-permute-start.13 = (bf16[64,128]{1,0:T(8,128)(2,1)S(1)}, bf16[64,128]{1,0:T(8,128)(2,1)S(1)}, u32[]{:S(2)}, u32[]{:S(2)}) collective-permute-start(bf16[64,128]{1,0:T(8,128)(2,1)S(1)} %row_terms.1.refs_0_), channel_id=1, source_target_pairs={{0,16},{8,24},{16,0},{24,8},{1,17},{9,25},{17,1},{25,9},{2,18},{10... | collective-permute-start | bytes 49160 | tf_op jit(solution)/shard_map/ppermute | solution.py:18
  59.8 4.6 %collective-permute-start.14 = (bf16[64,128]{1,0:T(8,128)(2,1)S(1)}, bf16[64,128]{1,0:T(8,128)(2,1)S(1)}, u32[]{:S(2)}, u32[]{:S(2)}) collective-permute-start(bf16[64,128]{1,0:T(8,128)(2,1)S(1)} %row_terms.1.refs_0_), channel_id=1, source_target_pairs={{0,24},{8,16},{16,8},{24,0},{1,25},{9,17},{17,9},{25,1},{2,26},{10... | collective-permute-start | bytes 49160 | tf_op jit(solution)/shard_map/ppermute | solution.py:18
  64.8 1.3 %collective-permute-start.15 = (f32[64,64]{1,0:T(8,128)S(1)}, f32[64,64]{1,0:T(8,128)S(1)}, u32[]{:S(2)}, u32[]{:S(2)}) collective-permute-start(f32[64,64]{1,0:T(8,128)S(1)} %get-tuple-element.11), channel_id=1, source_target_pairs={{0,1},{1,0},{2,3},{3,2},{4,5},{5,4},{6,7},{7,6},{8,9},{9,8},{10,11... | collective-permute-start | bytes 49160 | tf_op jit(solution)/shard_map/ppermute | solution.py:18
  66.1 4.4 %collective-permute-start.16 = (f32[64,64]{1,0:T(8,128)S(1)}, f32[64,64]{1,0:T(8,128)S(1)}, u32[]{:S(2)}, u32[]{:S(2)}) collective-permute-start(f32[64,64]{1,0:T(8,128)S(1)} %add.50), channel_id=1, source_target_pairs={{0,2},{1,3},{2,0},{3,1},{4,6},{5,7},{6,4},{7,5},{8,10},{9,11},{10,... | collective-permute-start | bytes 49160 | tf_op jit(solution)/shard_map/ppermute | solution.py:18
  67.4 5.5 %collective-permute-start.17 = (f32[64,64]{1,0:T(8,128)S(1)}, f32[64,64]{1,0:T(8,128)S(1)}, u32[]{:S(2)}, u32[]{:S(2)}) collective-permute-start(f32[64,64]{1,0:T(8,128)S(1)} %add.50), channel_id=1, source_target_pairs={{0,4},{1,5},{2,6},{3,7},{4,0},{5,1},{6,2},{7,3},{8,12},{9,13},{10,... | collective-permute-start | bytes 49160 | tf_op jit(solution)/shard_map/ppermute | solution.py:18
  68.3 5.7 %collective-permute-start.18 = (f32[64,64]{1,0:T(8,128)S(1)}, f32[64,64]{1,0:T(8,128)S(1)}, u32[]{:S(2)}, u32[]{:S(2)}) collective-permute-start(f32[64,64]{1,0:T(8,128)S(1)} %add.50), channel_id=1, source_target_pairs={{0,6},{1,7},{2,4},{3,5},{4,2},{5,3},{6,0},{7,1},{8,14},{9,15},{10,... | collective-permute-start | bytes 49160 | tf_op jit(solution)/shard_map/ppermute | solution.py:18

commit v2 on v0

v2 whole, which is shorter than its diff:
```python
import functools

import jax
import jax.numpy as jnp
from jax import lax
from jax.experimental import pallas as pl
from jax.experimental.pallas import tpu as pltpu
from jax.sharding import PartitionSpec as P

F32 = jnp.float32
BF16 = jnp.bfloat16
VMEM = pl.BlockSpec(memory_space=pltpu.VMEM)
SMEM = pl.BlockSpec(memory_space=pltpu.SMEM)
DIRECT_LIMIT = 8


def partner(i, mask, size):
    return i ^ mask if size & (size - 1) == 0 else (i + mask) % size


def swap(x, axis, size, mask):
    return lax.ppermute(x, axis, [(i, partner(i, mask, size)) for i in range(size)])


def is_direct(size):
    return size <= DIRECT_LIMIT and size & (size - 1) == 0


def params(limit):
    return pltpu.CompilerParams(vmem_limit_bytes=limit)


def dup(u):
    return jnp.concatenate([u, u], axis=1)


def contract_kernel(*refs, n_tables, n_grp, split, slots, row_blocks, edge, rank):
    places, counts, blocks = refs[:3]
    tables, refs = refs[3 : 3 + n_tables], refs[3 + n_tables :]
    outs, refs = refs[: n_grp * split], refs[n_grp * split :]
    place, live, xbuf, fbuf, zbuf, vbuf, wbuf, meta_sem, block_sem = refs
    half = edge // 2
    lanes = 2 * rank
    tile = 8

    meta = [
        pltpu.make_async_copy(source, target, meta_sem.at[i])
        for i, (source, target) in enumerate(((places, place), (counts, live)))
    ]
    loads = [pltpu.make_async_copy(blocks.at[s], xbuf.at[s], block_sem.at[s]) for s in range(slots)]
    for copy in meta + loads:
        copy.start()

    height = tables[0].shape[0]
    total = height * n_tables
    low = lax.broadcasted_iota(jnp.int32, (height, lanes), 1) < rank
    for i in range(n_tables):
        for j in range(half):
            pair = tables[i][:, j * lanes : (j + 1) * lanes].astype(F32)
            turned = pltpu.roll(pair, rank, 1)
            for q in range(2):
                k = 2 * j + q
                at = k // tile * total * tile + i * height * tile + k % tile
                fbuf[pl.ds(at, height, stride=tile), :] = (
                    jnp.where(low, turned, pair) if q else jnp.where(low, pair, turned)
                )
    for copy in meta:
        copy.wait()
    me = lax.axis_index("dev").astype(jnp.int32) if split > 1 else 0
    core = me % split
    per_owner = 2 * row_blocks
    per_core = total // per_owner // split

    def factor_rows(p, which):
        owner = (p // row_blocks) ^ me
        row = (owner % split * per_core + owner // split) * per_owner + which * row_blocks + p % row_blocks
        parts = []
        for k in range(edge // tile):
            at = pl.multiple_of((k * total + row) * tile, tile)
            parts.append(fbuf[pl.ds(at, tile), :])
        return jnp.concatenate(parts, axis=0)

    lane = lax.broadcasted_iota(jnp.int32, (edge, lanes), 1)
    low = lane < rank
    weights = []
    for s in range(slots):
        pos = [place[m, s] for m in range(3)]
        u2 = factor_rows(pos[1], 0)
        u3 = factor_rows(pos[2], 1)
        low3 = jnp.where(low, u3, 0.0).astype(BF16)
        high3 = jnp.where(low, 0.0, u3).astype(BF16)
        none = jnp.zeros_like(low3)
        weights.append(
            jnp.concatenate(
                [
                    jnp.concatenate([low3, none], axis=1),
                    jnp.concatenate([none, low3], axis=1),
                    jnp.concatenate([high3, none], axis=1),
                    jnp.concatenate([none, high3], axis=1),
                ],
                axis=0,
            )
        )
        mine = jnp.where(s < live[0], pos[0] % row_blocks, row_blocks)
        for p in range(row_blocks // 2):
            keep = 2 * p + lane // rank == mine
            wbuf[s * edge : (s + 1) * edge, p * lanes : (p + 1) * lanes] = jnp.where(keep, u2, 0.0)
    left = wbuf[...].T.astype(BF16)

    for s in range(slots):
        loads[s].wait()
        slabs = []
        for j in range(half):
            cols = slice(j * 2 * edge, (j + 1) * 2 * edge)
            slabs.append(jnp.concatenate([xbuf[s, :half, cols], xbuf[s, half:, cols]], axis=1))
        first = jnp.dot(jnp.concatenate(slabs, axis=0), weights[s], preferred_element_type=F32)
        for j in range(half):
            for q in range(2):
                k = 2 * j + q
                at = (s * (edge // tile) + k // tile) * half * tile + k % tile
                zbuf[pl.ds(at, half, stride=tile), :] = first[
                    j * half : (j + 1) * half, q * lanes : (q + 1) * lanes
                ]

    rows = row_blocks * rank
    for a in range(0, half, 2):
        right = jnp.concatenate(
            [
                jnp.concatenate(
                    [
                        zbuf[(k * half + a + b) * tile : (k * half + a + b + 1) * tile, :]
                        for k in range(slots * edge // tile)
                    ],
                    axis=0,
                )
                for b in range(2)
            ],
            axis=1,
        ).astype(BF16)
        panel = jnp.dot(left, right, preferred_element_type=F32)
        for b in range(2):
            at = (a + b) // tile * rows * tile + (a + b) % tile
            vbuf[pl.ds(at, rows, stride=tile), :] = panel[:, b * lanes : (b + 1) * lanes]
    share = rank // (n_grp * split)
    group = lax.axis_index("grp").astype(jnp.int32)
    for i, out in enumerate(outs):
        side, m = divmod(i, n_grp)
        start = (partner(group, m, n_grp) * split + (core + side) % split) * share
        for p in range(row_blocks):
            for r in range(share):
                parts = []
                for k in range(half // tile):
                    at = pl.multiple_of((k * rows + p * rank + r + start) * tile, tile)
                    parts.append(vbuf[pl.ds(at, tile), :])
                out[p * half : (p + 1) * half, r * lanes : (r + 1) * lanes] = jnp.concatenate(
                    parts, axis=0
                ).astype(BF16)


def contract(places, counts, blocks, tables, n_grp, split, row_blocks, rank):
    slots, edge, width = blocks.shape
    half, lanes = edge // 2, 2 * rank
    out = jax.ShapeDtypeStruct((row_blocks * half, rank // (n_grp * split) * lanes), BF16)
    factor_rows = sum(table.shape[0] for table in tables)
    flops = 2 * slots * edge * width * 4 * edge + 2 * row_blocks * rank * slots * edge * edge * rank
    floats = [
        (edge * factor_rows, lanes),
        (slots * edge * half, lanes),
        (row_blocks * rank * half, lanes),
        (slots * edge, row_blocks * rank),
    ]
    held = 2 * blocks.size + sum(4 * rows * columns for rows, columns in floats)
    far = pl.BlockSpec(memory_space=pltpu.HBM)
    return pl.pallas_call(
        functools.partial(
            contract_kernel,
            n_tables=len(tables),
            n_grp=n_grp,
            split=split,
            slots=slots,
            row_blocks=row_blocks,
            edge=edge,
            rank=rank,
        ),
        in_specs=[far] * 3 + [VMEM] * len(tables),
        out_specs=[VMEM] * (n_grp * split),
        out_shape=[out] * (n_grp * split),
        scratch_shapes=[
            pltpu.SMEM(places.shape, jnp.int32),
            pltpu.SMEM(counts.shape, jnp.int32),
            pltpu.VMEM(blocks.shape, BF16),
            *(pltpu.VMEM(shape, F32) for shape in floats),
            pltpu.SemaphoreType.DMA((2,)),
            pltpu.SemaphoreType.DMA((slots,)),
        ],
        compiler_params=params(max(held + 8 * 1024 * 1024, 50 * 1024 * 1024)),
        cost_estimate=pl.CostEstimate(
            flops=flops, bytes_accessed=2 * blocks.size + 4 * row_blocks * edge * rank * rank, transcendentals=0
        ),
        name="contract",
    )(places, counts, blocks, *tables)


def project_kernel(*refs, sides, rank, row_blocks):
    olds, pieces, panel, out = refs[:sides], refs[sides:-2], refs[-2], refs[-1]
    count = len(pieces) // sides
    edge = olds[0].shape[0] // row_blocks
    half, lanes = edge // 2, 2 * rank
    totals, lefts = [], []
    for d in range(sides):
        total = pieces[d * count][...].astype(F32)
        for piece in pieces[d * count + 1 : (d + 1) * count]:
            total = total + piece[...].astype(F32)
        totals.append(total.astype(BF16))
        parts = []
        for q in range(2):
            rows = [olds[d][p * edge + q * half : p * edge + (q + 1) * half, :] for p in range(row_blocks)]
            parts.append(jnp.concatenate(rows, axis=0))
        lefts.append(jnp.concatenate(parts, axis=1))
    total = jnp.concatenate(totals, axis=0)
    panel[...] = total
    left = jnp.concatenate(lefts, axis=0).astype(F32).T.astype(BF16)
    both = jnp.dot(left, total, preferred_element_type=F32)
    low = lax.broadcasted_iota(jnp.int32, (rank, lanes), 1) < rank
    sums = []
    for r in range(total.shape[1] // lanes):
        cols = slice(r * lanes, (r + 1) * lanes)
        own = jnp.where(low, both[:rank, cols], both[rank:, cols])
        sums.append(own + pltpu.roll(own, rank, 1))
    for r in range(0, len(sums), 2):
        out[:, r // 2 * lanes : (r // 2 + 1) * lanes] = jnp.where(low, sums[r], sums[r + 1]).astype(out.dtype)


def project(olds, pieces, rank, row_blocks, kind):
    sides = len(olds)
    height, width = pieces[0].shape
    shapes = [
        jax.ShapeDtypeStruct((height * sides, width), BF16),
        jax.ShapeDtypeStruct((rank, width // 2), kind),
    ]
    return pl.pallas_call(
        functools.partial(project_kernel, sides=sides, rank=rank, row_blocks=row_blocks),
        in_specs=[VMEM] * (sides + len(pieces)),
        out_specs=[VMEM] * 2,
        out_shape=shapes,
        compiler_params=params(24 * 1024 * 1024),
        name="project",
    )(*olds, *pieces)


def rows_kernel(panel, *refs, rank):
    pieces, out = refs[:-1], refs[-1]
    lanes = 2 * rank
    total = pieces[0][...].astype(F32)
    for piece in pieces[1:]:
        total = total + piece[...].astype(F32)
    low = lax.broadcasted_iota(jnp.int32, (rank, lanes), 1) < rank
    zero = jnp.zeros((rank, lanes), F32)
    upper, lower = [], []
    for r in range(total.shape[1] // lanes):
        value = total[:, r * lanes : (r + 1) * lanes]
        turned = pltpu.roll(value, rank, 1)
        upper += [jnp.where(low, value, zero).astype(BF16), jnp.where(low, turned, zero).astype(BF16)]
        lower += [jnp.where(low, zero, turned).astype(BF16), jnp.where(low, zero, value).astype(BF16)]
    right = jnp.concatenate([jnp.concatenate(upper, axis=1), jnp.concatenate(lower, axis=1)], axis=0)
    out[...] = lax.dot_general(
        panel[...], right, (((1,), (1,)), ((), ())), preferred_element_type=F32
    ).astype(BF16)


def row_terms(panel, pieces, rank):
    return pl.pallas_call(
        functools.partial(rows_kernel, rank=rank),
        in_specs=[VMEM] * (1 + len(pieces)),
        out_specs=VMEM,
        out_shape=jax.ShapeDtypeStruct((panel.shape[0], 2 * rank), BF16),
        compiler_params=params(24 * 1024 * 1024),
        name="row_terms",
    )(panel, *pieces)


def gram_kernel(*refs, rank):
    terms, rows, gram = refs[:-2], refs[-2], refs[-1]
    height = rows.shape[0]
    if len(terms) == 1:
        total = terms[0][...]
    else:
        own = terms[0][:height, :] + terms[1][height:, :]
        total = jnp.concatenate([own, terms[0][height:, :] + terms[1][:height, :]], axis=0)
    rows[...] = total[:height, :]
    full = jnp.dot(total.T, total, precision=lax.Precision.HIGHEST, preferred_element_type=F32)
    gram[...] = full[:rank, :rank] + full[rank:, rank:]


def gram_terms(terms, rank):
    height, lanes = terms[0].shape
    shapes = [
        jax.ShapeDtypeStruct((height // len(terms), lanes), F32),
        jax.ShapeDtypeStruct((rank, rank), F32),
    ]
    return pl.pallas_call(
        functools.partial(gram_kernel, rank=rank),
        in_specs=[VMEM] * len(terms),
        out_specs=[VMEM] * 2,
        out_shape=shapes,
        compiler_params=params(24 * 1024 * 1024),
        name="gram_terms",
    )(*terms)


def finish_kernel(*refs, rows_total):
    pieces, rows, new_rows, gram = refs[:-3], refs[-3], refs[-2], refs[-1]
    total = pieces[0][...]
    for piece in pieces[1:]:
        total = total + piece[...]
    rank = total.shape[0]
    square = total.shape
    diagonal = lax.broadcasted_iota(jnp.int32, square, 0) == lax.broadcasted_iota(jnp.int32, square, 1)
    trace = jnp.sum(jnp.where(diagonal, total, 0.0), axis=1, keepdims=True)
    trace = jnp.sum(trace, axis=0, keepdims=True)
    gram[...] = total * (rank / trace)
    scale = lax.rsqrt(trace / (rows_total * rank))
    row_blocks = new_rows.shape[0]
    lanes = 2 * rank
    half = rows.shape[0] // row_blocks
    pairs = half // 2
    low = lax.broadcasted_iota(jnp.int32, (pairs, lanes), 1) < rank
    for p in range(row_blocks):
        even = rows[pl.ds(p * half, pairs, stride=2), :] * scale
        odd = rows[pl.ds(p * half + 1, pairs, stride=2), :] * scale
        lower = jnp.where(low, even, pltpu.roll(odd, rank, 1))
        upper = jnp.where(low, pltpu.roll(even, rank, 1), odd)
        for q, value in enumerate((lower, upper)):
            for i in range(pairs):
                at = (q * pairs + i) * lanes
                new_rows[p : p + 1, at : at + lanes] = value[i : i + 1, :]


def finish(pieces, rows, row_blocks, rows_total):
    rank = pieces[0].shape[0]
    shapes = [
        jax.ShapeDtypeStruct((row_blocks, rows.size // row_blocks), F32),
        jax.ShapeDtypeStruct((rank, rank), F32),
    ]
    return pl.pallas_call(
        functools.partial(finish_kernel, rows_total=rows_total),
        in_specs=[VMEM] * (len(pieces) + 1),
        out_specs=[VMEM] * 2,
        out_shape=shapes,
        compiler_params=params(24 * 1024 * 1024),
        name="finish",
    )(*pieces, rows)


def body(blocks, coords, counts, row_place, factor_one, factor_two, factor_three):
    edge = blocks.shape[1]
    rank = factor_one.shape[1] // edge
    row_blocks = factor_one.shape[0]
    n_grp, n_dev = lax.axis_size("grp"), lax.axis_size("dev")
    direct = is_direct(n_dev)
    split = 2 if direct else 1
    far = range(2, n_dev, 2)

    def sibling(x):
        return swap(x, "dev", n_dev, 1)

    def over_grp(pieces):
        return pieces[:1] + [swap(pieces[m], "grp", n_grp, m) for m in range(1, n_grp)]

    packed = jnp.concatenate([factor_two, factor_three], axis=0)
    if direct:
        tables = [packed] + [swap(packed, "dev", n_dev, m) for m in far]
        tables += [sibling(table) for table in tables]
    else:
        tables = [lax.all_gather(packed, "dev", axis=0, tiled=True)]
    hits = coords[:, :, None] == jnp.arange(row_place.shape[0])[None, None, :]
    places = jnp.sum(jnp.where(hits, row_place[None, None, :], 0), axis=2)
    old = factor_one.reshape(row_blocks * edge, rank)
    olds = [old, sibling(old)] if direct else [old]
    shares = list(contract(places, counts, blocks, tables, n_grp, split, row_blocks, rank))
    pieces = over_grp(shares[:n_grp])
    if direct:
        pieces += over_grp([sibling(share) for share in shares[n_grp:]])

    panel, proj = project(olds, pieces, rank, row_blocks, BF16 if direct else F32)
    if direct:
        projs = [proj] + [swap(proj, "dev", n_dev, m) for m in far]
    else:
        projs = [lax.psum(proj, "dev")]
    terms = row_terms(panel, projs, rank)
    rows = sum(part.astype(F32) for part in over_grp([terms] * n_grp))
    rows, gram_local = gram_terms([rows, sibling(rows)] if direct else [rows], rank)
    if direct:
        grams = [gram_local] + [swap(gram_local, "dev", n_dev, m) for m in far]
    else:
        grams = [lax.psum(gram_local, "dev")]
    return tuple(finish(grams, rows, row_blocks, row_blocks * edge * n_dev))


def solution(mesh):
    placed = (
        P(("grp", "dev"), None, None),
        P(None, ("grp", "dev")),
        P(("grp", "dev")),
        P(),
        P("dev", None),
        P("dev", None),
        P("dev", None),
    )
    return jax.shard_map(
        body, mesh=mesh, in_specs=placed, out_specs=(P("dev", None), P()), check_vma=False
    )
```

time: 237 us -> 63.1 us (0.27)
  blocking collectives: 103 us -> 0 us
  local copies, waits for them, and re-layouts: 40.5 us -> 0.81 us
  matrix products: 38.3 us -> 0 us
  starting transfers between devices: 0.04 us -> 29 us
  between operations: 16.2 us -> 1.39 us
  waiting for transfers between devices: 36.2 us -> 22.3 us
  Pallas kernels: 0 us -> 7.44 us
    psum x3 -> x0, blocking collectives: 73 us -> none  [the longest x1 31.6 us: body(): proj = lax.psum(proj_terms, 'dev').astype(jnp.bfloat16)]
    dot_general x8 -> x0, matrix products: 38.3 us -> none  [the longest x1 15.3 us: body(): jnp.einsum('bl,bam->lam', assign, contrib, precision=lax.Precision.HIGHEST)]
    reduce_scatter x1 -> x0, waiting for transfers between devices: 36.2 us -> none  [body(): share = lax.psum_scatter(panels, 'grp', scatter_dimension=1, tiled=True)]
    reshape x7 -> x1, local copies, waits for them, and re-layouts: 36.9 us -> 0.81 us  [body(): old = factor_one.reshape(row_blocks * edge, rank)]
    all_gather x2 -> x0, blocking collectives: 29.9 us -> none  [the longest x1 15.9 us: body(): lax.all_gather(factor_three, 'dev', axis=0, tiled=True)]
    ppermute x0 -> x28, starting transfers between devices: none -> 29 us  [swap(): lax.ppermute(x, axis, [(i, partner(i, mask, size)) for i in range(size)])]
    ppermute x0 -> x28, waiting for transfers between devices: none -> 22.3 us  [swap(): lax.ppermute(x, axis, [(i, partner(i, mask, size)) for i in range(size)])]
    pallas_call x0 -> x5, Pallas kernels: none -> 7.44 us  [the longest x1 5.53 us: contract(): pl.pallas_call(functools.partial(contract_kernel, n_tables=len(tables), n...]
  transfers between devices with their start and end apart: 1 -> 28, of which waited for: 1 -> 13; matrix products, arithmetic and copies ran while one was open for 0% -> 3% of each run, Pallas kernels for 0% -> 9%
where the time goes in v2:
time: 63.1 us; the launch traced here: 62.7 us
  starting transfers between devices  29 us (46%)
  waiting for transfers between devices  22.3 us (35%)
  Pallas kernels  7.44 us (12%)
  other arithmetic  1.7 us (3%)
  between operations  1.39 us (2%)
  local copies, waits for them, and re-layouts  0.81 us (1%)
    ppermute x28, starting transfers between devices, swap(): lax.ppermute(x, axis, [(i, partner(i, mask, size)) for i in range(size)])  29 us
    ppermute x28, waiting for transfers between devices, swap(): lax.ppermute(x, axis, [(i, partner(i, mask, size)) for i in range(size)])  22.3 us
    pallas_call x1, Pallas kernels, contract(): pl.pallas_call(functools.partial(contract_kernel, n_tables=len(tables), n...  5.53 us
  transfers between devices with their start and end apart: 28, of which 13 were waited for; matrix products, arithmetic and copies ran while one was open for 3% of the time, Pallas kernels for 9%

profile of v2, /device:TPU:0, one launch (start us, length us, event | category | flops | bytes accessed | tf_op | source)
XLA Modules:
  0.0 62.7 jit_solution(6140679244385999215)
XLA Ops:
  0.6 0.8 %pad_maximum_fusion.refs_3_ = bf16[4,4096]{1,0:T(4,128)(2,1)S(1)} fusion(bf16[2,4096]{1,0:T(2,128)(2,1)} %param.13, bf16[2,4096]{1,0:T(2,128)(2,1)} %param.12), kind=kLoop, calls=%fused_computation.1 | loop fusion | flops 65536 | bytes 65536 | tf_op jit(solution)/shard_map/concatenate | solution.py:370
  1.4 5.1 %collective-permute-start.3 = (bf16[4,4096]{1,0:T(4,128)(2,1)S(1)}, bf16[4,4096]{1,0:T(4,128)(2,1)S(1)}, u32[]{:S(2)}, u32[]{:S(2)}) collective-permute-start(bf16[4,4096]{1,0:T(4,128)(2,1)S(1)} %pad_maximum_fusion.refs_3_), channel_id=1, source_target_pairs={{0,6},{1,7},{2,4},{3,5},{4,2},{5,3},{6,0},{7,1},{8,14},{9,15},{10,... | collective-permute-start | bytes 98312 | tf_op jit(solution)/shard_map/ppermute | solution.py:22
  6.5 0.0 collective-permute-start.2
  6.5 0.6 %collective-permute-start.1 = (bf16[4,4096]{1,0:T(4,128)(2,1)S(1)}, bf16[4,4096]{1,0:T(4,128)(2,1)S(1)}, u32[]{:S(2)}, u32[]{:S(2)}) collective-permute-start(bf16[4,4096]{1,0:T(4,128)(2,1)S(1)} %pad_maximum_fusion.refs_3_), channel_id=1, source_target_pairs={{0,2},{1,3},{2,0},{3,1},{4,6},{5,7},{6,4},{7,5},{8,10},{9,11},{10,... | collective-permute-start | bytes 98312 | tf_op jit(solution)/shard_map/ppermute | solution.py:22
  7.2 0.0 collective-permute-start.4
  7.2 0.8 %reshape.9.refs_0_ = bf16[128,64]{1,0:T(8,128)(2,1)S(1)} reshape(bf16[2,4096]{1,0:T(2,128)(2,1)} %param.11) | data formatting | bytes 32768 | tf_op jit(solution)/shard_map/reshape | solution.py:378
  8.0 0.6 collective-permute-start
  8.6 0.1 collective-permute-start.7
  8.6 2.7 %collective-permute-done.2.refs_5_ = bf16[4,4096]{1,0:T(4,128)(2,1)S(1)} collective-permute-done((bf16[4,4096]{1,0:T(4,128)(2,1)S(1)}, bf16[4,4096]{1,0:T(4,128)(2,1)S(1)}, u32[]{:S(2)}, u32[]{:S(2)}) %collective-permute-start.2) | collective-permute-done | bytes 32800 | tf_op jit(solution)/shard_map/ppermute | solution.py:22
  11.3 0.0 collective-permute-start.6
  11.3 0.5 collective-permute-start.5
  11.9 0.9 %select_reduce_fusion.refs_0_ = s32[3,8]{1,0:T(4,128)S(1)} fusion(s32[16]{0:T(128)} %param.10, s32[3,8]{1,0:T(4,128)} %param.8), kind=kLoop, calls=%fused_computation.2 | loop fusion | flops 1128 | bytes 256 | tf_op jit(solution)/shard_map/reduce_sum | solution.py:377
  13.4 0.0 collective-permute-done.4.refs_7_
  13.4 0.0 collective-permute-done.5.refs_8_
  13.5 5.5 %contract.1 = (bf16[64,1024]{1,0:T(8,128)(2,1)S(1)}, bf16[64,1024]{1,0:T(8,128)(2,1)S(1)}, bf16[64,1024]{1,0:T(8,128)(2,1)S(1)}, bf16[64,1024]{1,0:T(8,128)(2,1)...) custom-call(s32[3,8]{1,0:T(4,128)S(1)} %select_reduce_fusion.refs_0_, ...), custom_call_target="tpu_custom_call" | custom-call | flops 1610612736 | bytes 6291456 | tf_op jit(solution)/shard_map/contract/pallas_call | solution.py:174
  19.0 1.6 %collective-permute-start.8 = (bf16[64,1024]{1,0:T(8,128)(2,1)S(1)}, bf16[64,1024]{1,0:T(8,128)(2,1)S(1)}, u32[]{:S(2)}, u32[]{:S(2)}) collective-permute-start(bf16[64,1024]{1,0:T(8,128)(2,1)S(1)} %get-tuple-element.15), channel_id=1, source_target_pairs={{0,8},{8,0},{16,24},{24,16},{1,9},{9,1},{17,25},{25,17},{2,10},{10... | collective-permute-start | bytes 393224 | tf_op jit(solution)/shard_map/ppermute | solution.py:22
  20.6 1.5 %collective-permute-start.9 = (bf16[64,1024]{1,0:T(8,128)(2,1)S(1)}, bf16[64,1024]{1,0:T(8,128)(2,1)S(1)}, u32[]{:S(2)}, u32[]{:S(2)}) collective-permute-start(bf16[64,1024]{1,0:T(8,128)(2,1)S(1)} %get-tuple-element.16), channel_id=1, source_target_pairs={{0,16},{8,24},{16,0},{24,8},{1,17},{9,25},{17,1},{25,9},{2,18},{10... | collective-permute-start | bytes 393224 | tf_op jit(solution)/shard_map/ppermute | solution.py:22
  22.1 0.5 collective-permute-start.14
  22.6 0.0 collective-permute-start.16
  22.6 1.9 %collective-permute-done.8.refs_3_ = bf16[64,1024]{1,0:T(8,128)(2,1)S(1)} collective-permute-done((bf16[64,1024]{1,0:T(8,128)(2,1)S(1)}, bf16[64,1024]{1,0:T(8,128)(2,1)S(1)}, u32[]{:S(2)}, u32[]{:S(2)}) %collective-permute-start.8) | collective-permute-done | bytes 131104 | tf_op jit(solution)/shard_map/ppermute | solution.py:22
  24.5 2.4 %collective-permute-start.10 = (bf16[64,1024]{1,0:T(8,128)(2,1)S(1)}, bf16[64,1024]{1,0:T(8,128)(2,1)S(1)}, u32[]{:S(2)}, u32[]{:S(2)}) collective-permute-start(bf16[64,1024]{1,0:T(8,128)(2,1)S(1)} %get-tuple-element.17), channel_id=1, source_target_pairs={{0,24},{8,16},{16,8},{24,0},{1,25},{9,17},{17,9},{25,1},{2,26},{10... | collective-permute-start | bytes 393224 | tf_op jit(solution)/shard_map/ppermute | solution.py:22
  26.9 0.6 collective-permute-start.13
  27.5 0.5 collective-permute-start.15
  28.0 2.4 %collective-permute-start.17 = (bf16[64,1024]{1,0:T(8,128)(2,1)S(1)}, bf16[64,1024]{1,0:T(8,128)(2,1)S(1)}, u32[]{:S(2)}, u32[]{:S(2)}) collective-permute-start(bf16[64,1024]{1,0:T(8,128)(2,1)S(1)} %collective-permute-done.16), channel_id=1, source_target_pairs={{0,24},{8,16},{16,8},{24,0},{1,25},{9,17},{17,9},{25,1},{2,26},{10... | collective-permute-start | bytes 393224 | tf_op jit(solution)/shard_map/ppermute | solution.py:22
  30.5 0.2 collective-permute-done.10.refs_5_
  30.7 2.8 %collective-permute-done.13.refs_7_ = bf16[64,1024]{1,0:T(8,128)(2,1)S(1)} collective-permute-done((bf16[64,1024]{1,0:T(8,128)(2,1)S(1)}, bf16[64,1024]{1,0:T(8,128)(2,1)S(1)}, u32[]{:S(2)}, u32[]{:S(2)}) %collective-permute-start.13) | collective-permute-done | bytes 131104 | tf_op jit(solution)/shard_map/ppermute | solution.py:22
  33.6 2.5 %collective-permute-done.15.refs_8_ = bf16[64,1024]{1,0:T(8,128)(2,1)S(1)} collective-permute-done((bf16[64,1024]{1,0:T(8,128)(2,1)S(1)}, bf16[64,1024]{1,0:T(8,128)(2,1)S(1)}, u32[]{:S(2)}, u32[]{:S(2)}) %collective-permute-start.15) | collective-permute-done | bytes 131104 | tf_op jit(solution)/shard_map/ppermute | solution.py:22
  36.1 0.5 project.1
  36.6 1.6 %collective-permute-start.20 = (bf16[64,512]{1,0:T(8,128)(2,1)S(1)}, bf16[64,512]{1,0:T(8,128)(2,1)S(1)}, u32[]{:S(2)}, u32[]{:S(2)}) collective-permute-start(bf16[64,512]{1,0:T(8,128)(2,1)S(1)} %get-tuple-element.23.refs_0_), channel_id=1, source_target_pairs={{0,6},{1,7},{2,4},{3,5},{4,2},{5,3},{6,0},{7,1},{8,14},{9,15},{10,... | collective-permute-start | bytes 196616 | tf_op jit(solution)/shard_map/ppermute | solution.py:22
  38.2 0.7 %collective-permute-start.19 = (bf16[64,512]{1,0:T(8,128)(2,1)S(1)}, bf16[64,512]{1,0:T(8,128)(2,1)S(1)}, u32[]{:S(2)}, u32[]{:S(2)}) collective-permute-start(bf16[64,512]{1,0:T(8,128)(2,1)S(1)} %get-tuple-element.23.refs_0_), channel_id=1, source_target_pairs={{0,4},{1,5},{2,6},{3,7},{4,0},{5,1},{6,2},{7,3},{8,12},{9,13},{10,... | collective-permute-start | bytes 196616 | tf_op jit(solution)/shard_map/ppermute | solution.py:22
  38.9 2.1 %collective-permute-start.18 = (bf16[64,512]{1,0:T(8,128)(2,1)S(1)}, bf16[64,512]{1,0:T(8,128)(2,1)S(1)}, u32[]{:S(2)}, u32[]{:S(2)}) collective-permute-start(bf16[64,512]{1,0:T(8,128)(2,1)S(1)} %get-tuple-element.23.refs_0_), channel_id=1, source_target_pairs={{0,2},{1,3},{2,0},{3,1},{4,6},{5,7},{6,4},{7,5},{8,10},{9,11},{10,... | collective-permute-start | bytes 196616 | tf_op jit(solution)/shard_map/ppermute | solution.py:22
  41.0 2.3 %collective-permute-done.20.refs_3_ = bf16[64,512]{1,0:T(8,128)(2,1)S(1)} collective-permute-done((bf16[64,512]{1,0:T(8,128)(2,1)S(1)}, bf16[64,512]{1,0:T(8,128)(2,1)S(1)}, u32[]{:S(2)}, u32[]{:S(2)}) %collective-permute-start.20) | collective-permute-done | bytes 65568 | tf_op jit(solution)/shard_map/ppermute | solution.py:22
  43.3 1.9 %collective-permute-done.19.refs_2_ = bf16[64,512]{1,0:T(8,128)(2,1)S(1)} collective-permute-done((bf16[64,512]{1,0:T(8,128)(2,1)S(1)}, bf16[64,512]{1,0:T(8,128)(2,1)S(1)}, u32[]{:S(2)}, u32[]{:S(2)}) %collective-permute-start.19) | collective-permute-done | bytes 65568 | tf_op jit(solution)/shard_map/ppermute | solution.py:22
  45.3 0.3 row_terms.1
  45.6 1.8 %collective-permute-start.23 = (bf16[128,128]{1,0:T(8,128)(2,1)S(1)}, bf16[128,128]{1,0:T(8,128)(2,1)S(1)}, u32[]{:S(2)}, u32[]{:S(2)}) collective-permute-start(bf16[128,128]{1,0:T(8,128)(2,1)S(1)} %row_terms.1), channel_id=1, source_target_pairs={{0,24},{8,16},{16,8},{24,0},{1,25},{9,17},{17,9},{25,1},{2,26},{10... | collective-permute-start | bytes 98312 | tf_op jit(solution)/shard_map/ppermute | solution.py:22
  47.4 1.6 %collective-permute-start.22 = (bf16[128,128]{1,0:T(8,128)(2,1)S(1)}, bf16[128,128]{1,0:T(8,128)(2,1)S(1)}, u32[]{:S(2)}, u32[]{:S(2)}) collective-permute-start(bf16[128,128]{1,0:T(8,128)(2,1)S(1)} %row_terms.1), channel_id=1, source_target_pairs={{0,16},{8,24},{16,0},{24,8},{1,17},{9,25},{17,1},{25,9},{2,18},{10... | collective-permute-start | bytes 98312 | tf_op jit(solution)/shard_map/ppermute | solution.py:22
  49.0 0.2 collective-permute-start.21
  49.2 1.3 %collective-permute-done.23 = bf16[128,128]{1,0:T(8,128)(2,1)S(1)} collective-permute-done((bf16[128,128]{1,0:T(8,128)(2,1)S(1)}, bf16[128,128]{1,0:T(8,128)(2,1)S(1)}, u32[]{:S(2)}, u32[]{:S(2)}) %collective-permute-start.23) | collective-permute-done | bytes 32800 | tf_op jit(solution)/shard_map/ppermute | solution.py:22
  50.5 0.8 %collective-permute-done.22 = bf16[128,128]{1,0:T(8,128)(2,1)S(1)} collective-permute-done((bf16[128,128]{1,0:T(8,128)(2,1)S(1)}, bf16[128,128]{1,0:T(8,128)(2,1)S(1)}, u32[]{:S(2)}, u32[]{:S(2)}) %collective-permute-start.22) | collective-permute-done | bytes 32800 | tf_op jit(solution)/shard_map/ppermute | solution.py:22
  51.3 1.6 %collective-permute-done.21 = bf16[128,128]{1,0:T(8,128)(2,1)S(1)} collective-permute-done((bf16[128,128]{1,0:T(8,128)(2,1)S(1)}, bf16[128,128]{1,0:T(8,128)(2,1)S(1)}, u32[]{:S(2)}, u32[]{:S(2)}) %collective-permute-start.21) | collective-permute-done | bytes 32800 | tf_op jit(solution)/shard_map/ppermute | solution.py:22
  52.9 0.1 collective-permute-start.24
  53.0 1.2 %collective-permute-done.24.refs_1_ = f32[128,128]{1,0:T(8,128)S(1)} collective-permute-done((f32[128,128]{1,0:T(8,128)S(1)}, f32[128,128]{1,0:T(8,128)S(1)}, u32[]{:S(2)}, u32[]{:S(2)}) %collective-permute-start.24) | collective-permute-done | bytes 65568 | tf_op jit(solution)/shard_map/ppermute | solution.py:22
  54.3 0.3 gram_terms.1
  54.6 2.5 %collective-permute-start.27 = (f32[64,64]{1,0:T(8,128)S(1)}, f32[64,64]{1,0:T(8,128)S(1)}, u32[]{:S(2)}, u32[]{:S(2)}) collective-permute-start(f32[64,64]{1,0:T(8,128)S(1)} %get-tuple-element.24.refs_0_), channel_id=1, source_target_pairs={{0,6},{1,7},{2,4},{3,5},{4,2},{5,3},{6,0},{7,1},{8,14},{9,15},{10,... | collective-permute-start | bytes 49160 | tf_op jit(solution)/shard_map/ppermute | solution.py:22
  57.1 2.0 %collective-permute-start.25 = (f32[64,64]{1,0:T(8,128)S(1)}, f32[64,64]{1,0:T(8,128)S(1)}, u32[]{:S(2)}, u32[]{:S(2)}) collective-permute-start(f32[64,64]{1,0:T(8,128)S(1)} %get-tuple-element.24.refs_0_), channel_id=1, source_target_pairs={{0,2},{1,3},{2,0},{3,1},{4,6},{5,7},{6,4},{7,5},{8,10},{9,11},{10,... | collective-permute-start | bytes 49160 | tf_op jit(solution)/shard_map/ppermute | solution.py:22
  59.1 1.3 %collective-permute-done.27.refs_3_ = f32[64,64]{1,0:T(8,128)S(1)} collective-permute-done((f32[64,64]{1,0:T(8,128)S(1)}, f32[64,64]{1,0:T(8,128)S(1)}, u32[]{:S(2)}, u32[]{:S(2)}) %collective-permute-start.27) | collective-permute-done | bytes 16416 | tf_op jit(solution)/shard_map/ppermute | solution.py:22
  60.4 1.5 %collective-permute-done.26.refs_2_ = f32[64,64]{1,0:T(8,128)S(1)} collective-permute-done((f32[64,64]{1,0:T(8,128)S(1)}, f32[64,64]{1,0:T(8,128)S(1)}, u32[]{:S(2)}, u32[]{:S(2)}) %collective-permute-start.26) | collective-permute-done | bytes 16416 | tf_op jit(solution)/shard_map/ppermute | solution.py:22
  61.9 0.8 %finish.1 = (f32[2,4096]{1,0:T(2,128)}, f32[64,64]{1,0:T(8,128)}) custom-call(f32[64,64]{1,0:T(8,128)S(1)} %get-tuple-element.24.refs_0_, f32[64,64]{1,0:T(8,128)S(1)} %collective-permute-done.25.refs_1_, f32[64,64]{1,0:T(8,128)S(1)} %collective-permute-done.26.refs_2_, f32[64,64]{1,0:T(8,128)S(1)} %collective-permute-done.27.refs_3_, ...), custom_call_target="tpu_custom_call" | custom-call | tf_op jit(solution)/shard_map/finish/pallas_call | solution.py:345
  (17 shorter events, 0.1 us)
Async XLA Ops:
  1.4 7.1 %collective-permute-start.3 = (bf16[4,4096]{1,0:T(4,128)(2,1)S(1)}, bf16[4,4096]{1,0:T(4,128)(2,1)S(1)}, u32[]{:S(2)}, u32[]{:S(2)}) collective-permute-start(bf16[4,4096]{1,0:T(4,128)(2,1)S(1)} %pad_maximum_fusion.refs_3_), channel_id=1, source_target_pairs={{0,6},{1,7},{2,4},{3,5},{4,2},{5,3},{6,0},{7,1},{8,14},{9,15},{10,... | collective-permute-start | bytes 98312 | tf_op jit(solution)/shard_map/ppermute | solution.py:22
  6.5 4.8 %collective-permute-start.2 = (bf16[4,4096]{1,0:T(4,128)(2,1)S(1)}, bf16[4,4096]{1,0:T(4,128)(2,1)S(1)}, u32[]{:S(2)}, u32[]{:S(2)}) collective-permute-start(bf16[4,4096]{1,0:T(4,128)(2,1)S(1)} %pad_maximum_fusion.refs_3_), channel_id=1, source_target_pairs={{0,4},{1,5},{2,6},{3,7},{4,0},{5,1},{6,2},{7,3},{8,12},{9,13},{10,... | collective-permute-start | bytes 98312 | tf_op jit(solution)/shard_map/ppermute | solution.py:22
  6.5 4.8 %collective-permute-start.1 = (bf16[4,4096]{1,0:T(4,128)(2,1)S(1)}, bf16[4,4096]{1,0:T(4,128)(2,1)S(1)}, u32[]{:S(2)}, u32[]{:S(2)}) collective-permute-start(bf16[4,4096]{1,0:T(4,128)(2,1)S(1)} %pad_maximum_fusion.refs_3_), channel_id=1, source_target_pairs={{0,2},{1,3},{2,0},{3,1},{4,6},{5,7},{6,4},{7,5},{8,10},{9,11},{10,... | collective-permute-start | bytes 98312 | tf_op jit(solution)/shard_map/ppermute | solution.py:22
  7.2 6.3 %collective-permute-start.4 = (bf16[4,4096]{1,0:T(4,128)(2,1)S(1)}, bf16[4,4096]{1,0:T(4,128)(2,1)S(1)}, u32[]{:S(2)}, u32[]{:S(2)}) collective-permute-start(bf16[4,4096]{1,0:T(4,128)(2,1)S(1)} %pad_maximum_fusion.refs_3_), channel_id=1, source_target_pairs={{0,1},{1,0},{2,3},{3,2},{4,5},{5,4},{6,7},{7,6},{8,9},{9,8},{10,11... | collective-permute-start | bytes 98312 | tf_op jit(solution)/shard_map/ppermute | solution.py:22
  8.0 14.6 %collective-permute-start = (bf16[128,64]{1,0:T(8,128)(2,1)S(1)}, bf16[128,64]{1,0:T(8,128)(2,1)S(1)}, u32[]{:S(2)}, u32[]{:S(2)}) collective-permute-start(bf16[128,64]{1,0:T(8,128)(2,1)S(1)} %reshape.9.refs_0_), channel_id=1, source_target_pairs={{0,1},{1,0},{2,3},{3,2},{4,5},{5,4},{6,7},{7,6},{8,9},{9,8},{10,11... | collective-permute-start | bytes 49160 | tf_op jit(solution)/shard_map/ppermute | solution.py:22
  8.6 4.9 %collective-permute-start.7 = (bf16[4,4096]{1,0:T(4,128)(2,1)S(1)}, bf16[4,4096]{1,0:T(4,128)(2,1)S(1)}, u32[]{:S(2)}, u32[]{:S(2)}) collective-permute-start(bf16[4,4096]{1,0:T(4,128)(2,1)S(1)} %collective-permute-done.3.refs_6_), channel_id=1, source_target_pairs={{0,1},{1,0},{2,3},{3,2},{4,5},{5,4},{6,7},{7,6},{8,9},{9,8},{10,11... | collective-permute-start | bytes 98312 | tf_op jit(solution)/shard_map/ppermute | solution.py:22
  11.3 2.1 %collective-permute-start.6 = (bf16[4,4096]{1,0:T(4,128)(2,1)S(1)}, bf16[4,4096]{1,0:T(4,128)(2,1)S(1)}, u32[]{:S(2)}, u32[]{:S(2)}) collective-permute-start(bf16[4,4096]{1,0:T(4,128)(2,1)S(1)} %collective-permute-done.2.refs_5_), channel_id=1, source_target_pairs={{0,1},{1,0},{2,3},{3,2},{4,5},{5,4},{6,7},{7,6},{8,9},{9,8},{10,11... | collective-permute-start | bytes 98312 | tf_op jit(solution)/shard_map/ppermute | solution.py:22
  11.3 2.1 %collective-permute-start.5 = (bf16[4,4096]{1,0:T(4,128)(2,1)S(1)}, bf16[4,4096]{1,0:T(4,128)(2,1)S(1)}, u32[]{:S(2)}, u32[]{:S(2)}) collective-permute-start(bf16[4,4096]{1,0:T(4,128)(2,1)S(1)} %collective-permute-done.1.refs_4_), channel_id=1, source_target_pairs={{0,1},{1,0},{2,3},{3,2},{4,5},{5,4},{6,7},{7,6},{8,9},{9,8},{10,11... | collective-permute-start | bytes 98312 | tf_op jit(solution)/shard_map/ppermute | solution.py:22
  19.0 5.5 %collective-permute-start.8 = (bf16[64,1024]{1,0:T(8,128)(2,1)S(1)}, bf16[64,1024]{1,0:T(8,128)(2,1)S(1)}, u32[]{:S(2)}, u32[]{:S(2)}) collective-permute-start(bf16[64,1024]{1,0:T(8,128)(2,1)S(1)} %get-tuple-element.15), channel_id=1, source_target_pairs={{0,8},{8,0},{16,24},{24,16},{1,9},{9,1},{17,25},{25,17},{2,10},{10... | collective-permute-start | bytes 393224 | tf_op jit(solution)/shard_map/ppermute | solution.py:22
  20.6 6.4 %collective-permute-start.9 = (bf16[64,1024]{1,0:T(8,128)(2,1)S(1)}, bf16[64,1024]{1,0:T(8,128)(2,1)S(1)}, u32[]{:S(2)}, u32[]{:S(2)}) collective-permute-start(bf16[64,1024]{1,0:T(8,128)(2,1)S(1)} %get-tuple-element.16), channel_id=1, source_target_pairs={{0,16},{8,24},{16,0},{24,8},{1,17},{9,25},{17,1},{25,9},{2,18},{10... | collective-permute-start | bytes 393224 | tf_op jit(solution)/shard_map/ppermute | solution.py:22
  22.1 4.9 %collective-permute-start.12 = (bf16[64,1024]{1,0:T(8,128)(2,1)S(1)}, bf16[64,1024]{1,0:T(8,128)(2,1)S(1)}, u32[]{:S(2)}, u32[]{:S(2)}) collective-permute-start(bf16[64,1024]{1,0:T(8,128)(2,1)S(1)} %get-tuple-element.19), channel_id=1, source_target_pairs={{0,1},{1,0},{2,3},{3,2},{4,5},{5,4},{6,7},{7,6},{8,9},{9,8},{10,11... | collective-permute-start | bytes 393224 | tf_op jit(solution)/shard_map/ppermute | solution.py:22
  22.1 5.5 %collective-permute-start.14 = (bf16[64,1024]{1,0:T(8,128)(2,1)S(1)}, bf16[64,1024]{1,0:T(8,128)(2,1)S(1)}, u32[]{:S(2)}, u32[]{:S(2)}) collective-permute-start(bf16[64,1024]{1,0:T(8,128)(2,1)S(1)} %get-tuple-element.20), channel_id=1, source_target_pairs={{0,1},{1,0},{2,3},{3,2},{4,5},{5,4},{6,7},{7,6},{8,9},{9,8},{10,11... | collective-permute-start | bytes 393224 | tf_op jit(solution)/shard_map/ppermute | solution.py:22
  22.6 5.5 %collective-permute-start.16 = (bf16[64,1024]{1,0:T(8,128)(2,1)S(1)}, bf16[64,1024]{1,0:T(8,128)(2,1)S(1)}, u32[]{:S(2)}, u32[]{:S(2)}) collective-permute-start(bf16[64,1024]{1,0:T(8,128)(2,1)S(1)} %get-tuple-element.21), channel_id=1, source_target_pairs={{0,1},{1,0},{2,3},{3,2},{4,5},{5,4},{6,7},{7,6},{8,9},{9,8},{10,11... | collective-permute-start | bytes 393224 | tf_op jit(solution)/shard_map/ppermute | solution.py:22
  24.5 6.2 %collective-permute-start.10 = (bf16[64,1024]{1,0:T(8,128)(2,1)S(1)}, bf16[64,1024]{1,0:T(8,128)(2,1)S(1)}, u32[]{:S(2)}, u32[]{:S(2)}) collective-permute-start(bf16[64,1024]{1,0:T(8,128)(2,1)S(1)} %get-tuple-element.17), channel_id=1, source_target_pairs={{0,24},{8,16},{16,8},{24,0},{1,25},{9,17},{17,9},{25,1},{2,26},{10... | collective-permute-start | bytes 393224 | tf_op jit(solution)/shard_map/ppermute | solution.py:22
  26.9 3.8 %collective-permute-start.11 = (bf16[64,1024]{1,0:T(8,128)(2,1)S(1)}, bf16[64,1024]{1,0:T(8,128)(2,1)S(1)}, u32[]{:S(2)}, u32[]{:S(2)}) collective-permute-start(bf16[64,1024]{1,0:T(8,128)(2,1)S(1)} %get-tuple-element.18), channel_id=1, source_target_pairs={{0,1},{1,0},{2,3},{3,2},{4,5},{5,4},{6,7},{7,6},{8,9},{9,8},{10,11... | collective-permute-start | bytes 393224 | tf_op jit(solution)/shard_map/ppermute | solution.py:22
  26.9 6.6 %collective-permute-start.13 = (bf16[64,1024]{1,0:T(8,128)(2,1)S(1)}, bf16[64,1024]{1,0:T(8,128)(2,1)S(1)}, u32[]{:S(2)}, u32[]{:S(2)}) collective-permute-start(bf16[64,1024]{1,0:T(8,128)(2,1)S(1)} %collective-permute-done.12), channel_id=1, source_target_pairs={{0,8},{8,0},{16,24},{24,16},{1,9},{9,1},{17,25},{25,17},{2,10},{10... | collective-permute-start | bytes 393224 | tf_op jit(solution)/shard_map/ppermute | solution.py:22
  27.5 8.6 %collective-permute-start.15 = (bf16[64,1024]{1,0:T(8,128)(2,1)S(1)}, bf16[64,1024]{1,0:T(8,128)(2,1)S(1)}, u32[]{:S(2)}, u32[]{:S(2)}) collective-permute-start(bf16[64,1024]{1,0:T(8,128)(2,1)S(1)} %collective-permute-done.14), channel_id=1, source_target_pairs={{0,16},{8,24},{16,0},{24,8},{1,17},{9,25},{17,1},{25,9},{2,18},{10... | collective-permute-start | bytes 393224 | tf_op jit(solution)/shard_map/ppermute | solution.py:22
  28.0 8.1 %collective-permute-start.17 = (bf16[64,1024]{1,0:T(8,128)(2,1)S(1)}, bf16[64,1024]{1,0:T(8,128)(2,1)S(1)}, u32[]{:S(2)}, u32[]{:S(2)}) collective-permute-start(bf16[64,1024]{1,0:T(8,128)(2,1)S(1)} %collective-permute-done.16), channel_id=1, source_target_pairs={{0,24},{8,16},{16,8},{24,0},{1,25},{9,17},{17,9},{25,1},{2,26},{10... | collective-permute-start | bytes 393224 | tf_op jit(solution)/shard_map/ppermute | solution.py:22
  36.6 6.8 %collective-permute-start.20 = (bf16[64,512]{1,0:T(8,128)(2,1)S(1)}, bf16[64,512]{1,0:T(8,128)(2,1)S(1)}, u32[]{:S(2)}, u32[]{:S(2)}) collective-permute-start(bf16[64,512]{1,0:T(8,128)(2,1)S(1)} %get-tuple-element.23.refs_0_), channel_id=1, source_target_pairs={{0,6},{1,7},{2,4},{3,5},{4,2},{5,3},{6,0},{7,1},{8,14},{9,15},{10,... | collective-permute-start | bytes 196616 | tf_op jit(solution)/shard_map/ppermute | solution.py:22
  38.2 7.1 %collective-permute-start.19 = (bf16[64,512]{1,0:T(8,128)(2,1)S(1)}, bf16[64,512]{1,0:T(8,128)(2,1)S(1)}, u32[]{:S(2)}, u32[]{:S(2)}) collective-permute-start(bf16[64,512]{1,0:T(8,128)(2,1)S(1)} %get-tuple-element.23.refs_0_), channel_id=1, source_target_pairs={{0,4},{1,5},{2,6},{3,7},{4,0},{5,1},{6,2},{7,3},{8,12},{9,13},{10,... | collective-permute-start | bytes 196616 | tf_op jit(solution)/shard_map/ppermute | solution.py:22
  38.9 6.4 %collective-permute-start.18 = (bf16[64,512]{1,0:T(8,128)(2,1)S(1)}, bf16[64,512]{1,0:T(8,128)(2,1)S(1)}, u32[]{:S(2)}, u32[]{:S(2)}) collective-permute-start(bf16[64,512]{1,0:T(8,128)(2,1)S(1)} %get-tuple-element.23.refs_0_), channel_id=1, source_target_pairs={{0,2},{1,3},{2,0},{3,1},{4,6},{5,7},{6,4},{7,5},{8,10},{9,11},{10,... | collective-permute-start | bytes 196616 | tf_op jit(solution)/shard_map/ppermute | solution.py:22
  45.6 4.9 %collective-permute-start.23 = (bf16[128,128]{1,0:T(8,128)(2,1)S(1)}, bf16[128,128]{1,0:T(8,128)(2,1)S(1)}, u32[]{:S(2)}, u32[]{:S(2)}) collective-permute-start(bf16[128,128]{1,0:T(8,128)(2,1)S(1)} %row_terms.1), channel_id=1, source_target_pairs={{0,24},{8,16},{16,8},{24,0},{1,25},{9,17},{17,9},{25,1},{2,26},{10... | collective-permute-start | bytes 98312 | tf_op jit(solution)/shard_map/ppermute | solution.py:22
  47.4 3.9 %collective-permute-start.22 = (bf16[128,128]{1,0:T(8,128)(2,1)S(1)}, bf16[128,128]{1,0:T(8,128)(2,1)S(1)}, u32[]{:S(2)}, u32[]{:S(2)}) collective-permute-start(bf16[128,128]{1,0:T(8,128)(2,1)S(1)} %row_terms.1), channel_id=1, source_target_pairs={{0,16},{8,24},{16,0},{24,8},{1,17},{9,25},{17,1},{25,9},{2,18},{10... | collective-permute-start | bytes 98312 | tf_op jit(solution)/shard_map/ppermute | solution.py:22
  49.0 3.9 %collective-permute-start.21 = (bf16[128,128]{1,0:T(8,128)(2,1)S(1)}, bf16[128,128]{1,0:T(8,128)(2,1)S(1)}, u32[]{:S(2)}, u32[]{:S(2)}) collective-permute-start(bf16[128,128]{1,0:T(8,128)(2,1)S(1)} %row_terms.1), channel_id=1, source_target_pairs={{0,8},{8,0},{16,24},{24,16},{1,9},{9,1},{17,25},{25,17},{2,10},{10... | collective-permute-start | bytes 98312 | tf_op jit(solution)/shard_map/ppermute | solution.py:22
  52.9 1.3 %collective-permute-start.24 = (f32[128,128]{1,0:T(8,128)S(1)}, f32[128,128]{1,0:T(8,128)S(1)}, u32[]{:S(2)}, u32[]{:S(2)}) collective-permute-start(f32[128,128]{1,0:T(8,128)S(1)} %convert_add_fusion.refs_0_), channel_id=1, source_target_pairs={{0,1},{1,0},{2,3},{3,2},{4,5},{5,4},{6,7},{7,6},{8,9},{9,8},{10,11... | collective-permute-start | bytes 196616 | tf_op jit(solution)/shard_map/ppermute | solution.py:22
  54.6 5.8 %collective-permute-start.27 = (f32[64,64]{1,0:T(8,128)S(1)}, f32[64,64]{1,0:T(8,128)S(1)}, u32[]{:S(2)}, u32[]{:S(2)}) collective-permute-start(f32[64,64]{1,0:T(8,128)S(1)} %get-tuple-element.24.refs_0_), channel_id=1, source_target_pairs={{0,6},{1,7},{2,4},{3,5},{4,2},{5,3},{6,0},{7,1},{8,14},{9,15},{10,... | collective-permute-start | bytes 49160 | tf_op jit(solution)/shard_map/ppermute | solution.py:22
  57.0 4.8 %collective-permute-start.26 = (f32[64,64]{1,0:T(8,128)S(1)}, f32[64,64]{1,0:T(8,128)S(1)}, u32[]{:S(2)}, u32[]{:S(2)}) collective-permute-start(f32[64,64]{1,0:T(8,128)S(1)} %get-tuple-element.24.refs_0_), channel_id=1, source_target_pairs={{0,4},{1,5},{2,6},{3,7},{4,0},{5,1},{6,2},{7,3},{8,12},{9,13},{10,... | collective-permute-start | bytes 49160 | tf_op jit(solution)/shard_map/ppermute | solution.py:22
  57.1 4.8 %collective-permute-start.25 = (f32[64,64]{1,0:T(8,128)S(1)}, f32[64,64]{1,0:T(8,128)S(1)}, u32[]{:S(2)}, u32[]{:S(2)}) collective-permute-start(f32[64,64]{1,0:T(8,128)S(1)} %get-tuple-element.24.refs_0_), channel_id=1, source_target_pairs={{0,2},{1,3},{2,0},{3,1},{4,6},{5,7},{6,4},{7,5},{8,10},{9,11},{10,... | collective-permute-start | bytes 49160 | tf_op jit(solution)/shard_map/ppermute | solution.py:22

commit v3 on v2

--- a/solution.py
+++ b/solution.py
@@ -34,10 +34,10 @@
     return jnp.concatenate([u, u], axis=1)
 
 
-def contract_kernel(*refs, n_tables, n_grp, split, slots, row_blocks, edge, rank):
+def contract_kernel(*refs, n_tables, n_grp, split, n_outs, slots, row_blocks, edge, rank):
     places, counts, blocks = refs[:3]
     tables, refs = refs[3 : 3 + n_tables], refs[3 + n_tables :]
-    outs, refs = refs[: n_grp * split], refs[n_grp * split :]
+    outs, refs = refs[:n_outs], refs[n_outs:]
     place, live, xbuf, fbuf, zbuf, vbuf, wbuf, meta_sem, block_sem = refs
     half = edge // 2
     lanes = 2 * rank
@@ -73,7 +73,8 @@
 
     def factor_rows(p, which):
         owner = (p // row_blocks) ^ me
-        row = (owner % split * per_core + owner // split) * per_owner + which * row_blocks + p % row_blocks
+        turn = (per_core - owner // split) % per_core if split > 1 else owner
+        row = (owner % split * per_core + turn) * per_owner + which * row_blocks + p % row_blocks
         parts = []
         for k in range(edge // tile):
             at = pl.multiple_of((k * total + row) * tile, tile)
@@ -143,24 +144,27 @@
             vbuf[pl.ds(at, rows, stride=tile), :] = panel[:, b * lanes : (b + 1) * lanes]
     share = rank // (n_grp * split)
     group = lax.axis_index("grp").astype(jnp.int32)
-    for i, out in enumerate(outs):
-        side, m = divmod(i, n_grp)
-        start = (partner(group, m, n_grp) * split + (core + side) % split) * share
-        for p in range(row_blocks):
-            for r in range(share):
-                parts = []
-                for k in range(half // tile):
-                    at = pl.multiple_of((k * rows + p * rank + r + start) * tile, tile)
-                    parts.append(vbuf[pl.ds(at, tile), :])
-                out[p * half : (p + 1) * half, r * lanes : (r + 1) * lanes] = jnp.concatenate(
-                    parts, axis=0
-                ).astype(BF16)
+    for out, pieces in zip(outs, reduce_layout(n_grp, split, core)):
+        for n, (m, h) in enumerate(pieces):
+            start = (partner(group, m, n_grp) * split + h) * share
+            for p in range(row_blocks):
+                for r in range(share):
+                    parts = []
+                    for k in range(half // tile):
+                        at = pl.multiple_of((k * rows + p * rank + r + start) * tile, tile)
+                        parts.append(vbuf[pl.ds(at, tile), :])
+                    cols = slice((n * share + r) * lanes, (n * share + r + 1) * lanes)
+                    out[p * half : (p + 1) * half, cols] = jnp.concatenate(parts, axis=0).astype(BF16)
 
 
 def contract(places, counts, blocks, tables, n_grp, split, row_blocks, rank):
     slots, edge, width = blocks.shape
     half, lanes = edge // 2, 2 * rank
-    out = jax.ShapeDtypeStruct((row_blocks * half, rank // (n_grp * split) * lanes), BF16)
+    part = rank // (n_grp * split) * lanes
+    shapes = [
+        jax.ShapeDtypeStruct((row_blocks * half, part * len(pieces)), BF16)
+        for pieces in reduce_layout(n_grp, split, 0)
+    ]
     factor_rows = sum(table.shape[0] for table in tables)
     flops = 2 * slots * edge * width * 4 * edge + 2 * row_blocks * rank * slots * edge * edge * rank
     floats = [
@@ -177,14 +181,15 @@
             n_tables=len(tables),
             n_grp=n_grp,
             split=split,
+            n_outs=len(shapes),
             slots=slots,
             row_blocks=row_blocks,
             edge=edge,
             rank=rank,
         ),
         in_specs=[far] * 3 + [VMEM] * len(tables),
-        out_specs=[VMEM] * (n_grp * split),
-        out_shape=[out] * (n_grp * split),
+        out_specs=[VMEM] * len(shapes),
+        out_shape=shapes,
         scratch_shapes=[
             pltpu.SMEM(places.shape, jnp.int32),
             pltpu.SMEM(counts.shape, jnp.int32),
@@ -201,29 +206,25 @@
     )(places, counts, blocks, *tables)
 
 
-def project_kernel(*refs, sides, rank, row_blocks):
+def project_kernel(*refs, sides, rank):
     olds, pieces, panel, out = refs[:sides], refs[sides:-2], refs[-2], refs[-1]
     count = len(pieces) // sides
-    edge = olds[0].shape[0] // row_blocks
-    half, lanes = edge // 2, 2 * rank
+    width = panel.shape[1]
+    lanes = 2 * rank
     totals, lefts = [], []
     for d in range(sides):
-        total = pieces[d * count][...].astype(F32)
+        total = pieces[d * count][:, :width].astype(F32)
         for piece in pieces[d * count + 1 : (d + 1) * count]:
-            total = total + piece[...].astype(F32)
+            total = total + piece[:, :width].astype(F32)
         totals.append(total.astype(BF16))
-        parts = []
-        for q in range(2):
-            rows = [olds[d][p * edge + q * half : p * edge + (q + 1) * half, :] for p in range(row_blocks)]
-            parts.append(jnp.concatenate(rows, axis=0))
-        lefts.append(jnp.concatenate(parts, axis=1))
+        lefts.append(olds[d][:, olds[d].shape[1] - lanes :])
     total = jnp.concatenate(totals, axis=0)
     panel[...] = total
     left = jnp.concatenate(lefts, axis=0).astype(F32).T.astype(BF16)
     both = jnp.dot(left, total, preferred_element_type=F32)
     low = lax.broadcasted_iota(jnp.int32, (rank, lanes), 1) < rank
     sums = []
-    for r in range(total.shape[1] // lanes):
+    for r in range(width // lanes):
         cols = slice(r * lanes, (r + 1) * lanes)
         own = jnp.where(low, both[:rank, cols], both[rank:, cols])
         sums.append(own + pltpu.roll(own, rank, 1))
@@ -231,7 +232,7 @@
         out[:, r // 2 * lanes : (r // 2 + 1) * lanes] = jnp.where(low, sums[r], sums[r + 1]).astype(out.dtype)
 
 
-def project(olds, pieces, rank, row_blocks, kind):
+def project(olds, pieces, rank, kind):
     sides = len(olds)
     height, width = pieces[0].shape
     shapes = [
@@ -239,7 +240,7 @@
         jax.ShapeDtypeStruct((rank, width // 2), kind),
     ]
     return pl.pallas_call(
-        functools.partial(project_kernel, sides=sides, rank=rank, row_blocks=row_blocks),
+        functools.partial(project_kernel, sides=sides, rank=rank),
         in_specs=[VMEM] * (sides + len(pieces)),
         out_specs=[VMEM] * 2,
         out_shape=shapes,
@@ -352,6 +353,60 @@
     )(*pieces, rows)
 
 
+def two_step(n_grp, split):
+    return n_grp == 4 and split == 2
+
+
+def reduce_layout(n_grp, split, core):
+    if not two_step(n_grp, split):
+        return [[(m, h) for h in range(split)] for m in range(n_grp)]
+    near, side = 1 + core, 2 - core
+    other = 1 - core
+    return [
+        [(near, core), (3, core)],
+        [(side, other), (3, other)],
+        [(0, core), (0, other), (side, core), (near, other)],
+    ]
+
+
+def reduce_panel(shares, old, n_grp, n_dev, split):
+    if not two_step(n_grp, split):
+        width = shares[0].shape[1] // split
+        parts = [shares[0]] + [swap(shares[m], "grp", n_grp, m) for m in range(1, n_grp)]
+        if split == 1:
+            return [old], parts
+        core = lax.axis_index("dev") % split
+
+        def side(i):
+            at = (core + i) % split * width
+            return [lax.dynamic_slice_in_dim(part, at, width, 1) for part in parts]
+
+        total = sum(part.astype(F32) for part in side(1)).astype(BF16)
+        crossed = swap(jnp.concatenate([total, old], axis=1), "dev", n_dev, 1)
+        own = sum(part.astype(F32) for part in side(0)).astype(BF16)
+        return [old, crossed], [own, crossed]
+
+    def send(x, own, cross):
+        pairs = []
+        for g in range(n_grp):
+            for d in range(n_dev):
+                core = d % 2
+                mask = 1 + core if own else 2 - core
+                pairs.append((g * n_dev + d, (g ^ mask) * n_dev + (d ^ cross)))
+        return lax.ppermute(x, ("grp", "dev"), pairs)
+
+    width = shares[0].shape[1] // 2
+    first = send(shares[0], True, 0).astype(F32)
+    second = send(shares[1], False, 0).astype(F32)
+    rest = [shares[2][:, i * width : (i + 1) * width].astype(F32) for i in range(4)]
+    own = send((rest[2] + first[:, width:]).astype(BF16), False, 0)
+    other = send((rest[3] + second[:, width:]).astype(BF16), True, 1)
+    crossed = (rest[1] + second[:, :width]).astype(BF16)
+    crossed = swap(jnp.concatenate([crossed, old], axis=1), "dev", n_dev, 1)
+    kept = (rest[0] + first[:, :width]).astype(BF16)
+    return [old, crossed], [kept, own, crossed, other]
+
+
 def body(blocks, coords, counts, row_place, factor_one, factor_two, factor_three):
     edge = blocks.shape[1]
     rank = factor_one.shape[1] // edge
@@ -359,13 +414,13 @@
     n_grp, n_dev = lax.axis_size("grp"), lax.axis_size("dev")
     direct = is_direct(n_dev)
     split = 2 if direct else 1
-    far = range(2, n_dev, 2)
+    far = range(n_dev - 2, 0, -2)
 
     def sibling(x):
         return swap(x, "dev", n_dev, 1)
 
     def over_grp(pieces):
-        return pieces[:1] + [swap(pieces[m], "grp", n_grp, m) for m in range(1, n_grp)]
+        return pieces[:1] + [swap(pieces[m], "grp", n_grp, m) for m in range(n_grp - 1, 0, -1)]
 
     packed = jnp.concatenate([factor_two, factor_three], axis=0)
     if direct:
@@ -375,14 +430,12 @@
         tables = [lax.all_gather(packed, "dev", axis=0, tiled=True)]
     hits = coords[:, :, None] == jnp.arange(row_place.shape[0])[None, None, :]
     places = jnp.sum(jnp.where(hits, row_place[None, None, :], 0), axis=2)
-    old = factor_one.reshape(row_blocks * edge, rank)
-    olds = [old, sibling(old)] if direct else [old]
     shares = list(contract(places, counts, blocks, tables, n_grp, split, row_blocks, rank))
-    pieces = over_grp(shares[:n_grp])
-    if direct:
-        pieces += over_grp([sibling(share) for share in shares[n_grp:]])
-
-    panel, proj = project(olds, pieces, rank, row_blocks, BF16 if direct else F32)
+    factor_one, shares[0] = lax.optimization_barrier((factor_one, shares[0]))
+    old = factor_one.reshape(row_blocks, 2, edge // 2, rank).transpose(0, 2, 1, 3)
+    old = old.reshape(row_blocks * edge // 2, 2 * rank)
+    olds, pieces = reduce_panel(shares, old, n_grp, n_dev, split)
+    panel, proj = project(olds, pieces, rank, BF16 if direct else F32)
     if direct:
         projs = [proj] + [swap(proj, "dev", n_dev, m) for m in far]
     else:

time: 63.1 us -> 60.2 us (0.954)
  starting transfers between devices: 29 us -> 23.8 us
  waiting for transfers between devices: 22.3 us -> 25.2 us
    ppermute x0 -> x4, waiting for transfers between devices: none -> 10.3 us  [send(): return lax.ppermute(x, ('grp', 'dev'), pairs)]
    ppermute x28 -> x18, starting transfers between devices: 29 us -> 18.9 us  [swap(): lax.ppermute(x, axis, [(i, partner(i, mask, size)) for i in range(size)])]
    ppermute x28 -> x18, waiting for transfers between devices: 22.3 us -> 14.9 us  [swap(): lax.ppermute(x, axis, [(i, partner(i, mask, size)) for i in range(size)])]
    ppermute x0 -> x4, starting transfers between devices: none -> 4.87 us  [send(): return lax.ppermute(x, ('grp', 'dev'), pairs)]
  transfers between devices with their start and end apart: 28 -> 22, of which waited for: 13 -> 13; matrix products, arithmetic and copies ran while one was open for 3% -> 2% of each run, Pallas kernels for 9% -> 0%
where the time goes in v3:
time: 60.2 us; the launch traced here: 59.9 us
  waiting for transfers between devices  25.2 us (42%)
  starting transfers between devices  23.8 us (40%)
  Pallas kernels  7.35 us (12%)
  other arithmetic  1.93 us (3%)
  between operations  1.43 us (2%)
    ppermute x18, starting transfers between devices, swap(): lax.ppermute(x, axis, [(i, partner(i, mask, size)) for i in range(size)])  18.9 us
    ppermute x18, waiting for transfers between devices, swap(): lax.ppermute(x, axis, [(i, partner(i, mask, size)) for i in range(size)])  14.9 us
    ppermute x4, waiting for transfers between devices, send(): return lax.ppermute(x, ('grp', 'dev'), pairs)  10.3 us
    pallas_call x1, Pallas kernels, contract(): pl.pallas_call(functools.partial(contract_kernel, n_tables=len(tables), n...  5.52 us
    ppermute x4, starting transfers between devices, send(): return lax.ppermute(x, ('grp', 'dev'), pairs)  4.87 us
  transfers between devices with their start and end apart: 22, of which 13 were waited for; matrix products, arithmetic and copies ran while one was open for 2% of the time, Pallas kernels for 0%

profile of v3, /device:TPU:0, one launch (start us, length us, event | category | flops | bytes accessed | tf_op | source)
XLA Modules:
  0.0 59.9 jit_solution(6296278826371297279)
XLA Ops:
  0.6 0.8 %pad_maximum_fusion.1.refs_3_ = bf16[4,4096]{1,0:T(4,128)(2,1)S(1)} fusion(bf16[2,4096]{1,0:T(2,128)(2,1)} %param.13, bf16[2,4096]{1,0:T(2,128)(2,1)} %param.12), kind=kLoop, calls=%fused_computation.10 | loop fusion | flops 65536 | bytes 65536 | tf_op jit(solution)/shard_map/concatenate | solution.py:425
  1.4 5.1 %collective-permute-start = (bf16[4,4096]{1,0:T(4,128)(2,1)S(1)}, bf16[4,4096]{1,0:T(4,128)(2,1)S(1)}, u32[]{:S(2)}, u32[]{:S(2)}) collective-permute-start(bf16[4,4096]{1,0:T(4,128)(2,1)S(1)} %pad_maximum_fusion.1.refs_3_), channel_id=1, source_target_pairs={{0,6},{1,7},{2,4},{3,5},{4,2},{5,3},{6,0},{7,1},{8,14},{9,15},{10,... | collective-permute-start | bytes 98312 | tf_op jit(solution)/shard_map/ppermute | solution.py:22
  6.5 0.6 %collective-permute-start.2 = (bf16[4,4096]{1,0:T(4,128)(2,1)S(1)}, bf16[4,4096]{1,0:T(4,128)(2,1)S(1)}, u32[]{:S(2)}, u32[]{:S(2)}) collective-permute-start(bf16[4,4096]{1,0:T(4,128)(2,1)S(1)} %pad_maximum_fusion.1.refs_3_), channel_id=1, source_target_pairs={{0,2},{1,3},{2,0},{3,1},{4,6},{5,7},{6,4},{7,5},{8,10},{9,11},{10,... | collective-permute-start | bytes 98312 | tf_op jit(solution)/shard_map/ppermute | solution.py:22
  7.2 1.2 %collective-permute-done.refs_4_ = bf16[4,4096]{1,0:T(4,128)(2,1)S(1)} collective-permute-done((bf16[4,4096]{1,0:T(4,128)(2,1)S(1)}, bf16[4,4096]{1,0:T(4,128)(2,1)S(1)}, u32[]{:S(2)}, u32[]{:S(2)}) %collective-permute-start) | collective-permute-done | bytes 32800 | tf_op jit(solution)/shard_map/ppermute | solution.py:22
  8.4 2.9 %collective-permute-done.1.refs_5_ = bf16[4,4096]{1,0:T(4,128)(2,1)S(1)} collective-permute-done((bf16[4,4096]{1,0:T(4,128)(2,1)S(1)}, bf16[4,4096]{1,0:T(4,128)(2,1)S(1)}, u32[]{:S(2)}, u32[]{:S(2)}) %collective-permute-start.1) | collective-permute-done | bytes 32800 | tf_op jit(solution)/shard_map/ppermute | solution.py:22
  11.4 0.0 collective-permute-start.5
  11.4 0.0 collective-permute-done.2.refs_6_
  11.4 0.5 collective-permute-start.6
  11.9 0.9 %select_reduce_fusion.refs_0_ = s32[3,8]{1,0:T(4,128)S(1)} fusion(s32[16]{0:T(128)} %param.10, s32[3,8]{1,0:T(4,128)} %param.8), kind=kLoop, calls=%fused_computation.12 | loop fusion | flops 1128 | bytes 256 | tf_op jit(solution)/shard_map/reduce_sum | solution.py:432
  13.4 0.0 collective-permute-done.4.refs_8_
  13.5 0.0 collective-permute-done.5.refs_9_
  13.5 5.5 %contract.1 = (bf16[64,2048]{1,0:T(8,128)(2,1)S(1)}, bf16[64,2048]{1,0:T(8,128)(2,1)S(1)}, bf16[64,4096]{1,0:T(8,128)(2,1)S(1)}) custom-call(s32[3,8]{1,0:T(4,128)S(1)} %select_reduce_fusion.refs_0_, s32[1]{0:T(128)S(6)} %copy.13.refs_1_, bf16[8,64,4096]{2,1,0:T(8,128)(2,1)} %refs_2_.1, bf16[4,4096]{1,0:T(4,128)(2,1)S(1)} %pad_maximum_fusion.1.refs_3_, ...), custom_call_target="tpu_custom_call" | custom-call | flops 1610612736 | bytes 6291456 | tf_op jit(solution)/shard_map/contract/pallas_call | solution.py:178
  19.0 1.6 %collective-permute-start.9 = (bf16[64,2048]{1,0:T(8,128)(2,1)S(1)}, bf16[64,2048]{1,0:T(8,128)(2,1)S(1)}, u32[]{:S(2)}, u32[]{:S(2)}) collective-permute-start(bf16[64,2048]{1,0:T(8,128)(2,1)S(1)} %get-tuple-element.15), channel_id=1, source_target_pairs={{0,8},{1,17},{2,10},{3,19},{4,12},{5,21},{6,14},{7,23},{8,0},{9,25... | collective-permute-start | bytes 786440 | tf_op jit(solution)/shard_map/ppermute | solution.py:396
  20.6 1.5 %collective-permute-start.7 = (bf16[64,2048]{1,0:T(8,128)(2,1)S(1)}, bf16[64,2048]{1,0:T(8,128)(2,1)S(1)}, u32[]{:S(2)}, u32[]{:S(2)}) collective-permute-start(bf16[64,2048]{1,0:T(8,128)(2,1)S(1)} %get-tuple-element.14), channel_id=1, source_target_pairs={{0,16},{1,9},{2,18},{3,11},{4,20},{5,13},{6,22},{7,15},{8,24},{9,1... | collective-permute-start | bytes 786440 | tf_op jit(solution)/shard_map/ppermute | solution.py:396
  22.1 0.1 reshape.12
  22.2 0.1 reshape.13.refs_0_
  22.3 5.7 %collective-permute-done.9 = bf16[64,2048]{1,0:T(8,128)(2,1)S(1)} collective-permute-done((bf16[64,2048]{1,0:T(8,128)(2,1)S(1)}, bf16[64,2048]{1,0:T(8,128)(2,1)S(1)}, u32[]{:S(2)}, u32[]{:S(2)}) %collective-permute-start.9) | collective-permute-done | bytes 262176 | tf_op jit(solution)/shard_map/ppermute | solution.py:396
  28.0 0.0 collective-permute-done.7
  28.1 0.1 fusion
  28.2 0.1 collective-permute-start.8
  28.4 1.1 %collective-permute-start.10 = (bf16[64,1024]{1,0:T(8,128)(2,1)S(1)}, bf16[64,1024]{1,0:T(8,128)(2,1)S(1)}, u32[]{:S(2)}, u32[]{:S(2)}) collective-permute-start(bf16[64,1024]{1,0:T(8,128)(2,1)S(1)} %get-tuple-element.25), channel_id=1, source_target_pairs={{0,16},{1,9},{2,18},{3,11},{4,20},{5,13},{6,22},{7,15},{8,24},{9,1... | collective-permute-start | bytes 393224 | tf_op jit(solution)/shard_map/ppermute | solution.py:396
  29.4 0.7 %collective-permute-start.11 = (bf16[64,1024]{1,0:T(8,128)(2,1)S(1)}, bf16[64,1024]{1,0:T(8,128)(2,1)S(1)}, u32[]{:S(2)}, u32[]{:S(2)}) collective-permute-start(bf16[64,1024]{1,0:T(8,128)(2,1)S(1)} %get-tuple-element.20), channel_id=1, source_target_pairs={{0,9},{1,16},{2,11},{3,18},{4,13},{5,20},{6,15},{7,22},{8,1},{9,24... | collective-permute-start | bytes 393224 | tf_op jit(solution)/shard_map/ppermute | solution.py:396
  30.2 4.2 %collective-permute-done.10.refs_3_ = bf16[64,1024]{1,0:T(8,128)(2,1)S(1)} collective-permute-done((bf16[64,1024]{1,0:T(8,128)(2,1)S(1)}, bf16[64,1024]{1,0:T(8,128)(2,1)S(1)}, u32[]{:S(2)}, u32[]{:S(2)}) %collective-permute-start.10) | collective-permute-done | bytes 131104 | tf_op jit(solution)/shard_map/ppermute | solution.py:396
  34.4 0.4 collective-permute-done.11.refs_5_
  34.8 0.0 collective-permute-done.8.refs_1_.refs_4_
  34.8 0.4 project.1
  35.2 1.0 %collective-permute-start.12 = (bf16[64,512]{1,0:T(8,128)(2,1)S(1)}, bf16[64,512]{1,0:T(8,128)(2,1)S(1)}, u32[]{:S(2)}, u32[]{:S(2)}) collective-permute-start(bf16[64,512]{1,0:T(8,128)(2,1)S(1)} %get-tuple-element.17.refs_0_), channel_id=1, source_target_pairs={{0,6},{1,7},{2,4},{3,5},{4,2},{5,3},{6,0},{7,1},{8,14},{9,15},{10,... | collective-permute-start | bytes 196616 | tf_op jit(solution)/shard_map/ppermute | solution.py:22
  36.1 0.6 %collective-permute-start.13 = (bf16[64,512]{1,0:T(8,128)(2,1)S(1)}, bf16[64,512]{1,0:T(8,128)(2,1)S(1)}, u32[]{:S(2)}, u32[]{:S(2)}) collective-permute-start(bf16[64,512]{1,0:T(8,128)(2,1)S(1)} %get-tuple-element.17.refs_0_), channel_id=1, source_target_pairs={{0,4},{1,5},{2,6},{3,7},{4,0},{5,1},{6,2},{7,3},{8,12},{9,13},{10,... | collective-permute-start | bytes 196616 | tf_op jit(solution)/shard_map/ppermute | solution.py:22
  36.8 2.8 %collective-permute-start.14 = (bf16[64,512]{1,0:T(8,128)(2,1)S(1)}, bf16[64,512]{1,0:T(8,128)(2,1)S(1)}, u32[]{:S(2)}, u32[]{:S(2)}) collective-permute-start(bf16[64,512]{1,0:T(8,128)(2,1)S(1)} %get-tuple-element.17.refs_0_), channel_id=1, source_target_pairs={{0,2},{1,3},{2,0},{3,1},{4,6},{5,7},{6,4},{7,5},{8,10},{9,11},{10,... | collective-permute-start | bytes 196616 | tf_op jit(solution)/shard_map/ppermute | solution.py:22
  39.6 2.4 %collective-permute-done.12.refs_1_ = bf16[64,512]{1,0:T(8,128)(2,1)S(1)} collective-permute-done((bf16[64,512]{1,0:T(8,128)(2,1)S(1)}, bf16[64,512]{1,0:T(8,128)(2,1)S(1)}, u32[]{:S(2)}, u32[]{:S(2)}) %collective-permute-start.12) | collective-permute-done | bytes 65568 | tf_op jit(solution)/shard_map/ppermute | solution.py:22
  42.0 1.3 %collective-permute-done.13.refs_2_ = bf16[64,512]{1,0:T(8,128)(2,1)S(1)} collective-permute-done((bf16[64,512]{1,0:T(8,128)(2,1)S(1)}, bf16[64,512]{1,0:T(8,128)(2,1)S(1)}, u32[]{:S(2)}, u32[]{:S(2)}) %collective-permute-start.13) | collective-permute-done | bytes 65568 | tf_op jit(solution)/shard_map/ppermute | solution.py:22
  43.3 0.3 row_terms.1
  43.7 2.3 %collective-permute-start.15 = (bf16[128,128]{1,0:T(8,128)(2,1)S(1)}, bf16[128,128]{1,0:T(8,128)(2,1)S(1)}, u32[]{:S(2)}, u32[]{:S(2)}) collective-permute-start(bf16[128,128]{1,0:T(8,128)(2,1)S(1)} %row_terms.1), channel_id=1, source_target_pairs={{0,24},{8,16},{16,8},{24,0},{1,25},{9,17},{17,9},{25,1},{2,26},{10... | collective-permute-start | bytes 98312 | tf_op jit(solution)/shard_map/ppermute | solution.py:22
  45.9 0.6 collective-permute-start.16
  46.5 0.7 %collective-permute-start.17 = (bf16[128,128]{1,0:T(8,128)(2,1)S(1)}, bf16[128,128]{1,0:T(8,128)(2,1)S(1)}, u32[]{:S(2)}, u32[]{:S(2)}) collective-permute-start(bf16[128,128]{1,0:T(8,128)(2,1)S(1)} %row_terms.1), channel_id=1, source_target_pairs={{0,8},{8,0},{16,24},{24,16},{1,9},{9,1},{17,25},{25,17},{2,10},{10... | collective-permute-start | bytes 98312 | tf_op jit(solution)/shard_map/ppermute | solution.py:22
  47.2 1.4 %collective-permute-done.15 = bf16[128,128]{1,0:T(8,128)(2,1)S(1)} collective-permute-done((bf16[128,128]{1,0:T(8,128)(2,1)S(1)}, bf16[128,128]{1,0:T(8,128)(2,1)S(1)}, u32[]{:S(2)}, u32[]{:S(2)}) %collective-permute-start.15) | collective-permute-done | bytes 32800 | tf_op jit(solution)/shard_map/ppermute | solution.py:22
  48.6 1.3 %collective-permute-done.16 = bf16[128,128]{1,0:T(8,128)(2,1)S(1)} collective-permute-done((bf16[128,128]{1,0:T(8,128)(2,1)S(1)}, bf16[128,128]{1,0:T(8,128)(2,1)S(1)}, u32[]{:S(2)}, u32[]{:S(2)}) %collective-permute-start.16) | collective-permute-done | bytes 32800 | tf_op jit(solution)/shard_map/ppermute | solution.py:22
  49.8 0.6 collective-permute-done.17
  50.4 0.1 collective-permute-start.18
  50.5 1.2 %collective-permute-done.18.refs_1_ = f32[128,128]{1,0:T(8,128)S(1)} collective-permute-done((f32[128,128]{1,0:T(8,128)S(1)}, f32[128,128]{1,0:T(8,128)S(1)}, u32[]{:S(2)}, u32[]{:S(2)}) %collective-permute-start.18) | collective-permute-done | bytes 65568 | tf_op jit(solution)/shard_map/ppermute | solution.py:22
  51.7 0.3 gram_terms.1
  52.1 2.2 %collective-permute-start.19 = (f32[64,64]{1,0:T(8,128)S(1)}, f32[64,64]{1,0:T(8,128)S(1)}, u32[]{:S(2)}, u32[]{:S(2)}) collective-permute-start(f32[64,64]{1,0:T(8,128)S(1)} %get-tuple-element.18.refs_0_), channel_id=1, source_target_pairs={{0,6},{1,7},{2,4},{3,5},{4,2},{5,3},{6,0},{7,1},{8,14},{9,15},{10,... | collective-permute-start | bytes 49160 | tf_op jit(solution)/shard_map/ppermute | solution.py:22
  54.3 0.0 collective-permute-start.20
  54.3 2.2 %collective-permute-start.21 = (f32[64,64]{1,0:T(8,128)S(1)}, f32[64,64]{1,0:T(8,128)S(1)}, u32[]{:S(2)}, u32[]{:S(2)}) collective-permute-start(f32[64,64]{1,0:T(8,128)S(1)} %get-tuple-element.18.refs_0_), channel_id=1, source_target_pairs={{0,2},{1,3},{2,0},{3,1},{4,6},{5,7},{6,4},{7,5},{8,10},{9,11},{10,... | collective-permute-start | bytes 49160 | tf_op jit(solution)/shard_map/ppermute | solution.py:22
  56.5 1.3 %collective-permute-done.19.refs_1_ = f32[64,64]{1,0:T(8,128)S(1)} collective-permute-done((f32[64,64]{1,0:T(8,128)S(1)}, f32[64,64]{1,0:T(8,128)S(1)}, u32[]{:S(2)}, u32[]{:S(2)}) %collective-permute-start.19) | collective-permute-done | bytes 16416 | tf_op jit(solution)/shard_map/ppermute | solution.py:22
  57.9 1.2 %collective-permute-done.20.refs_2_ = f32[64,64]{1,0:T(8,128)S(1)} collective-permute-done((f32[64,64]{1,0:T(8,128)S(1)}, f32[64,64]{1,0:T(8,128)S(1)}, u32[]{:S(2)}, u32[]{:S(2)}) %collective-permute-start.20) | collective-permute-done | bytes 16416 | tf_op jit(solution)/shard_map/ppermute | solution.py:22
  59.1 0.0 collective-permute-done.21.refs_3_
  59.1 0.8 %finish.1 = (f32[2,4096]{1,0:T(2,128)}, f32[64,64]{1,0:T(8,128)}) custom-call(f32[64,64]{1,0:T(8,128)S(1)} %get-tuple-element.18.refs_0_, f32[64,64]{1,0:T(8,128)S(1)} %collective-permute-done.19.refs_1_, f32[64,64]{1,0:T(8,128)S(1)} %collective-permute-done.20.refs_2_, f32[64,64]{1,0:T(8,128)S(1)} %collective-permute-done.21.refs_3_, ...), custom_call_target="tpu_custom_call" | custom-call | tf_op jit(solution)/shard_map/finish/pallas_call | solution.py:346
  (13 shorter events, 0.2 us)
Async XLA Ops:
  0.6 21.5 %copy-start = (bf16[2,4096]{1,0:T(2,128)(2,1)S(1)}, bf16[2,4096]{1,0:T(2,128)(2,1)}, u32[]{:S(2)}) copy-start(bf16[2,4096]{1,0:T(2,128)(2,1)} %param.11) | copy-start | bytes 49156
  1.4 7.0 %collective-permute-start = (bf16[4,4096]{1,0:T(4,128)(2,1)S(1)}, bf16[4,4096]{1,0:T(4,128)(2,1)S(1)}, u32[]{:S(2)}, u32[]{:S(2)}) collective-permute-start(bf16[4,4096]{1,0:T(4,128)(2,1)S(1)} %pad_maximum_fusion.1.refs_3_), channel_id=1, source_target_pairs={{0,6},{1,7},{2,4},{3,5},{4,2},{5,3},{6,0},{7,1},{8,14},{9,15},{10,... | collective-permute-start | bytes 98312 | tf_op jit(solution)/shard_map/ppermute | solution.py:22
  6.5 4.8 %collective-permute-start.1 = (bf16[4,4096]{1,0:T(4,128)(2,1)S(1)}, bf16[4,4096]{1,0:T(4,128)(2,1)S(1)}, u32[]{:S(2)}, u32[]{:S(2)}) collective-permute-start(bf16[4,4096]{1,0:T(4,128)(2,1)S(1)} %pad_maximum_fusion.1.refs_3_), channel_id=1, source_target_pairs={{0,4},{1,5},{2,6},{3,7},{4,0},{5,1},{6,2},{7,3},{8,12},{9,13},{10,... | collective-permute-start | bytes 98312 | tf_op jit(solution)/shard_map/ppermute | solution.py:22
  6.5 4.8 %collective-permute-start.2 = (bf16[4,4096]{1,0:T(4,128)(2,1)S(1)}, bf16[4,4096]{1,0:T(4,128)(2,1)S(1)}, u32[]{:S(2)}, u32[]{:S(2)}) collective-permute-start(bf16[4,4096]{1,0:T(4,128)(2,1)S(1)} %pad_maximum_fusion.1.refs_3_), channel_id=1, source_target_pairs={{0,2},{1,3},{2,0},{3,1},{4,6},{5,7},{6,4},{7,5},{8,10},{9,11},{10,... | collective-permute-start | bytes 98312 | tf_op jit(solution)/shard_map/ppermute | solution.py:22
  7.2 6.3 %collective-permute-start.3 = (bf16[4,4096]{1,0:T(4,128)(2,1)S(1)}, bf16[4,4096]{1,0:T(4,128)(2,1)S(1)}, u32[]{:S(2)}, u32[]{:S(2)}) collective-permute-start(bf16[4,4096]{1,0:T(4,128)(2,1)S(1)} %pad_maximum_fusion.1.refs_3_), channel_id=1, source_target_pairs={{0,1},{1,0},{2,3},{3,2},{4,5},{5,4},{6,7},{7,6},{8,9},{9,8},{10,11... | collective-permute-start | bytes 98312 | tf_op jit(solution)/shard_map/ppermute | solution.py:22
  8.4 5.0 %collective-permute-start.4 = (bf16[4,4096]{1,0:T(4,128)(2,1)S(1)}, bf16[4,4096]{1,0:T(4,128)(2,1)S(1)}, u32[]{:S(2)}, u32[]{:S(2)}) collective-permute-start(bf16[4,4096]{1,0:T(4,128)(2,1)S(1)} %collective-permute-done.refs_4_), channel_id=1, source_target_pairs={{0,1},{1,0},{2,3},{3,2},{4,5},{5,4},{6,7},{7,6},{8,9},{9,8},{10,11... | collective-permute-start | bytes 98312 | tf_op jit(solution)/shard_map/ppermute | solution.py:22
  11.4 2.1 %collective-permute-start.5 = (bf16[4,4096]{1,0:T(4,128)(2,1)S(1)}, bf16[4,4096]{1,0:T(4,128)(2,1)S(1)}, u32[]{:S(2)}, u32[]{:S(2)}) collective-permute-start(bf16[4,4096]{1,0:T(4,128)(2,1)S(1)} %collective-permute-done.1.refs_5_), channel_id=1, source_target_pairs={{0,1},{1,0},{2,3},{3,2},{4,5},{5,4},{6,7},{7,6},{8,9},{9,8},{10,11... | collective-permute-start | bytes 98312 | tf_op jit(solution)/shard_map/ppermute | solution.py:22
  11.4 2.1 %collective-permute-start.6 = (bf16[4,4096]{1,0:T(4,128)(2,1)S(1)}, bf16[4,4096]{1,0:T(4,128)(2,1)S(1)}, u32[]{:S(2)}, u32[]{:S(2)}) collective-permute-start(bf16[4,4096]{1,0:T(4,128)(2,1)S(1)} %collective-permute-done.2.refs_6_), channel_id=1, source_target_pairs={{0,1},{1,0},{2,3},{3,2},{4,5},{5,4},{6,7},{7,6},{8,9},{9,8},{10,11... | collective-permute-start | bytes 98312 | tf_op jit(solution)/shard_map/ppermute | solution.py:22
  19.0 9.0 %collective-permute-start.9 = (bf16[64,2048]{1,0:T(8,128)(2,1)S(1)}, bf16[64,2048]{1,0:T(8,128)(2,1)S(1)}, u32[]{:S(2)}, u32[]{:S(2)}) collective-permute-start(bf16[64,2048]{1,0:T(8,128)(2,1)S(1)} %get-tuple-element.15), channel_id=1, source_target_pairs={{0,8},{1,17},{2,10},{3,19},{4,12},{5,21},{6,14},{7,23},{8,0},{9,25... | collective-permute-start | bytes 786440 | tf_op jit(solution)/shard_map/ppermute | solution.py:396
  20.6 7.5 %collective-permute-start.7 = (bf16[64,2048]{1,0:T(8,128)(2,1)S(1)}, bf16[64,2048]{1,0:T(8,128)(2,1)S(1)}, u32[]{:S(2)}, u32[]{:S(2)}) collective-permute-start(bf16[64,2048]{1,0:T(8,128)(2,1)S(1)} %get-tuple-element.14), channel_id=1, source_target_pairs={{0,16},{1,9},{2,18},{3,11},{4,20},{5,13},{6,22},{7,15},{8,24},{9,1... | collective-permute-start | bytes 786440 | tf_op jit(solution)/shard_map/ppermute | solution.py:396
  28.2 6.5 %collective-permute-start.8 = (bf16[64,1152]{1,0:T(8,128)(2,1)S(1)}, bf16[64,1152]{1,0:T(8,128)(2,1)S(1)}, u32[]{:S(2)}, u32[]{:S(2)}) collective-permute-start(bf16[64,1152]{1,0:T(8,128)(2,1)S(1)} %pad_maximum_fusion), channel_id=1, source_target_pairs={{0,1},{1,0},{2,3},{3,2},{4,5},{5,4},{6,7},{7,6},{8,9},{9,8},{10,11... | collective-permute-start | bytes 442376 | tf_op jit(solution)/shard_map/ppermute | solution.py:22
  28.4 6.0 %collective-permute-start.10 = (bf16[64,1024]{1,0:T(8,128)(2,1)S(1)}, bf16[64,1024]{1,0:T(8,128)(2,1)S(1)}, u32[]{:S(2)}, u32[]{:S(2)}) collective-permute-start(bf16[64,1024]{1,0:T(8,128)(2,1)S(1)} %get-tuple-element.25), channel_id=1, source_target_pairs={{0,16},{1,9},{2,18},{3,11},{4,20},{5,13},{6,22},{7,15},{8,24},{9,1... | collective-permute-start | bytes 393224 | tf_op jit(solution)/shard_map/ppermute | solution.py:396
  29.4 5.3 %collective-permute-start.11 = (bf16[64,1024]{1,0:T(8,128)(2,1)S(1)}, bf16[64,1024]{1,0:T(8,128)(2,1)S(1)}, u32[]{:S(2)}, u32[]{:S(2)}) collective-permute-start(bf16[64,1024]{1,0:T(8,128)(2,1)S(1)} %get-tuple-element.20), channel_id=1, source_target_pairs={{0,9},{1,16},{2,11},{3,18},{4,13},{5,20},{6,15},{7,22},{8,1},{9,24... | collective-permute-start | bytes 393224 | tf_op jit(solution)/shard_map/ppermute | solution.py:396
  35.2 6.9 %collective-permute-start.12 = (bf16[64,512]{1,0:T(8,128)(2,1)S(1)}, bf16[64,512]{1,0:T(8,128)(2,1)S(1)}, u32[]{:S(2)}, u32[]{:S(2)}) collective-permute-start(bf16[64,512]{1,0:T(8,128)(2,1)S(1)} %get-tuple-element.17.refs_0_), channel_id=1, source_target_pairs={{0,6},{1,7},{2,4},{3,5},{4,2},{5,3},{6,0},{7,1},{8,14},{9,15},{10,... | collective-permute-start | bytes 196616 | tf_op jit(solution)/shard_map/ppermute | solution.py:22
  36.1 7.2 %collective-permute-start.13 = (bf16[64,512]{1,0:T(8,128)(2,1)S(1)}, bf16[64,512]{1,0:T(8,128)(2,1)S(1)}, u32[]{:S(2)}, u32[]{:S(2)}) collective-permute-start(bf16[64,512]{1,0:T(8,128)(2,1)S(1)} %get-tuple-element.17.refs_0_), channel_id=1, source_target_pairs={{0,4},{1,5},{2,6},{3,7},{4,0},{5,1},{6,2},{7,3},{8,12},{9,13},{10,... | collective-permute-start | bytes 196616 | tf_op jit(solution)/shard_map/ppermute | solution.py:22
  36.8 6.6 %collective-permute-start.14 = (bf16[64,512]{1,0:T(8,128)(2,1)S(1)}, bf16[64,512]{1,0:T(8,128)(2,1)S(1)}, u32[]{:S(2)}, u32[]{:S(2)}) collective-permute-start(bf16[64,512]{1,0:T(8,128)(2,1)S(1)} %get-tuple-element.17.refs_0_), channel_id=1, source_target_pairs={{0,2},{1,3},{2,0},{3,1},{4,6},{5,7},{6,4},{7,5},{8,10},{9,11},{10,... | collective-permute-start | bytes 196616 | tf_op jit(solution)/shard_map/ppermute | solution.py:22
  43.7 4.9 %collective-permute-start.15 = (bf16[128,128]{1,0:T(8,128)(2,1)S(1)}, bf16[128,128]{1,0:T(8,128)(2,1)S(1)}, u32[]{:S(2)}, u32[]{:S(2)}) collective-permute-start(bf16[128,128]{1,0:T(8,128)(2,1)S(1)} %row_terms.1), channel_id=1, source_target_pairs={{0,24},{8,16},{16,8},{24,0},{1,25},{9,17},{17,9},{25,1},{2,26},{10... | collective-permute-start | bytes 98312 | tf_op jit(solution)/shard_map/ppermute | solution.py:22
  45.9 3.9 %collective-permute-start.16 = (bf16[128,128]{1,0:T(8,128)(2,1)S(1)}, bf16[128,128]{1,0:T(8,128)(2,1)S(1)}, u32[]{:S(2)}, u32[]{:S(2)}) collective-permute-start(bf16[128,128]{1,0:T(8,128)(2,1)S(1)} %row_terms.1), channel_id=1, source_target_pairs={{0,16},{8,24},{16,0},{24,8},{1,17},{9,25},{17,1},{25,9},{2,18},{10... | collective-permute-start | bytes 98312 | tf_op jit(solution)/shard_map/ppermute | solution.py:22
  46.5 3.9 %collective-permute-start.17 = (bf16[128,128]{1,0:T(8,128)(2,1)S(1)}, bf16[128,128]{1,0:T(8,128)(2,1)S(1)}, u32[]{:S(2)}, u32[]{:S(2)}) collective-permute-start(bf16[128,128]{1,0:T(8,128)(2,1)S(1)} %row_terms.1), channel_id=1, source_target_pairs={{0,8},{8,0},{16,24},{24,16},{1,9},{9,1},{17,25},{25,17},{2,10},{10... | collective-permute-start | bytes 98312 | tf_op jit(solution)/shard_map/ppermute | solution.py:22
  50.4 1.3 %collective-permute-start.18 = (f32[128,128]{1,0:T(8,128)S(1)}, f32[128,128]{1,0:T(8,128)S(1)}, u32[]{:S(2)}, u32[]{:S(2)}) collective-permute-start(f32[128,128]{1,0:T(8,128)S(1)} %convert_add_fusion.refs_0_), channel_id=1, source_target_pairs={{0,1},{1,0},{2,3},{3,2},{4,5},{5,4},{6,7},{7,6},{8,9},{9,8},{10,11... | collective-permute-start | bytes 196616 | tf_op jit(solution)/shard_map/ppermute | solution.py:22
  52.1 5.8 %collective-permute-start.19 = (f32[64,64]{1,0:T(8,128)S(1)}, f32[64,64]{1,0:T(8,128)S(1)}, u32[]{:S(2)}, u32[]{:S(2)}) collective-permute-start(f32[64,64]{1,0:T(8,128)S(1)} %get-tuple-element.18.refs_0_), channel_id=1, source_target_pairs={{0,6},{1,7},{2,4},{3,5},{4,2},{5,3},{6,0},{7,1},{8,14},{9,15},{10,... | collective-permute-start | bytes 49160 | tf_op jit(solution)/shard_map/ppermute | solution.py:22
  54.3 4.8 %collective-permute-start.20 = (f32[64,64]{1,0:T(8,128)S(1)}, f32[64,64]{1,0:T(8,128)S(1)}, u32[]{:S(2)}, u32[]{:S(2)}) collective-permute-start(f32[64,64]{1,0:T(8,128)S(1)} %get-tuple-element.18.refs_0_), channel_id=1, source_target_pairs={{0,4},{1,5},{2,6},{3,7},{4,0},{5,1},{6,2},{7,3},{8,12},{9,13},{10,... | collective-permute-start | bytes 49160 | tf_op jit(solution)/shard_map/ppermute | solution.py:22
  54.3 4.8 %collective-permute-start.21 = (f32[64,64]{1,0:T(8,128)S(1)}, f32[64,64]{1,0:T(8,128)S(1)}, u32[]{:S(2)}, u32[]{:S(2)}) collective-permute-start(f32[64,64]{1,0:T(8,128)S(1)} %get-tuple-element.18.refs_0_), channel_id=1, source_target_pairs={{0,2},{1,3},{2,0},{3,1},{4,6},{5,7},{6,4},{7,5},{8,10},{9,11},{10,... | collective-permute-start | bytes 49160 | tf_op jit(solution)/shard_map/ppermute | solution.py:22

commit v4 on v3

--- a/solution.py
+++ b/solution.py
@@ -12,6 +12,7 @@
 VMEM = pl.BlockSpec(memory_space=pltpu.VMEM)
 SMEM = pl.BlockSpec(memory_space=pltpu.SMEM)
 DIRECT_LIMIT = 8
+GROUPS = (0, 1, 4)
 
 
 def partner(i, mask, size):
@@ -35,28 +36,26 @@
 
 
 def contract_kernel(*refs, n_tables, n_grp, split, n_outs, slots, row_blocks, edge, rank):
-    places, counts, blocks = refs[:3]
-    tables, refs = refs[3 : 3 + n_tables], refs[3 + n_tables :]
+    places, blocks = refs[:2]
+    tables, refs = refs[2 : 2 + n_tables], refs[2 + n_tables :]
     outs, refs = refs[:n_outs], refs[n_outs:]
-    place, live, xbuf, fbuf, zbuf, vbuf, wbuf, meta_sem, block_sem = refs
+    place, xbuf, fbuf, zbuf, vbuf, wbuf, meta_sem, block_sem = refs
     half = edge // 2
     lanes = 2 * rank
     tile = 8
 
-    meta = [
-        pltpu.make_async_copy(source, target, meta_sem.at[i])
-        for i, (source, target) in enumerate(((places, place), (counts, live)))
-    ]
+    meta = pltpu.make_async_copy(places, place, meta_sem.at[0])
     loads = [pltpu.make_async_copy(blocks.at[s], xbuf.at[s], block_sem.at[s]) for s in range(slots)]
-    for copy in meta + loads:
+    for copy in [meta] + loads:
         copy.start()
 
-    height = tables[0].shape[0]
-    total = height * n_tables
+    owners = [table.at[i] for table in tables for i in range(table.shape[0])]
+    height = owners[0].shape[0]
+    total = height * len(owners)
     low = lax.broadcasted_iota(jnp.int32, (height, lanes), 1) < rank
-    for i in range(n_tables):
+    for i, owner in enumerate(owners):
         for j in range(half):
-            pair = tables[i][:, j * lanes : (j + 1) * lanes].astype(F32)
+            pair = owner[:, j * lanes : (j + 1) * lanes].astype(F32)
             turned = pltpu.roll(pair, rank, 1)
             for q in range(2):
                 k = 2 * j + q
@@ -64,8 +63,7 @@
                 fbuf[pl.ds(at, height, stride=tile), :] = (
                     jnp.where(low, turned, pair) if q else jnp.where(low, pair, turned)
                 )
-    for copy in meta:
-        copy.wait()
+    meta.wait()
     me = lax.axis_index("dev").astype(jnp.int32) if split > 1 else 0
     core = me % split
     per_owner = 2 * row_blocks
@@ -102,14 +100,16 @@
                 axis=0,
             )
         )
-        mine = jnp.where(s < live[0], pos[0] % row_blocks, row_blocks)
         for p in range(row_blocks // 2):
-            keep = 2 * p + lane // rank == mine
+            keep = 2 * p + lane // rank == pos[0]
             wbuf[s * edge : (s + 1) * edge, p * lanes : (p + 1) * lanes] = jnp.where(keep, u2, 0.0)
     left = wbuf[...].T.astype(BF16)
 
     for s in range(slots):
-        loads[s].wait()
+        if s in GROUPS:
+            last = min([g for g in GROUPS if g > s] + [slots])
+            for t in range(s, last):
+                loads[t].wait()
         slabs = []
         for j in range(half):
             cols = slice(j * 2 * edge, (j + 1) * 2 * edge)
@@ -157,7 +157,7 @@
                     out[p * half : (p + 1) * half, cols] = jnp.concatenate(parts, axis=0).astype(BF16)
 
 
-def contract(places, counts, blocks, tables, n_grp, split, row_blocks, rank):
+def contract(places, blocks, tables, n_grp, split, row_blocks, rank):
     slots, edge, width = blocks.shape
     half, lanes = edge // 2, 2 * rank
     part = rank // (n_grp * split) * lanes
@@ -165,7 +165,7 @@
         jax.ShapeDtypeStruct((row_blocks * half, part * len(pieces)), BF16)
         for pieces in reduce_layout(n_grp, split, 0)
     ]
-    factor_rows = sum(table.shape[0] for table in tables)
+    factor_rows = sum(table.shape[0] * table.shape[1] for table in tables)
     flops = 2 * slots * edge * width * 4 * edge + 2 * row_blocks * rank * slots * edge * edge * rank
     floats = [
         (edge * factor_rows, lanes),
@@ -187,15 +187,14 @@
             edge=edge,
             rank=rank,
         ),
-        in_specs=[far] * 3 + [VMEM] * len(tables),
+        in_specs=[far] * 2 + [VMEM] * len(tables),
         out_specs=[VMEM] * len(shapes),
         out_shape=shapes,
         scratch_shapes=[
             pltpu.SMEM(places.shape, jnp.int32),
-            pltpu.SMEM(counts.shape, jnp.int32),
             pltpu.VMEM(blocks.shape, BF16),
             *(pltpu.VMEM(shape, F32) for shape in floats),
-            pltpu.SemaphoreType.DMA((2,)),
+            pltpu.SemaphoreType.DMA((1,)),
             pltpu.SemaphoreType.DMA((slots,)),
         ],
         compiler_params=params(max(held + 8 * 1024 * 1024, 50 * 1024 * 1024)),
@@ -203,11 +202,11 @@
             flops=flops, bytes_accessed=2 * blocks.size + 4 * row_blocks * edge * rank * rank, transcendentals=0
         ),
         name="contract",
-    )(places, counts, blocks, *tables)
+    )(places, blocks, *tables)
 
 
 def project_kernel(*refs, sides, rank):
-    olds, pieces, panel, out = refs[:sides], refs[sides:-2], refs[-2], refs[-1]
+    pieces, olds, panel, out = refs[: -sides - 2], refs[-sides - 2 : -2], refs[-2], refs[-1]
     count = len(pieces) // sides
     width = panel.shape[1]
     lanes = 2 * rank
@@ -246,7 +245,7 @@
         out_shape=shapes,
         compiler_params=params(24 * 1024 * 1024),
         name="project",
-    )(*olds, *pieces)
+    )(*pieces, *olds)
 
 
 def rows_kernel(panel, *refs, rank):
@@ -290,14 +289,15 @@
         total = jnp.concatenate([own, terms[0][height:, :] + terms[1][:height, :]], axis=0)
     rows[...] = total[:height, :]
     full = jnp.dot(total.T, total, precision=lax.Precision.HIGHEST, preferred_element_type=F32)
-    gram[...] = full[:rank, :rank] + full[rank:, rank:]
+    square = full[:rank, :rank] + full[rank:, rank:]
+    gram[...] = jnp.concatenate([square[: rank // 2, :], square[rank // 2 :, :]], axis=1)
 
 
 def gram_terms(terms, rank):
     height, lanes = terms[0].shape
     shapes = [
         jax.ShapeDtypeStruct((height // len(terms), lanes), F32),
-        jax.ShapeDtypeStruct((rank, rank), F32),
+        jax.ShapeDtypeStruct((rank // 2, lanes), F32),
     ]
     return pl.pallas_call(
         functools.partial(gram_kernel, rank=rank),
@@ -314,7 +314,8 @@
     total = pieces[0][...]
     for piece in pieces[1:]:
         total = total + piece[...]
-    rank = total.shape[0]
+    rank = gram.shape[0]
+    total = jnp.concatenate([total[:, :rank], total[:, rank:]], axis=0)
     square = total.shape
     diagonal = lax.broadcasted_iota(jnp.int32, square, 0) == lax.broadcasted_iota(jnp.int32, square, 1)
     trace = jnp.sum(jnp.where(diagonal, total, 0.0), axis=1, keepdims=True)
@@ -338,7 +339,7 @@
 
 
 def finish(pieces, rows, row_blocks, rows_total):
-    rank = pieces[0].shape[0]
+    rank = pieces[0].shape[1] // 2
     shapes = [
         jax.ShapeDtypeStruct((row_blocks, rows.size // row_blocks), F32),
         jax.ShapeDtypeStruct((rank, rank), F32),
@@ -365,7 +366,8 @@
     return [
         [(near, core), (3, core)],
         [(side, other), (3, other)],
-        [(0, core), (0, other), (side, core), (near, other)],
+        [(side, core)],
+        [(0, core), (0, other), (near, other)],
     ]
 
 
@@ -398,13 +400,13 @@
     width = shares[0].shape[1] // 2
     first = send(shares[0], True, 0).astype(F32)
     second = send(shares[1], False, 0).astype(F32)
-    rest = [shares[2][:, i * width : (i + 1) * width].astype(F32) for i in range(4)]
-    own = send((rest[2] + first[:, width:]).astype(BF16), False, 0)
-    other = send((rest[3] + second[:, width:]).astype(BF16), True, 1)
+    own = send((shares[2].astype(F32) + first[:, width:]).astype(BF16), False, 0)
+    rest = [shares[3][:, i * width : (i + 1) * width].astype(F32) for i in range(3)]
+    other = send((rest[2] + second[:, width:]).astype(BF16), True, 1)
     crossed = (rest[1] + second[:, :width]).astype(BF16)
     crossed = swap(jnp.concatenate([crossed, old], axis=1), "dev", n_dev, 1)
     kept = (rest[0] + first[:, :width]).astype(BF16)
-    return [old, crossed], [kept, own, crossed, other]
+    return [old, crossed], [kept, own, other, crossed]
 
 
 def body(blocks, coords, counts, row_place, factor_one, factor_two, factor_three):
@@ -424,13 +426,16 @@
 
     packed = jnp.concatenate([factor_two, factor_three], axis=0)
     if direct:
-        tables = [packed] + [swap(packed, "dev", n_dev, m) for m in far]
-        tables += [sibling(table) for table in tables]
+        tables = [jnp.stack([packed] + [swap(packed, "dev", n_dev, m) for m in far])]
+        tables.append(sibling(tables[0]))
     else:
-        tables = [lax.all_gather(packed, "dev", axis=0, tiled=True)]
+        tables = [lax.all_gather(packed, "dev", axis=0)]
     hits = coords[:, :, None] == jnp.arange(row_place.shape[0])[None, None, :]
     places = jnp.sum(jnp.where(hits, row_place[None, None, :], 0), axis=2)
-    shares = list(contract(places, counts, blocks, tables, n_grp, split, row_blocks, rank))
+    live = jnp.arange(coords.shape[1])[None, :] < counts[0]
+    row = jnp.where(live, places % row_blocks, row_blocks)
+    places = jnp.where(jnp.arange(coords.shape[0])[:, None] == 0, row, places)
+    shares = list(contract(places, blocks, tables, n_grp, split, row_blocks, rank))
     factor_one, shares[0] = lax.optimization_barrier((factor_one, shares[0]))
     old = factor_one.reshape(row_blocks, 2, edge // 2, rank).transpose(0, 2, 1, 3)
     old = old.reshape(row_blocks * edge // 2, 2 * rank)

time: 60.2 us -> 58.9 us (0.978)
  Pallas kernels: 7.35 us -> 6.44 us
    pallas_call x1, Pallas kernels: 5.52 us -> 4.49 us  [contract(): pl.pallas_call(functools.partial(contract_kernel, n_tables=len(tables), n...]
    another operation x0 -> x2, other arithmetic: none -> 0.89 us  [body(): jnp.stack([packed] + [swap(packed, 'dev', n_dev, m) for m in far])]
    concatenate x1 -> x0, other arithmetic: 0.78 us -> none  [body(): packed = jnp.concatenate([factor_two, factor_three], axis=0)]
    ppermute x18 -> x15, starting transfers between devices: 18.9 us -> 18.5 us  [swap(): lax.ppermute(x, axis, [(i, partner(i, mask, size)) for i in range(size)])]
    ppermute x18 -> x15, waiting for transfers between devices: 14.9 us -> 14.9 us  [swap(): lax.ppermute(x, axis, [(i, partner(i, mask, size)) for i in range(size)])]
  transfers between devices with their start and end apart: 22 -> 19, of which waited for: 13 -> 13; matrix products, arithmetic and copies ran while one was open for 2% -> 2% of each run, Pallas kernels for 0% -> 0%
where the time goes in v4:
time: 58.9 us; the launch traced here: 58.6 us
  waiting for transfers between devices  25.1 us (43%)
  starting transfers between devices  23.3 us (40%)
  Pallas kernels  6.44 us (11%)
  other arithmetic  2.13 us (4%)
  between operations  1.41 us (2%)
    ppermute x15, starting transfers between devices, swap(): lax.ppermute(x, axis, [(i, partner(i, mask, size)) for i in range(size)])  18.5 us
    ppermute x15, waiting for transfers between devices, swap(): lax.ppermute(x, axis, [(i, partner(i, mask, size)) for i in range(size)])  14.9 us
    ppermute x4, waiting for transfers between devices, send(): return lax.ppermute(x, ('grp', 'dev'), pairs)  10.2 us
    ppermute x4, starting transfers between devices, send(): return lax.ppermute(x, ('grp', 'dev'), pairs)  4.84 us
    pallas_call x1, Pallas kernels, contract(): pl.pallas_call(functools.partial(contract_kernel, n_tables=len(tables), n...  4.49 us
  transfers between devices with their start and end apart: 19, of which 13 were waited for; matrix products, arithmetic and copies ran while one was open for 2% of the time, Pallas kernels for 0%

profile of v4, /device:TPU:0, one launch (start us, length us, event | category | flops | bytes accessed | tf_op | source)
XLA Modules:
  0.0 58.6 jit_solution(15332709987771488553)
XLA Ops:
  0.6 0.8 %fusion.7 = (bf16[1,4,4096]{2,1,0:T(4,128)(2,1)S(1)}, bf16[4,4096]{1,0:T(4,128)(2,1)S(1)}) fusion(bf16[2,4096]{1,0:T(2,128)(2,1)} %param.13, bf16[2,4096]{1,0:T(2,128)(2,1)} %param.12), kind=kLoop, calls=%fused_computation.23 | loop fusion | flops 65536 | bytes 98304 | tf_op jit(solution)/shard_map/stack | solution.py:429
  1.4 5.1 %collective-permute-start = (bf16[4,4096]{1,0:T(4,128)(2,1)S(1)}, bf16[4,4096]{1,0:T(4,128)(2,1)S(1)}, u32[]{:S(2)}, u32[]{:S(2)}) collective-permute-start(bf16[4,4096]{1,0:T(4,128)(2,1)S(1)} %get-tuple-element.29), channel_id=1, source_target_pairs={{0,6},{1,7},{2,4},{3,5},{4,2},{5,3},{6,0},{7,1},{8,14},{9,15},{10,... | collective-permute-start | bytes 98312 | tf_op jit(solution)/shard_map/ppermute | solution.py:23
  6.5 0.0 collective-permute-start.1
  6.5 0.6 %collective-permute-start.2 = (bf16[4,4096]{1,0:T(4,128)(2,1)S(1)}, bf16[4,4096]{1,0:T(4,128)(2,1)S(1)}, u32[]{:S(2)}, u32[]{:S(2)}) collective-permute-start(bf16[4,4096]{1,0:T(4,128)(2,1)S(1)} %get-tuple-element.29), channel_id=1, source_target_pairs={{0,2},{1,3},{2,0},{3,1},{4,6},{5,7},{6,4},{7,5},{8,10},{9,11},{10,... | collective-permute-start | bytes 98312 | tf_op jit(solution)/shard_map/ppermute | solution.py:23
  7.8 0.9 %select_reduce_fusion = s32[3,8]{1,0:T(4,128)S(1)} fusion(s32[16]{0:T(128)} %param.10, s32[3,8]{1,0:T(4,128)} %param.8), kind=kLoop, calls=%fused_computation.13 | loop fusion | flops 1128 | bytes 256 | tf_op jit(solution)/shard_map/reduce_sum | solution.py:434
  8.8 0.0 collective-permute-done
  8.8 2.6 %collective-permute-done.1 = bf16[4,4096]{1,0:T(4,128)(2,1)S(1)} collective-permute-done((bf16[4,4096]{1,0:T(4,128)(2,1)S(1)}, bf16[4,4096]{1,0:T(4,128)(2,1)S(1)}, u32[]{:S(2)}, u32[]{:S(2)}) %collective-permute-start.1) | collective-permute-done | bytes 32800 | tf_op jit(solution)/shard_map/ppermute | solution.py:23
  11.4 0.0 collective-permute-done.2
  11.4 0.1 pad_maximum_fusion.1.refs_2_
  11.5 0.1 collective-permute-start.3
  11.6 0.1 fusion.6.refs_0_
  11.6 1.3 %collective-permute-done.3.refs_3_ = bf16[4,4,4096]{2,1,0:T(4,128)(2,1)S(1)} collective-permute-done((bf16[4,4,4096]{2,1,0:T(4,128)(2,1)S(1)}, bf16[4,4,4096]{2,1,0:T(4,128)(2,1)S(1)}, u32[]{:S(2)}, u32[]{:S(2)}) %collective-permute-start.3) | collective-permute-done | bytes 131104 | tf_op jit(solution)/shard_map/ppermute | solution.py:23
  12.9 4.5 %contract.1 = (bf16[64,2048]{1,0:T(8,128)(2,1)S(1)}, bf16[64,2048]{1,0:T(8,128)(2,1)S(1)}, bf16[64,1024]{1,0:T(8,128)(2,1)S(1)}, bf16[64,3072]{1,0:T(8,128)(2,1)S(1)}) custom-call(s32[3,8]{1,0:T(4,128)S(1)} %fusion.6.refs_0_, bf16[8,64,4096]{2,1,0:T(8,128)(2,1)} %refs_1_.1, bf16[4,4,4096]{2,1,0:T(4,128)(2,1)S(1)} %pad_maximum_fusion.1.refs_2_, ...), custom_call_target="tpu_custom_call" | custom-call | flops 1610612736 | bytes 6291456 | tf_op jit(solution)/shard_map/contract/pallas_call | solution.py:178
  17.4 1.6 %collective-permute-start.4 = (bf16[64,2048]{1,0:T(8,128)(2,1)S(1)}, bf16[64,2048]{1,0:T(8,128)(2,1)S(1)}, u32[]{:S(2)}, u32[]{:S(2)}) collective-permute-start(bf16[64,2048]{1,0:T(8,128)(2,1)S(1)} %get-tuple-element.14), channel_id=1, source_target_pairs={{0,8},{1,17},{2,10},{3,19},{4,12},{5,21},{6,14},{7,23},{8,0},{9,25... | collective-permute-start | bytes 786440 | tf_op jit(solution)/shard_map/ppermute | solution.py:398
  18.9 1.5 %collective-permute-start.6 = (bf16[64,2048]{1,0:T(8,128)(2,1)S(1)}, bf16[64,2048]{1,0:T(8,128)(2,1)S(1)}, u32[]{:S(2)}, u32[]{:S(2)}) collective-permute-start(bf16[64,2048]{1,0:T(8,128)(2,1)S(1)} %get-tuple-element.16), channel_id=1, source_target_pairs={{0,16},{1,9},{2,18},{3,11},{4,20},{5,13},{6,22},{7,15},{8,24},{9,1... | collective-permute-start | bytes 786440 | tf_op jit(solution)/shard_map/ppermute | solution.py:398
  20.5 0.1 reshape.22
  20.6 0.1 reshape.23.refs_4_
  20.7 5.6 %collective-permute-done.4 = bf16[64,2048]{1,0:T(8,128)(2,1)S(1)} collective-permute-done((bf16[64,2048]{1,0:T(8,128)(2,1)S(1)}, bf16[64,2048]{1,0:T(8,128)(2,1)S(1)}, u32[]{:S(2)}, u32[]{:S(2)}) %collective-permute-start.4) | collective-permute-done | bytes 262176 | tf_op jit(solution)/shard_map/ppermute | solution.py:398
  26.3 0.0 collective-permute-done.6
  26.4 0.1 fusion.2
  26.6 0.2 collective-permute-start.8
  26.7 1.2 %collective-permute-start.5 = (bf16[64,1024]{1,0:T(8,128)(2,1)S(1)}, bf16[64,1024]{1,0:T(8,128)(2,1)S(1)}, u32[]{:S(2)}, u32[]{:S(2)}) collective-permute-start(bf16[64,1024]{1,0:T(8,128)(2,1)S(1)} %get-tuple-element.24), channel_id=1, source_target_pairs={{0,16},{1,9},{2,18},{3,11},{4,20},{5,13},{6,22},{7,15},{8,24},{9,1... | collective-permute-start | bytes 393224 | tf_op jit(solution)/shard_map/ppermute | solution.py:398
  28.0 0.5 collective-permute-start.7
  28.5 4.0 %collective-permute-done.5.refs_1_ = bf16[64,1024]{1,0:T(8,128)(2,1)S(1)} collective-permute-done((bf16[64,1024]{1,0:T(8,128)(2,1)S(1)}, bf16[64,1024]{1,0:T(8,128)(2,1)S(1)}, u32[]{:S(2)}, u32[]{:S(2)}) %collective-permute-start.5) | collective-permute-done | bytes 131104 | tf_op jit(solution)/shard_map/ppermute | solution.py:398
  32.5 0.6 %collective-permute-done.7.refs_2_ = bf16[64,1024]{1,0:T(8,128)(2,1)S(1)} collective-permute-done((bf16[64,1024]{1,0:T(8,128)(2,1)S(1)}, bf16[64,1024]{1,0:T(8,128)(2,1)S(1)}, u32[]{:S(2)}, u32[]{:S(2)}) %collective-permute-start.7) | collective-permute-done | bytes 131104 | tf_op jit(solution)/shard_map/ppermute | solution.py:398
  33.1 0.4 project.1
  33.5 2.1 %collective-permute-start.10 = (bf16[64,512]{1,0:T(8,128)(2,1)S(1)}, bf16[64,512]{1,0:T(8,128)(2,1)S(1)}, u32[]{:S(2)}, u32[]{:S(2)}) collective-permute-start(bf16[64,512]{1,0:T(8,128)(2,1)S(1)} %get-tuple-element.19.refs_0_), channel_id=1, source_target_pairs={{0,4},{1,5},{2,6},{3,7},{4,0},{5,1},{6,2},{7,3},{8,12},{9,13},{10,... | collective-permute-start | bytes 196616 | tf_op jit(solution)/shard_map/ppermute | solution.py:23
  35.6 2.4 %collective-permute-start.9 = (bf16[64,512]{1,0:T(8,128)(2,1)S(1)}, bf16[64,512]{1,0:T(8,128)(2,1)S(1)}, u32[]{:S(2)}, u32[]{:S(2)}) collective-permute-start(bf16[64,512]{1,0:T(8,128)(2,1)S(1)} %get-tuple-element.19.refs_0_), channel_id=1, source_target_pairs={{0,6},{1,7},{2,4},{3,5},{4,2},{5,3},{6,0},{7,1},{8,14},{9,15},{10,... | collective-permute-start | bytes 196616 | tf_op jit(solution)/shard_map/ppermute | solution.py:23
  37.9 1.4 %collective-permute-done.10.refs_2_ = bf16[64,512]{1,0:T(8,128)(2,1)S(1)} collective-permute-done((bf16[64,512]{1,0:T(8,128)(2,1)S(1)}, bf16[64,512]{1,0:T(8,128)(2,1)S(1)}, u32[]{:S(2)}, u32[]{:S(2)}) %collective-permute-start.10) | collective-permute-done | bytes 65568 | tf_op jit(solution)/shard_map/ppermute | solution.py:23
  39.3 2.5 %collective-permute-done.11.refs_3_ = bf16[64,512]{1,0:T(8,128)(2,1)S(1)} collective-permute-done((bf16[64,512]{1,0:T(8,128)(2,1)S(1)}, bf16[64,512]{1,0:T(8,128)(2,1)S(1)}, u32[]{:S(2)}, u32[]{:S(2)}) %collective-permute-start.11) | collective-permute-done | bytes 65568 | tf_op jit(solution)/shard_map/ppermute | solution.py:23
  41.8 0.0 collective-permute-done.9.refs_1_
  41.8 0.3 row_terms.1
  42.1 2.2 %collective-permute-start.12 = (bf16[128,128]{1,0:T(8,128)(2,1)S(1)}, bf16[128,128]{1,0:T(8,128)(2,1)S(1)}, u32[]{:S(2)}, u32[]{:S(2)}) collective-permute-start(bf16[128,128]{1,0:T(8,128)(2,1)S(1)} %row_terms.1), channel_id=1, source_target_pairs={{0,24},{8,16},{16,8},{24,0},{1,25},{9,17},{17,9},{25,1},{2,26},{10... | collective-permute-start | bytes 98312 | tf_op jit(solution)/shard_map/ppermute | solution.py:23
  44.3 0.8 %collective-permute-start.13 = (bf16[128,128]{1,0:T(8,128)(2,1)S(1)}, bf16[128,128]{1,0:T(8,128)(2,1)S(1)}, u32[]{:S(2)}, u32[]{:S(2)}) collective-permute-start(bf16[128,128]{1,0:T(8,128)(2,1)S(1)} %row_terms.1), channel_id=1, source_target_pairs={{0,16},{8,24},{16,0},{24,8},{1,17},{9,25},{17,1},{25,9},{2,18},{10... | collective-permute-start | bytes 98312 | tf_op jit(solution)/shard_map/ppermute | solution.py:23
  45.1 0.6 collective-permute-start.14
  45.7 1.4 %collective-permute-done.12 = bf16[128,128]{1,0:T(8,128)(2,1)S(1)} collective-permute-done((bf16[128,128]{1,0:T(8,128)(2,1)S(1)}, bf16[128,128]{1,0:T(8,128)(2,1)S(1)}, u32[]{:S(2)}, u32[]{:S(2)}) %collective-permute-start.12) | collective-permute-done | bytes 32800 | tf_op jit(solution)/shard_map/ppermute | solution.py:23
  47.0 1.2 %collective-permute-done.13 = bf16[128,128]{1,0:T(8,128)(2,1)S(1)} collective-permute-done((bf16[128,128]{1,0:T(8,128)(2,1)S(1)}, bf16[128,128]{1,0:T(8,128)(2,1)S(1)}, u32[]{:S(2)}, u32[]{:S(2)}) %collective-permute-start.13) | collective-permute-done | bytes 32800 | tf_op jit(solution)/shard_map/ppermute | solution.py:23
  48.2 0.8 %collective-permute-done.14 = bf16[128,128]{1,0:T(8,128)(2,1)S(1)} collective-permute-done((bf16[128,128]{1,0:T(8,128)(2,1)S(1)}, bf16[128,128]{1,0:T(8,128)(2,1)S(1)}, u32[]{:S(2)}, u32[]{:S(2)}) %collective-permute-start.14) | collective-permute-done | bytes 32800 | tf_op jit(solution)/shard_map/ppermute | solution.py:23
  49.0 0.1 collective-permute-start.15
  49.1 1.2 %collective-permute-done.15.refs_1_ = f32[128,128]{1,0:T(8,128)S(1)} collective-permute-done((f32[128,128]{1,0:T(8,128)S(1)}, f32[128,128]{1,0:T(8,128)S(1)}, u32[]{:S(2)}, u32[]{:S(2)}) %collective-permute-start.15) | collective-permute-done | bytes 65568 | tf_op jit(solution)/shard_map/ppermute | solution.py:23
  50.4 0.4 gram_terms.1
  50.7 2.4 %collective-permute-start.16 = (f32[32,128]{1,0:T(8,128)S(1)}, f32[32,128]{1,0:T(8,128)S(1)}, u32[]{:S(2)}, u32[]{:S(2)}) collective-permute-start(f32[32,128]{1,0:T(8,128)S(1)} %get-tuple-element.20.refs_0_), channel_id=1, source_target_pairs={{0,6},{1,7},{2,4},{3,5},{4,2},{5,3},{6,0},{7,1},{8,14},{9,15},{10,... | collective-permute-start | bytes 49160 | tf_op jit(solution)/shard_map/ppermute | solution.py:23
  53.1 0.0 collective-permute-start.17
  53.1 2.0 %collective-permute-start.18 = (f32[32,128]{1,0:T(8,128)S(1)}, f32[32,128]{1,0:T(8,128)S(1)}, u32[]{:S(2)}, u32[]{:S(2)}) collective-permute-start(f32[32,128]{1,0:T(8,128)S(1)} %get-tuple-element.20.refs_0_), channel_id=1, source_target_pairs={{0,2},{1,3},{2,0},{3,1},{4,6},{5,7},{6,4},{7,5},{8,10},{9,11},{10,... | collective-permute-start | bytes 49160 | tf_op jit(solution)/shard_map/ppermute | solution.py:23
  55.2 1.1 %collective-permute-done.16.refs_1_ = f32[32,128]{1,0:T(8,128)S(1)} collective-permute-done((f32[32,128]{1,0:T(8,128)S(1)}, f32[32,128]{1,0:T(8,128)S(1)}, u32[]{:S(2)}, u32[]{:S(2)}) %collective-permute-start.16) | collective-permute-done | bytes 16416 | tf_op jit(solution)/shard_map/ppermute | solution.py:23
  56.3 1.5 %collective-permute-done.17.refs_2_ = f32[32,128]{1,0:T(8,128)S(1)} collective-permute-done((f32[32,128]{1,0:T(8,128)S(1)}, f32[32,128]{1,0:T(8,128)S(1)}, u32[]{:S(2)}, u32[]{:S(2)}) %collective-permute-start.17) | collective-permute-done | bytes 16416 | tf_op jit(solution)/shard_map/ppermute | solution.py:23
  57.8 0.0 collective-permute-done.18.refs_3_
  57.8 0.9 %finish.1 = (f32[2,4096]{1,0:T(2,128)}, f32[64,64]{1,0:T(8,128)}) custom-call(f32[32,128]{1,0:T(8,128)S(1)} %get-tuple-element.20.refs_0_, f32[32,128]{1,0:T(8,128)S(1)} %collective-permute-done.16.refs_1_, f32[32,128]{1,0:T(8,128)S(1)} %collective-permute-done.17.refs_2_, f32[32,128]{1,0:T(8,128)S(1)} %collective-permute-done.18.refs_3_, ...), custom_call_target="tpu_custom_call" | custom-call | tf_op jit(solution)/shard_map/finish/pallas_call | solution.py:347
  (11 shorter events, 0.2 us)
Async XLA Ops:
  0.6 19.8 %copy-start = (bf16[2,4096]{1,0:T(2,128)(2,1)S(1)}, bf16[2,4096]{1,0:T(2,128)(2,1)}, u32[]{:S(2)}) copy-start(bf16[2,4096]{1,0:T(2,128)(2,1)} %param.11) | copy-start | bytes 49156
  1.4 7.3 %collective-permute-start = (bf16[4,4096]{1,0:T(4,128)(2,1)S(1)}, bf16[4,4096]{1,0:T(4,128)(2,1)S(1)}, u32[]{:S(2)}, u32[]{:S(2)}) collective-permute-start(bf16[4,4096]{1,0:T(4,128)(2,1)S(1)} %get-tuple-element.29), channel_id=1, source_target_pairs={{0,6},{1,7},{2,4},{3,5},{4,2},{5,3},{6,0},{7,1},{8,14},{9,15},{10,... | collective-permute-start | bytes 98312 | tf_op jit(solution)/shard_map/ppermute | solution.py:23
  6.5 4.8 %collective-permute-start.1 = (bf16[4,4096]{1,0:T(4,128)(2,1)S(1)}, bf16[4,4096]{1,0:T(4,128)(2,1)S(1)}, u32[]{:S(2)}, u32[]{:S(2)}) collective-permute-start(bf16[4,4096]{1,0:T(4,128)(2,1)S(1)} %get-tuple-element.29), channel_id=1, source_target_pairs={{0,4},{1,5},{2,6},{3,7},{4,0},{5,1},{6,2},{7,3},{8,12},{9,13},{10,... | collective-permute-start | bytes 98312 | tf_op jit(solution)/shard_map/ppermute | solution.py:23
  6.5 4.8 %collective-permute-start.2 = (bf16[4,4096]{1,0:T(4,128)(2,1)S(1)}, bf16[4,4096]{1,0:T(4,128)(2,1)S(1)}, u32[]{:S(2)}, u32[]{:S(2)}) collective-permute-start(bf16[4,4096]{1,0:T(4,128)(2,1)S(1)} %get-tuple-element.29), channel_id=1, source_target_pairs={{0,2},{1,3},{2,0},{3,1},{4,6},{5,7},{6,4},{7,5},{8,10},{9,11},{10,... | collective-permute-start | bytes 98312 | tf_op jit(solution)/shard_map/ppermute | solution.py:23
  11.5 1.4 %collective-permute-start.3 = (bf16[4,4,4096]{2,1,0:T(4,128)(2,1)S(1)}, bf16[4,4,4096]{2,1,0:T(4,128)(2,1)S(1)}, u32[]{:S(2)}, u32[]{:S(2)}) collective-permute-start(bf16[4,4,4096]{2,1,0:T(4,128)(2,1)S(1)} %pad_maximum_fusion.1.refs_2_), channel_id=1, source_target_pairs={{0,1},{1,0},{2,3},{3,2},{4,5},{5,4},{6,7},{7,6},{8,9},{9,8},{10,11... | collective-permute-start | bytes 393224 | tf_op jit(solution)/shard_map/ppermute | solution.py:23
  17.4 8.9 %collective-permute-start.4 = (bf16[64,2048]{1,0:T(8,128)(2,1)S(1)}, bf16[64,2048]{1,0:T(8,128)(2,1)S(1)}, u32[]{:S(2)}, u32[]{:S(2)}) collective-permute-start(bf16[64,2048]{1,0:T(8,128)(2,1)S(1)} %get-tuple-element.14), channel_id=1, source_target_pairs={{0,8},{1,17},{2,10},{3,19},{4,12},{5,21},{6,14},{7,23},{8,0},{9,25... | collective-permute-start | bytes 786440 | tf_op jit(solution)/shard_map/ppermute | solution.py:398
  18.9 7.4 %collective-permute-start.6 = (bf16[64,2048]{1,0:T(8,128)(2,1)S(1)}, bf16[64,2048]{1,0:T(8,128)(2,1)S(1)}, u32[]{:S(2)}, u32[]{:S(2)}) collective-permute-start(bf16[64,2048]{1,0:T(8,128)(2,1)S(1)} %get-tuple-element.16), channel_id=1, source_target_pairs={{0,16},{1,9},{2,18},{3,11},{4,20},{5,13},{6,22},{7,15},{8,24},{9,1... | collective-permute-start | bytes 786440 | tf_op jit(solution)/shard_map/ppermute | solution.py:398
  26.6 6.5 %collective-permute-start.8 = (bf16[64,1152]{1,0:T(8,128)(2,1)S(1)}, bf16[64,1152]{1,0:T(8,128)(2,1)S(1)}, u32[]{:S(2)}, u32[]{:S(2)}) collective-permute-start(bf16[64,1152]{1,0:T(8,128)(2,1)S(1)} %pad_maximum_fusion), channel_id=1, source_target_pairs={{0,1},{1,0},{2,3},{3,2},{4,5},{5,4},{6,7},{7,6},{8,9},{9,8},{10,11... | collective-permute-start | bytes 442376 | tf_op jit(solution)/shard_map/ppermute | solution.py:23
  26.7 5.8 %collective-permute-start.5 = (bf16[64,1024]{1,0:T(8,128)(2,1)S(1)}, bf16[64,1024]{1,0:T(8,128)(2,1)S(1)}, u32[]{:S(2)}, u32[]{:S(2)}) collective-permute-start(bf16[64,1024]{1,0:T(8,128)(2,1)S(1)} %get-tuple-element.24), channel_id=1, source_target_pairs={{0,16},{1,9},{2,18},{3,11},{4,20},{5,13},{6,22},{7,15},{8,24},{9,1... | collective-permute-start | bytes 393224 | tf_op jit(solution)/shard_map/ppermute | solution.py:398
  28.0 5.1 %collective-permute-start.7 = (bf16[64,1024]{1,0:T(8,128)(2,1)S(1)}, bf16[64,1024]{1,0:T(8,128)(2,1)S(1)}, u32[]{:S(2)}, u32[]{:S(2)}) collective-permute-start(bf16[64,1024]{1,0:T(8,128)(2,1)S(1)} %get-tuple-element.26), channel_id=1, source_target_pairs={{0,9},{1,16},{2,11},{3,18},{4,13},{5,20},{6,15},{7,22},{8,1},{9,24... | collective-permute-start | bytes 393224 | tf_op jit(solution)/shard_map/ppermute | solution.py:398
  33.5 5.8 %collective-permute-start.10 = (bf16[64,512]{1,0:T(8,128)(2,1)S(1)}, bf16[64,512]{1,0:T(8,128)(2,1)S(1)}, u32[]{:S(2)}, u32[]{:S(2)}) collective-permute-start(bf16[64,512]{1,0:T(8,128)(2,1)S(1)} %get-tuple-element.19.refs_0_), channel_id=1, source_target_pairs={{0,4},{1,5},{2,6},{3,7},{4,0},{5,1},{6,2},{7,3},{8,12},{9,13},{10,... | collective-permute-start | bytes 196616 | tf_op jit(solution)/shard_map/ppermute | solution.py:23
  35.6 6.2 %collective-permute-start.11 = (bf16[64,512]{1,0:T(8,128)(2,1)S(1)}, bf16[64,512]{1,0:T(8,128)(2,1)S(1)}, u32[]{:S(2)}, u32[]{:S(2)}) collective-permute-start(bf16[64,512]{1,0:T(8,128)(2,1)S(1)} %get-tuple-element.19.refs_0_), channel_id=1, source_target_pairs={{0,2},{1,3},{2,0},{3,1},{4,6},{5,7},{6,4},{7,5},{8,10},{9,11},{10,... | collective-permute-start | bytes 196616 | tf_op jit(solution)/shard_map/ppermute | solution.py:23
  35.6 6.2 %collective-permute-start.9 = (bf16[64,512]{1,0:T(8,128)(2,1)S(1)}, bf16[64,512]{1,0:T(8,128)(2,1)S(1)}, u32[]{:S(2)}, u32[]{:S(2)}) collective-permute-start(bf16[64,512]{1,0:T(8,128)(2,1)S(1)} %get-tuple-element.19.refs_0_), channel_id=1, source_target_pairs={{0,6},{1,7},{2,4},{3,5},{4,2},{5,3},{6,0},{7,1},{8,14},{9,15},{10,... | collective-permute-start | bytes 196616 | tf_op jit(solution)/shard_map/ppermute | solution.py:23
  42.1 4.9 %collective-permute-start.12 = (bf16[128,128]{1,0:T(8,128)(2,1)S(1)}, bf16[128,128]{1,0:T(8,128)(2,1)S(1)}, u32[]{:S(2)}, u32[]{:S(2)}) collective-permute-start(bf16[128,128]{1,0:T(8,128)(2,1)S(1)} %row_terms.1), channel_id=1, source_target_pairs={{0,24},{8,16},{16,8},{24,0},{1,25},{9,17},{17,9},{25,1},{2,26},{10... | collective-permute-start | bytes 98312 | tf_op jit(solution)/shard_map/ppermute | solution.py:23
  44.3 3.9 %collective-permute-start.13 = (bf16[128,128]{1,0:T(8,128)(2,1)S(1)}, bf16[128,128]{1,0:T(8,128)(2,1)S(1)}, u32[]{:S(2)}, u32[]{:S(2)}) collective-permute-start(bf16[128,128]{1,0:T(8,128)(2,1)S(1)} %row_terms.1), channel_id=1, source_target_pairs={{0,16},{8,24},{16,0},{24,8},{1,17},{9,25},{17,1},{25,9},{2,18},{10... | collective-permute-start | bytes 98312 | tf_op jit(solution)/shard_map/ppermute | solution.py:23
  45.1 3.9 %collective-permute-start.14 = (bf16[128,128]{1,0:T(8,128)(2,1)S(1)}, bf16[128,128]{1,0:T(8,128)(2,1)S(1)}, u32[]{:S(2)}, u32[]{:S(2)}) collective-permute-start(bf16[128,128]{1,0:T(8,128)(2,1)S(1)} %row_terms.1), channel_id=1, source_target_pairs={{0,8},{8,0},{16,24},{24,16},{1,9},{9,1},{17,25},{25,17},{2,10},{10... | collective-permute-start | bytes 98312 | tf_op jit(solution)/shard_map/ppermute | solution.py:23
  49.0 1.3 %collective-permute-start.15 = (f32[128,128]{1,0:T(8,128)S(1)}, f32[128,128]{1,0:T(8,128)S(1)}, u32[]{:S(2)}, u32[]{:S(2)}) collective-permute-start(f32[128,128]{1,0:T(8,128)S(1)} %convert_add_fusion.refs_0_), channel_id=1, source_target_pairs={{0,1},{1,0},{2,3},{3,2},{4,5},{5,4},{6,7},{7,6},{8,9},{9,8},{10,11... | collective-permute-start | bytes 196616 | tf_op jit(solution)/shard_map/ppermute | solution.py:23
  50.7 5.6 %collective-permute-start.16 = (f32[32,128]{1,0:T(8,128)S(1)}, f32[32,128]{1,0:T(8,128)S(1)}, u32[]{:S(2)}, u32[]{:S(2)}) collective-permute-start(f32[32,128]{1,0:T(8,128)S(1)} %get-tuple-element.20.refs_0_), channel_id=1, source_target_pairs={{0,6},{1,7},{2,4},{3,5},{4,2},{5,3},{6,0},{7,1},{8,14},{9,15},{10,... | collective-permute-start | bytes 49160 | tf_op jit(solution)/shard_map/ppermute | solution.py:23
  53.1 4.6 %collective-permute-start.17 = (f32[32,128]{1,0:T(8,128)S(1)}, f32[32,128]{1,0:T(8,128)S(1)}, u32[]{:S(2)}, u32[]{:S(2)}) collective-permute-start(f32[32,128]{1,0:T(8,128)S(1)} %get-tuple-element.20.refs_0_), channel_id=1, source_target_pairs={{0,4},{1,5},{2,6},{3,7},{4,0},{5,1},{6,2},{7,3},{8,12},{9,13},{10,... | collective-permute-start | bytes 49160 | tf_op jit(solution)/shard_map/ppermute | solution.py:23
  53.1 4.6 %collective-permute-start.18 = (f32[32,128]{1,0:T(8,128)S(1)}, f32[32,128]{1,0:T(8,128)S(1)}, u32[]{:S(2)}, u32[]{:S(2)}) collective-permute-start(f32[32,128]{1,0:T(8,128)S(1)} %get-tuple-element.20.refs_0_), channel_id=1, source_target_pairs={{0,2},{1,3},{2,0},{3,1},{4,6},{5,7},{6,4},{7,5},{8,10},{9,11},{10,... | collective-permute-start | bytes 49160 | tf_op jit(solution)/shard_map/ppermute | solution.py:23

commit v5 on v4

--- a/solution.py
+++ b/solution.py
@@ -21,6 +21,11 @@
 
 def swap(x, axis, size, mask):
     return lax.ppermute(x, axis, [(i, partner(i, mask, size)) for i in range(size)])
+
+
+def far_masks(size):
+    masks = list(range(2, size, 2))
+    return masks[1:2] + masks[:1] + masks[2:]
 
 
 def is_direct(size):
@@ -71,7 +76,9 @@
 
     def factor_rows(p, which):
         owner = (p // row_blocks) ^ me
-        turn = (per_core - owner // split) % per_core if split > 1 else owner
+        turn = owner
+        if split > 1:
+            turn = sum(jnp.where(owner // 2 == m // 2, i + 1, 0) for i, m in enumerate(far_masks(per_core * 2)))
         row = (owner % split * per_core + turn) * per_owner + which * row_blocks + p % row_blocks
         parts = []
         for k in range(edge // tile):
@@ -416,7 +423,7 @@
     n_grp, n_dev = lax.axis_size("grp"), lax.axis_size("dev")
     direct = is_direct(n_dev)
     split = 2 if direct else 1
-    far = range(n_dev - 2, 0, -2)
+    far = far_masks(n_dev)
 
     def sibling(x):
         return swap(x, "dev", n_dev, 1)

time: 58.9 us -> 61.4 us (1.042)
  waiting for transfers between devices: 25.1 us -> 28.6 us
  starting transfers between devices: 23.3 us -> 22.3 us
    ppermute x15, waiting for transfers between devices: 14.9 us -> 18.4 us  [swap(): lax.ppermute(x, axis, [(i, partner(i, mask, size)) for i in range(size)])]
    ppermute x15, starting transfers between devices: 18.5 us -> 17.5 us  [swap(): lax.ppermute(x, axis, [(i, partner(i, mask, size)) for i in range(size)])]
  transfers between devices with their start and end apart: 19 -> 19, of which waited for: 13 -> 15; matrix products, arithmetic and copies ran while one was open for 2% -> 2% of each run, Pallas kernels for 0% -> 0%
where the time goes in v5:
time: 61.4 us; the launch traced here: 61.1 us
  waiting for transfers between devices  28.6 us (47%)
  starting transfers between devices  22.3 us (36%)
  Pallas kernels  6.44 us (10%)
  other arithmetic  2.13 us (3%)
  between operations  1.43 us (2%)
    ppermute x15, waiting for transfers between devices, swap(): lax.ppermute(x, axis, [(i, partner(i, mask, size)) for i in range(size)])  18.4 us
    ppermute x15, starting transfers between devices, swap(): lax.ppermute(x, axis, [(i, partner(i, mask, size)) for i in range(size)])  17.5 us
    ppermute x4, waiting for transfers between devices, send(): return lax.ppermute(x, ('grp', 'dev'), pairs)  10.2 us
    ppermute x4, starting transfers between devices, send(): return lax.ppermute(x, ('grp', 'dev'), pairs)  4.86 us
    pallas_call x1, Pallas kernels, contract(): pl.pallas_call(functools.partial(contract_kernel, n_tables=len(tables), n...  4.49 us
  transfers between devices with their start and end apart: 19, of which 15 were waited for; matrix products, arithmetic and copies ran while one was open for 2% of the time, Pallas kernels for 0%

profile of v5, /device:TPU:0, one launch (start us, length us, event | category | flops | bytes accessed | tf_op | source)
XLA Modules:
  0.0 61.1 jit_solution(7134969649984467706)
XLA Ops:
  0.6 0.8 %fusion.7 = (bf16[1,4,4096]{2,1,0:T(4,128)(2,1)S(1)}, bf16[4,4096]{1,0:T(4,128)(2,1)S(1)}) fusion(bf16[2,4096]{1,0:T(2,128)(2,1)} %param.13, bf16[2,4096]{1,0:T(2,128)(2,1)} %param.12), kind=kLoop, calls=%fused_computation.23 | loop fusion | flops 65536 | bytes 98304 | tf_op jit(solution)/shard_map/stack | solution.py:436
  1.4 4.1 %collective-permute-start = (bf16[4,4096]{1,0:T(4,128)(2,1)S(1)}, bf16[4,4096]{1,0:T(4,128)(2,1)S(1)}, u32[]{:S(2)}, u32[]{:S(2)}) collective-permute-start(bf16[4,4096]{1,0:T(4,128)(2,1)S(1)} %get-tuple-element.29), channel_id=1, source_target_pairs={{0,4},{1,5},{2,6},{3,7},{4,0},{5,1},{6,2},{7,3},{8,12},{9,13},{10,... | collective-permute-start | bytes 98312 | tf_op jit(solution)/shard_map/ppermute | solution.py:23
  5.5 1.6 %collective-permute-start.1 = (bf16[4,4096]{1,0:T(4,128)(2,1)S(1)}, bf16[4,4096]{1,0:T(4,128)(2,1)S(1)}, u32[]{:S(2)}, u32[]{:S(2)}) collective-permute-start(bf16[4,4096]{1,0:T(4,128)(2,1)S(1)} %get-tuple-element.29), channel_id=1, source_target_pairs={{0,2},{1,3},{2,0},{3,1},{4,6},{5,7},{6,4},{7,5},{8,10},{9,11},{10,... | collective-permute-start | bytes 98312 | tf_op jit(solution)/shard_map/ppermute | solution.py:23
  7.8 0.9 %select_reduce_fusion = s32[3,8]{1,0:T(4,128)S(1)} fusion(s32[16]{0:T(128)} %param.10, s32[3,8]{1,0:T(4,128)} %param.8), kind=kLoop, calls=%fused_computation.13 | loop fusion | flops 1128 | bytes 256 | tf_op jit(solution)/shard_map/reduce_sum | solution.py:441
  8.7 0.0 collective-permute-done
  8.7 0.7 %collective-permute-done.1 = bf16[4,4096]{1,0:T(4,128)(2,1)S(1)} collective-permute-done((bf16[4,4096]{1,0:T(4,128)(2,1)S(1)}, bf16[4,4096]{1,0:T(4,128)(2,1)S(1)}, u32[]{:S(2)}, u32[]{:S(2)}) %collective-permute-start.1) | collective-permute-done | bytes 32800 | tf_op jit(solution)/shard_map/ppermute | solution.py:23
  9.4 3.4 %collective-permute-done.2 = bf16[4,4096]{1,0:T(4,128)(2,1)S(1)} collective-permute-done((bf16[4,4096]{1,0:T(4,128)(2,1)S(1)}, bf16[4,4096]{1,0:T(4,128)(2,1)S(1)}, u32[]{:S(2)}, u32[]{:S(2)}) %collective-permute-start.2) | collective-permute-done | bytes 32800 | tf_op jit(solution)/shard_map/ppermute | solution.py:23
  12.8 0.1 pad_maximum_fusion.1.refs_2_
  12.9 0.1 collective-permute-start.3
  13.0 0.1 fusion.6.refs_0_
  13.1 1.3 %collective-permute-done.3.refs_3_ = bf16[4,4,4096]{2,1,0:T(4,128)(2,1)S(1)} collective-permute-done((bf16[4,4,4096]{2,1,0:T(4,128)(2,1)S(1)}, bf16[4,4,4096]{2,1,0:T(4,128)(2,1)S(1)}, u32[]{:S(2)}, u32[]{:S(2)}) %collective-permute-start.3) | collective-permute-done | bytes 131104 | tf_op jit(solution)/shard_map/ppermute | solution.py:23
  14.3 4.5 %contract.1 = (bf16[64,2048]{1,0:T(8,128)(2,1)S(1)}, bf16[64,2048]{1,0:T(8,128)(2,1)S(1)}, bf16[64,1024]{1,0:T(8,128)(2,1)S(1)}, bf16[64,3072]{1,0:T(8,128)(2,1)S(1)}) custom-call(s32[3,8]{1,0:T(4,128)S(1)} %fusion.6.refs_0_, bf16[8,64,4096]{2,1,0:T(8,128)(2,1)} %refs_1_.1, bf16[4,4,4096]{2,1,0:T(4,128)(2,1)S(1)} %pad_maximum_fusion.1.refs_2_, ...), custom_call_target="tpu_custom_call" | custom-call | flops 1610612736 | bytes 6291456 | tf_op jit(solution)/shard_map/contract/pallas_call | solution.py:185
  18.8 1.6 %collective-permute-start.4 = (bf16[64,2048]{1,0:T(8,128)(2,1)S(1)}, bf16[64,2048]{1,0:T(8,128)(2,1)S(1)}, u32[]{:S(2)}, u32[]{:S(2)}) collective-permute-start(bf16[64,2048]{1,0:T(8,128)(2,1)S(1)} %get-tuple-element.14), channel_id=1, source_target_pairs={{0,8},{1,17},{2,10},{3,19},{4,12},{5,21},{6,14},{7,23},{8,0},{9,25... | collective-permute-start | bytes 786440 | tf_op jit(solution)/shard_map/ppermute | solution.py:405
  20.4 1.5 %collective-permute-start.6 = (bf16[64,2048]{1,0:T(8,128)(2,1)S(1)}, bf16[64,2048]{1,0:T(8,128)(2,1)S(1)}, u32[]{:S(2)}, u32[]{:S(2)}) collective-permute-start(bf16[64,2048]{1,0:T(8,128)(2,1)S(1)} %get-tuple-element.16), channel_id=1, source_target_pairs={{0,16},{1,9},{2,18},{3,11},{4,20},{5,13},{6,22},{7,15},{8,24},{9,1... | collective-permute-start | bytes 786440 | tf_op jit(solution)/shard_map/ppermute | solution.py:405
  21.9 0.1 reshape.22
  22.1 0.1 reshape.23.refs_4_
  22.2 5.6 %collective-permute-done.4 = bf16[64,2048]{1,0:T(8,128)(2,1)S(1)} collective-permute-done((bf16[64,2048]{1,0:T(8,128)(2,1)S(1)}, bf16[64,2048]{1,0:T(8,128)(2,1)S(1)}, u32[]{:S(2)}, u32[]{:S(2)}) %collective-permute-start.4) | collective-permute-done | bytes 262176 | tf_op jit(solution)/shard_map/ppermute | solution.py:405
  27.8 0.0 collective-permute-done.6
  27.8 0.1 fusion.2
  28.0 0.2 collective-permute-start.8
  28.2 1.2 %collective-permute-start.5 = (bf16[64,1024]{1,0:T(8,128)(2,1)S(1)}, bf16[64,1024]{1,0:T(8,128)(2,1)S(1)}, u32[]{:S(2)}, u32[]{:S(2)}) collective-permute-start(bf16[64,1024]{1,0:T(8,128)(2,1)S(1)} %get-tuple-element.24), channel_id=1, source_target_pairs={{0,16},{1,9},{2,18},{3,11},{4,20},{5,13},{6,22},{7,15},{8,24},{9,1... | collective-permute-start | bytes 393224 | tf_op jit(solution)/shard_map/ppermute | solution.py:405
  29.4 0.5 collective-permute-start.7
  29.9 4.0 %collective-permute-done.5.refs_1_ = bf16[64,1024]{1,0:T(8,128)(2,1)S(1)} collective-permute-done((bf16[64,1024]{1,0:T(8,128)(2,1)S(1)}, bf16[64,1024]{1,0:T(8,128)(2,1)S(1)}, u32[]{:S(2)}, u32[]{:S(2)}) %collective-permute-start.5) | collective-permute-done | bytes 131104 | tf_op jit(solution)/shard_map/ppermute | solution.py:405
  33.9 0.6 %collective-permute-done.7.refs_2_ = bf16[64,1024]{1,0:T(8,128)(2,1)S(1)} collective-permute-done((bf16[64,1024]{1,0:T(8,128)(2,1)S(1)}, bf16[64,1024]{1,0:T(8,128)(2,1)S(1)}, u32[]{:S(2)}, u32[]{:S(2)}) %collective-permute-start.7) | collective-permute-done | bytes 131104 | tf_op jit(solution)/shard_map/ppermute | solution.py:405
  34.6 0.0 collective-permute-done.8.refs_3_.refs_5_
  34.6 0.4 project.1
  35.0 0.1 collective-permute-start.10
  35.0 0.4 collective-permute-start.11
  35.5 3.0 %collective-permute-start.9 = (bf16[64,512]{1,0:T(8,128)(2,1)S(1)}, bf16[64,512]{1,0:T(8,128)(2,1)S(1)}, u32[]{:S(2)}, u32[]{:S(2)}) collective-permute-start(bf16[64,512]{1,0:T(8,128)(2,1)S(1)} %get-tuple-element.19.refs_0_), channel_id=1, source_target_pairs={{0,4},{1,5},{2,6},{3,7},{4,0},{5,1},{6,2},{7,3},{8,12},{9,13},{10,... | collective-permute-start | bytes 196616 | tf_op jit(solution)/shard_map/ppermute | solution.py:23
  38.5 0.8 %collective-permute-done.10.refs_2_ = bf16[64,512]{1,0:T(8,128)(2,1)S(1)} collective-permute-done((bf16[64,512]{1,0:T(8,128)(2,1)S(1)}, bf16[64,512]{1,0:T(8,128)(2,1)S(1)}, u32[]{:S(2)}, u32[]{:S(2)}) %collective-permute-start.10) | collective-permute-done | bytes 65568 | tf_op jit(solution)/shard_map/ppermute | solution.py:23
  39.3 2.4 %collective-permute-done.11.refs_3_ = bf16[64,512]{1,0:T(8,128)(2,1)S(1)} collective-permute-done((bf16[64,512]{1,0:T(8,128)(2,1)S(1)}, bf16[64,512]{1,0:T(8,128)(2,1)S(1)}, u32[]{:S(2)}, u32[]{:S(2)}) %collective-permute-start.11) | collective-permute-done | bytes 65568 | tf_op jit(solution)/shard_map/ppermute | solution.py:23
  41.6 2.7 %collective-permute-done.9.refs_1_ = bf16[64,512]{1,0:T(8,128)(2,1)S(1)} collective-permute-done((bf16[64,512]{1,0:T(8,128)(2,1)S(1)}, bf16[64,512]{1,0:T(8,128)(2,1)S(1)}, u32[]{:S(2)}, u32[]{:S(2)}) %collective-permute-start.9) | collective-permute-done | bytes 65568 | tf_op jit(solution)/shard_map/ppermute | solution.py:23
  44.4 0.3 row_terms.1
  44.7 1.9 %collective-permute-start.12 = (bf16[128,128]{1,0:T(8,128)(2,1)S(1)}, bf16[128,128]{1,0:T(8,128)(2,1)S(1)}, u32[]{:S(2)}, u32[]{:S(2)}) collective-permute-start(bf16[128,128]{1,0:T(8,128)(2,1)S(1)} %row_terms.1), channel_id=1, source_target_pairs={{0,24},{8,16},{16,8},{24,0},{1,25},{9,17},{17,9},{25,1},{2,26},{10... | collective-permute-start | bytes 98312 | tf_op jit(solution)/shard_map/ppermute | solution.py:23
  46.5 0.8 %collective-permute-start.13 = (bf16[128,128]{1,0:T(8,128)(2,1)S(1)}, bf16[128,128]{1,0:T(8,128)(2,1)S(1)}, u32[]{:S(2)}, u32[]{:S(2)}) collective-permute-start(bf16[128,128]{1,0:T(8,128)(2,1)S(1)} %row_terms.1), channel_id=1, source_target_pairs={{0,16},{8,24},{16,0},{24,8},{1,17},{9,25},{17,1},{25,9},{2,18},{10... | collective-permute-start | bytes 98312 | tf_op jit(solution)/shard_map/ppermute | solution.py:23
  47.3 0.9 %collective-permute-start.14 = (bf16[128,128]{1,0:T(8,128)(2,1)S(1)}, bf16[128,128]{1,0:T(8,128)(2,1)S(1)}, u32[]{:S(2)}, u32[]{:S(2)}) collective-permute-start(bf16[128,128]{1,0:T(8,128)(2,1)S(1)} %row_terms.1), channel_id=1, source_target_pairs={{0,8},{8,0},{16,24},{24,16},{1,9},{9,1},{17,25},{25,17},{2,10},{10... | collective-permute-start | bytes 98312 | tf_op jit(solution)/shard_map/ppermute | solution.py:23
  48.2 1.5 %collective-permute-done.12 = bf16[128,128]{1,0:T(8,128)(2,1)S(1)} collective-permute-done((bf16[128,128]{1,0:T(8,128)(2,1)S(1)}, bf16[128,128]{1,0:T(8,128)(2,1)S(1)}, u32[]{:S(2)}, u32[]{:S(2)}) %collective-permute-start.12) | collective-permute-done | bytes 32800 | tf_op jit(solution)/shard_map/ppermute | solution.py:23
  49.7 0.8 %collective-permute-done.13 = bf16[128,128]{1,0:T(8,128)(2,1)S(1)} collective-permute-done((bf16[128,128]{1,0:T(8,128)(2,1)S(1)}, bf16[128,128]{1,0:T(8,128)(2,1)S(1)}, u32[]{:S(2)}, u32[]{:S(2)}) %collective-permute-start.13) | collective-permute-done | bytes 32800 | tf_op jit(solution)/shard_map/ppermute | solution.py:23
  50.5 0.8 %collective-permute-done.14 = bf16[128,128]{1,0:T(8,128)(2,1)S(1)} collective-permute-done((bf16[128,128]{1,0:T(8,128)(2,1)S(1)}, bf16[128,128]{1,0:T(8,128)(2,1)S(1)}, u32[]{:S(2)}, u32[]{:S(2)}) %collective-permute-start.14) | collective-permute-done | bytes 32800 | tf_op jit(solution)/shard_map/ppermute | solution.py:23
  51.2 0.1 collective-permute-start.15
  51.3 1.2 %collective-permute-done.15.refs_1_ = f32[128,128]{1,0:T(8,128)S(1)} collective-permute-done((f32[128,128]{1,0:T(8,128)S(1)}, f32[128,128]{1,0:T(8,128)S(1)}, u32[]{:S(2)}, u32[]{:S(2)}) %collective-permute-start.15) | collective-permute-done | bytes 65568 | tf_op jit(solution)/shard_map/ppermute | solution.py:23
  52.6 0.4 gram_terms.1
  53.0 0.0 collective-permute-start.16
  53.0 1.7 %collective-permute-start.17 = (f32[32,128]{1,0:T(8,128)S(1)}, f32[32,128]{1,0:T(8,128)S(1)}, u32[]{:S(2)}, u32[]{:S(2)}) collective-permute-start(f32[32,128]{1,0:T(8,128)S(1)} %get-tuple-element.20.refs_0_), channel_id=1, source_target_pairs={{0,2},{1,3},{2,0},{3,1},{4,6},{5,7},{6,4},{7,5},{8,10},{9,11},{10,... | collective-permute-start | bytes 49160 | tf_op jit(solution)/shard_map/ppermute | solution.py:23
  54.7 2.6 %collective-permute-start.18 = (f32[32,128]{1,0:T(8,128)S(1)}, f32[32,128]{1,0:T(8,128)S(1)}, u32[]{:S(2)}, u32[]{:S(2)}) collective-permute-start(f32[32,128]{1,0:T(8,128)S(1)} %get-tuple-element.20.refs_0_), channel_id=1, source_target_pairs={{0,6},{1,7},{2,4},{3,5},{4,2},{5,3},{6,0},{7,1},{8,14},{9,15},{10,... | collective-permute-start | bytes 49160 | tf_op jit(solution)/shard_map/ppermute | solution.py:23
  57.4 0.2 collective-permute-done.16.refs_1_
  57.6 2.6 %collective-permute-done.18.refs_3_ = f32[32,128]{1,0:T(8,128)S(1)} collective-permute-done((f32[32,128]{1,0:T(8,128)S(1)}, f32[32,128]{1,0:T(8,128)S(1)}, u32[]{:S(2)}, u32[]{:S(2)}) %collective-permute-start.18) | collective-permute-done | bytes 16416 | tf_op jit(solution)/shard_map/ppermute | solution.py:23
  60.3 0.9 %finish.1 = (f32[2,4096]{1,0:T(2,128)}, f32[64,64]{1,0:T(8,128)}) custom-call(f32[32,128]{1,0:T(8,128)S(1)} %get-tuple-element.20.refs_0_, f32[32,128]{1,0:T(8,128)S(1)} %collective-permute-done.16.refs_1_, f32[32,128]{1,0:T(8,128)S(1)} %collective-permute-done.17.refs_2_, f32[32,128]{1,0:T(8,128)S(1)} %collective-permute-done.18.refs_3_, ...), custom_call_target="tpu_custom_call" | custom-call | tf_op jit(solution)/shard_map/finish/pallas_call | solution.py:354
  (11 shorter events, 0.2 us)
Async XLA Ops:
  0.6 21.3 %copy-start = (bf16[2,4096]{1,0:T(2,128)(2,1)S(1)}, bf16[2,4096]{1,0:T(2,128)(2,1)}, u32[]{:S(2)}) copy-start(bf16[2,4096]{1,0:T(2,128)(2,1)} %param.11) | copy-start | bytes 49156
  1.4 7.3 %collective-permute-start = (bf16[4,4096]{1,0:T(4,128)(2,1)S(1)}, bf16[4,4096]{1,0:T(4,128)(2,1)S(1)}, u32[]{:S(2)}, u32[]{:S(2)}) collective-permute-start(bf16[4,4096]{1,0:T(4,128)(2,1)S(1)} %get-tuple-element.29), channel_id=1, source_target_pairs={{0,4},{1,5},{2,6},{3,7},{4,0},{5,1},{6,2},{7,3},{8,12},{9,13},{10,... | collective-permute-start | bytes 98312 | tf_op jit(solution)/shard_map/ppermute | solution.py:23
  5.5 3.9 %collective-permute-start.1 = (bf16[4,4096]{1,0:T(4,128)(2,1)S(1)}, bf16[4,4096]{1,0:T(4,128)(2,1)S(1)}, u32[]{:S(2)}, u32[]{:S(2)}) collective-permute-start(bf16[4,4096]{1,0:T(4,128)(2,1)S(1)} %get-tuple-element.29), channel_id=1, source_target_pairs={{0,2},{1,3},{2,0},{3,1},{4,6},{5,7},{6,4},{7,5},{8,10},{9,11},{10,... | collective-permute-start | bytes 98312 | tf_op jit(solution)/shard_map/ppermute | solution.py:23
  7.1 5.7 %collective-permute-start.2 = (bf16[4,4096]{1,0:T(4,128)(2,1)S(1)}, bf16[4,4096]{1,0:T(4,128)(2,1)S(1)}, u32[]{:S(2)}, u32[]{:S(2)}) collective-permute-start(bf16[4,4096]{1,0:T(4,128)(2,1)S(1)} %get-tuple-element.29), channel_id=1, source_target_pairs={{0,6},{1,7},{2,4},{3,5},{4,2},{5,3},{6,0},{7,1},{8,14},{9,15},{10,... | collective-permute-start | bytes 98312 | tf_op jit(solution)/shard_map/ppermute | solution.py:23
  12.9 1.4 %collective-permute-start.3 = (bf16[4,4,4096]{2,1,0:T(4,128)(2,1)S(1)}, bf16[4,4,4096]{2,1,0:T(4,128)(2,1)S(1)}, u32[]{:S(2)}, u32[]{:S(2)}) collective-permute-start(bf16[4,4,4096]{2,1,0:T(4,128)(2,1)S(1)} %pad_maximum_fusion.1.refs_2_), channel_id=1, source_target_pairs={{0,1},{1,0},{2,3},{3,2},{4,5},{5,4},{6,7},{7,6},{8,9},{9,8},{10,11... | collective-permute-start | bytes 393224 | tf_op jit(solution)/shard_map/ppermute | solution.py:23
  18.8 8.9 %collective-permute-start.4 = (bf16[64,2048]{1,0:T(8,128)(2,1)S(1)}, bf16[64,2048]{1,0:T(8,128)(2,1)S(1)}, u32[]{:S(2)}, u32[]{:S(2)}) collective-permute-start(bf16[64,2048]{1,0:T(8,128)(2,1)S(1)} %get-tuple-element.14), channel_id=1, source_target_pairs={{0,8},{1,17},{2,10},{3,19},{4,12},{5,21},{6,14},{7,23},{8,0},{9,25... | collective-permute-start | bytes 786440 | tf_op jit(solution)/shard_map/ppermute | solution.py:405
  20.4 7.4 %collective-permute-start.6 = (bf16[64,2048]{1,0:T(8,128)(2,1)S(1)}, bf16[64,2048]{1,0:T(8,128)(2,1)S(1)}, u32[]{:S(2)}, u32[]{:S(2)}) collective-permute-start(bf16[64,2048]{1,0:T(8,128)(2,1)S(1)} %get-tuple-element.16), channel_id=1, source_target_pairs={{0,16},{1,9},{2,18},{3,11},{4,20},{5,13},{6,22},{7,15},{8,24},{9,1... | collective-permute-start | bytes 786440 | tf_op jit(solution)/shard_map/ppermute | solution.py:405
  28.0 6.5 %collective-permute-start.8 = (bf16[64,1152]{1,0:T(8,128)(2,1)S(1)}, bf16[64,1152]{1,0:T(8,128)(2,1)S(1)}, u32[]{:S(2)}, u32[]{:S(2)}) collective-permute-start(bf16[64,1152]{1,0:T(8,128)(2,1)S(1)} %pad_maximum_fusion), channel_id=1, source_target_pairs={{0,1},{1,0},{2,3},{3,2},{4,5},{5,4},{6,7},{7,6},{8,9},{9,8},{10,11... | collective-permute-start | bytes 442376 | tf_op jit(solution)/shard_map/ppermute | solution.py:23
  28.2 5.8 %collective-permute-start.5 = (bf16[64,1024]{1,0:T(8,128)(2,1)S(1)}, bf16[64,1024]{1,0:T(8,128)(2,1)S(1)}, u32[]{:S(2)}, u32[]{:S(2)}) collective-permute-start(bf16[64,1024]{1,0:T(8,128)(2,1)S(1)} %get-tuple-element.24), channel_id=1, source_target_pairs={{0,16},{1,9},{2,18},{3,11},{4,20},{5,13},{6,22},{7,15},{8,24},{9,1... | collective-permute-start | bytes 393224 | tf_op jit(solution)/shard_map/ppermute | solution.py:405
  29.4 5.1 %collective-permute-start.7 = (bf16[64,1024]{1,0:T(8,128)(2,1)S(1)}, bf16[64,1024]{1,0:T(8,128)(2,1)S(1)}, u32[]{:S(2)}, u32[]{:S(2)}) collective-permute-start(bf16[64,1024]{1,0:T(8,128)(2,1)S(1)} %get-tuple-element.26), channel_id=1, source_target_pairs={{0,9},{1,16},{2,11},{3,18},{4,13},{5,20},{6,15},{7,22},{8,1},{9,24... | collective-permute-start | bytes 393224 | tf_op jit(solution)/shard_map/ppermute | solution.py:405
  35.0 4.3 %collective-permute-start.10 = (bf16[64,512]{1,0:T(8,128)(2,1)S(1)}, bf16[64,512]{1,0:T(8,128)(2,1)S(1)}, u32[]{:S(2)}, u32[]{:S(2)}) collective-permute-start(bf16[64,512]{1,0:T(8,128)(2,1)S(1)} %get-tuple-element.19.refs_0_), channel_id=1, source_target_pairs={{0,2},{1,3},{2,0},{3,1},{4,6},{5,7},{6,4},{7,5},{8,10},{9,11},{10,... | collective-permute-start | bytes 196616 | tf_op jit(solution)/shard_map/ppermute | solution.py:23
  35.0 6.6 %collective-permute-start.11 = (bf16[64,512]{1,0:T(8,128)(2,1)S(1)}, bf16[64,512]{1,0:T(8,128)(2,1)S(1)}, u32[]{:S(2)}, u32[]{:S(2)}) collective-permute-start(bf16[64,512]{1,0:T(8,128)(2,1)S(1)} %get-tuple-element.19.refs_0_), channel_id=1, source_target_pairs={{0,6},{1,7},{2,4},{3,5},{4,2},{5,3},{6,0},{7,1},{8,14},{9,15},{10,... | collective-permute-start | bytes 196616 | tf_op jit(solution)/shard_map/ppermute | solution.py:23
  35.5 8.9 %collective-permute-start.9 = (bf16[64,512]{1,0:T(8,128)(2,1)S(1)}, bf16[64,512]{1,0:T(8,128)(2,1)S(1)}, u32[]{:S(2)}, u32[]{:S(2)}) collective-permute-start(bf16[64,512]{1,0:T(8,128)(2,1)S(1)} %get-tuple-element.19.refs_0_), channel_id=1, source_target_pairs={{0,4},{1,5},{2,6},{3,7},{4,0},{5,1},{6,2},{7,3},{8,12},{9,13},{10,... | collective-permute-start | bytes 196616 | tf_op jit(solution)/shard_map/ppermute | solution.py:23
  44.7 5.0 %collective-permute-start.12 = (bf16[128,128]{1,0:T(8,128)(2,1)S(1)}, bf16[128,128]{1,0:T(8,128)(2,1)S(1)}, u32[]{:S(2)}, u32[]{:S(2)}) collective-permute-start(bf16[128,128]{1,0:T(8,128)(2,1)S(1)} %row_terms.1), channel_id=1, source_target_pairs={{0,24},{8,16},{16,8},{24,0},{1,25},{9,17},{17,9},{25,1},{2,26},{10... | collective-permute-start | bytes 98312 | tf_op jit(solution)/shard_map/ppermute | solution.py:23
  46.5 3.9 %collective-permute-start.13 = (bf16[128,128]{1,0:T(8,128)(2,1)S(1)}, bf16[128,128]{1,0:T(8,128)(2,1)S(1)}, u32[]{:S(2)}, u32[]{:S(2)}) collective-permute-start(bf16[128,128]{1,0:T(8,128)(2,1)S(1)} %row_terms.1), channel_id=1, source_target_pairs={{0,16},{8,24},{16,0},{24,8},{1,17},{9,25},{17,1},{25,9},{2,18},{10... | collective-permute-start | bytes 98312 | tf_op jit(solution)/shard_map/ppermute | solution.py:23
  47.3 3.9 %collective-permute-start.14 = (bf16[128,128]{1,0:T(8,128)(2,1)S(1)}, bf16[128,128]{1,0:T(8,128)(2,1)S(1)}, u32[]{:S(2)}, u32[]{:S(2)}) collective-permute-start(bf16[128,128]{1,0:T(8,128)(2,1)S(1)} %row_terms.1), channel_id=1, source_target_pairs={{0,8},{8,0},{16,24},{24,16},{1,9},{9,1},{17,25},{25,17},{2,10},{10... | collective-permute-start | bytes 98312 | tf_op jit(solution)/shard_map/ppermute | solution.py:23
  51.2 1.3 %collective-permute-start.15 = (f32[128,128]{1,0:T(8,128)S(1)}, f32[128,128]{1,0:T(8,128)S(1)}, u32[]{:S(2)}, u32[]{:S(2)}) collective-permute-start(f32[128,128]{1,0:T(8,128)S(1)} %convert_add_fusion.refs_0_), channel_id=1, source_target_pairs={{0,1},{1,0},{2,3},{3,2},{4,5},{5,4},{6,7},{7,6},{8,9},{9,8},{10,11... | collective-permute-start | bytes 196616 | tf_op jit(solution)/shard_map/ppermute | solution.py:23
  53.0 4.7 %collective-permute-start.16 = (f32[32,128]{1,0:T(8,128)S(1)}, f32[32,128]{1,0:T(8,128)S(1)}, u32[]{:S(2)}, u32[]{:S(2)}) collective-permute-start(f32[32,128]{1,0:T(8,128)S(1)} %get-tuple-element.20.refs_0_), channel_id=1, source_target_pairs={{0,4},{1,5},{2,6},{3,7},{4,0},{5,1},{6,2},{7,3},{8,12},{9,13},{10,... | collective-permute-start | bytes 49160 | tf_op jit(solution)/shard_map/ppermute | solution.py:23
  53.0 4.6 %collective-permute-start.17 = (f32[32,128]{1,0:T(8,128)S(1)}, f32[32,128]{1,0:T(8,128)S(1)}, u32[]{:S(2)}, u32[]{:S(2)}) collective-permute-start(f32[32,128]{1,0:T(8,128)S(1)} %get-tuple-element.20.refs_0_), channel_id=1, source_target_pairs={{0,2},{1,3},{2,0},{3,1},{4,6},{5,7},{6,4},{7,5},{8,10},{9,11},{10,... | collective-permute-start | bytes 49160 | tf_op jit(solution)/shard_map/ppermute | solution.py:23
  54.7 5.5 %collective-permute-start.18 = (f32[32,128]{1,0:T(8,128)S(1)}, f32[32,128]{1,0:T(8,128)S(1)}, u32[]{:S(2)}, u32[]{:S(2)}) collective-permute-start(f32[32,128]{1,0:T(8,128)S(1)} %get-tuple-element.20.refs_0_), channel_id=1, source_target_pairs={{0,6},{1,7},{2,4},{3,5},{4,2},{5,3},{6,0},{7,1},{8,14},{9,15},{10,... | collective-permute-start | bytes 49160 | tf_op jit(solution)/shard_map/ppermute | solution.py:23
